TPU v7x, 32 devices: a whole 2x2x4 slice. The times are simulated.
32 devices in a mesh: groups: 2 (over y), tensor: 4 (over z), dp: 4 (over x, core).
Axes of the slice: x: 2, y: 2, z: 4, core: 2. Of those that a mesh axis runs over, the one named last changes fastest.
Arguments:
- root_features: bfloat16 [32, 16384], P('groups', 'dp'), parts along dimension 0, may hold values from -6 to 6
- branch_embeds: bfloat16 [32, 4, 8, 16384], P('groups', None, None, 'dp'), parts along dimension 0, may hold values from -6 to 6
- parents: int32 [32, 3, 8], P('groups'), parts along dimension 0, may hold values from 0 to 7
- cache_lengths: int32 [32], P(('groups', 'dp')), parts along dimension 0, may hold values from 128 to 512, as said below
- cache_kv: bfloat16 [32, 2, 512, 512], P(('groups', 'dp'), None, None, 'tensor'), parts along dimension 0, may hold values from -6 to 6, as said below
- norm_gain: bfloat16 [16384], P('dp'), may hold values from 0.099609375 to 1.8984375
- w_query: bfloat16 [16384, 2048], P('dp', 'tensor'), may hold values from -1 to 1
- w_keyval: bfloat16 [16384, 2, 512], P('dp', None, 'tensor'), may hold values from -1 to 1, as said below
- w_out: bfloat16 [2048, 16384], P('tensor', 'dp'), may hold values from -0.125 to 0.125
Outputs:
- tree_features: bfloat16 [32, 4, 8, 16384], P('groups', None, None, ('dp', 'tensor')), parts along dimension 0
There are 2 independent parts, one for each index of `groups`. A program takes and returns all parts, laid end to end along the dimension named above; an argument that names none is the same for every part. Nothing has to cross between parts.
Inputs may be any that keep to these rules, and one draw needn't show every extreme that they name: `cache_lengths`: some request has exactly 512 valid cache positions and some other exactly 128. `cache_kv`: for each request, keys and values, the 4 blocks of 128 columns k * 4 .. (k + 1) * 4 - 1 are equal; they hold key-value head k. `w_keyval`: for keys and values, the 4 blocks of 128 columns k * 4 .. (k + 1) * 4 - 1 are equal; they hold key-value head k.
All inputs are finite; a program needn't handle non-finite values.
Results may differ from a plain program's by a relative error of at most 0.017.
Values may be sent and summed in bfloat16 or wider, within the bound.
No kernel may reach another device: no remote copies, remote signals or barrier semaphores. Data moves between devices by JAX's collectives and lax.ppermute only.
A program may use at most 128 MiB of HBM per device.

v0:
```python
import jax
import jax.numpy as jnp
from jax import lax
from jax.sharding import PartitionSpec as P

D = 16384
HD = 128
BRANCH = 8
DEPTHS = 4
CACHE = 512


epsilon = 1e-05
masked_score = -1e30


def ancestor_path(parent_table, tree_level):
    current = jnp.broadcast_to(
        jnp.arange(BRANCH, dtype=jnp.int32)[None, :], (parent_table.shape[0], BRANCH)
    )
    path_nodes = [current]
    for upper in range(tree_level, 0, -1):
        current = jnp.take_along_axis(parent_table[:, upper - 1], current, axis=1)
        path_nodes.append(current)
    return path_nodes[::-1]


def tree_mask_of(parent_table, tree_level):
    path_nodes = ancestor_path(parent_table, tree_level)
    columns = jnp.arange(BRANCH, dtype=jnp.int32)
    blocks = []
    for other_level in range(DEPTHS):
        if other_level <= tree_level:
            blocks.append(columns[None, None, :] == path_nodes[other_level][:, :, None])
        else:
            blocks.append(jnp.zeros((parent_table.shape[0], BRANCH, BRANCH), dtype=bool))
    return jnp.concatenate(blocks, axis=2)


def shards(
    root_features,
    branch_embeds,
    parents,
    cache_lengths,
    cache_kv,
    norm_gain,
    w_query,
    w_keyval,
    w_out,
):
    request_count, feat_cols = root_features.shape
    local_requests = cache_lengths.shape[0]
    head_cols = w_query.shape[1]
    kv_cols = w_keyval.shape[2]
    kv_local = kv_cols // HD
    all_rows = request_count * BRANCH
    own_rows = local_requests * BRANCH
    share_cols = feat_cols // lax.axis_size("tensor")
    dp_index = lax.axis_index("dp")
    tensor_index = lax.axis_index("tensor")
    weights = jnp.concatenate([w_query, w_keyval.reshape(feat_cols, 2 * kv_cols)], axis=1)
    gain = norm_gain.astype(jnp.float32)
    own_parents = lax.dynamic_slice_in_dim(parents, dp_index * local_requests, local_requests, 0)
    cache_keys = cache_kv[:, 0].reshape(local_requests, CACHE, kv_local, HD)
    cache_values = cache_kv[:, 1].reshape(local_requests, CACHE, kv_local, HD)
    positions = jnp.arange(CACHE, dtype=jnp.int32)
    cache_valid = positions[None, :] < cache_lengths[:, None]
    tree_keys = jnp.zeros((local_requests, DEPTHS * BRANCH, kv_local, HD), jnp.bfloat16)
    tree_values = jnp.zeros((local_requests, DEPTHS * BRANCH, kv_local, HD), jnp.bfloat16)
    results = []
    previous = None
    for tree_level in range(DEPTHS):
        if tree_level == 0:
            parent = jnp.broadcast_to(root_features[:, None, :], (request_count, BRANCH, feat_cols))
        else:
            parent = jnp.take_along_axis(previous, parents[:, tree_level - 1][:, :, None], axis=1)
        node_state = parent.astype(jnp.float32) + branch_embeds[:, tree_level].astype(jnp.float32)
        flat_state = node_state.reshape(all_rows, feat_cols)
        square_sums = jnp.sum(flat_state * flat_state, axis=1)
        scaled = (flat_state * gain).astype(jnp.bfloat16)
        total_sums = lax.psum(square_sums, "dp")
        own_sums = lax.dynamic_slice_in_dim(total_sums, dp_index * own_rows, own_rows, 0)
        proj_terms = lax.psum_scatter(
            jnp.dot(scaled, weights, preferred_element_type=jnp.float32).astype(jnp.bfloat16),
            "dp",
            scatter_dimension=0,
            tiled=True,
        ).astype(jnp.float32)
        inv_rms = lax.rsqrt(own_sums / D + epsilon)[:, None]
        projected = (proj_terms * inv_rms).astype(jnp.bfloat16)
        queries = projected[:, :head_cols].reshape(local_requests, BRANCH, kv_local, -1, HD)
        new_keys = projected[:, head_cols : head_cols + kv_cols].reshape(
            local_requests, BRANCH, kv_local, HD
        )
        new_values = projected[:, head_cols + kv_cols :].reshape(
            local_requests, BRANCH, kv_local, HD
        )
        tree_keys = tree_keys.at[:, tree_level * BRANCH : (tree_level + 1) * BRANCH].set(new_keys)
        tree_values = tree_values.at[:, tree_level * BRANCH : (tree_level + 1) * BRANCH].set(
            new_values
        )
        tree_mask = tree_mask_of(own_parents, tree_level)
        cache_scores = jnp.einsum(
            "rbkgd,rckd->rkgbc", queries, cache_keys, preferred_element_type=jnp.float32
        ) * HD ** (-0.5)
        tree_scores = jnp.einsum(
            "rbkgd,rtkd->rkgbt", queries, tree_keys, preferred_element_type=jnp.float32
        ) * HD ** (-0.5)
        cache_scores = jnp.where(cache_valid[:, None, None, None, :], cache_scores, masked_score)
        tree_scores = jnp.where(tree_mask[:, None, None, :, :], tree_scores, masked_score)
        row_max = jnp.maximum(jnp.max(cache_scores, axis=4), jnp.max(tree_scores, axis=4))[
            ..., None
        ]
        cache_exp = jnp.exp(cache_scores - row_max)
        tree_exp = jnp.exp(tree_scores - row_max)
        denominator = jnp.sum(cache_exp, axis=4, keepdims=True) + jnp.sum(
            tree_exp, axis=4, keepdims=True
        )
        cache_weights = (cache_exp / denominator).astype(jnp.bfloat16)
        tree_weights = (tree_exp / denominator).astype(jnp.bfloat16)
        mixed = jnp.einsum(
            "rkgbc,rckd->rbkgd", cache_weights, cache_values, preferred_element_type=jnp.float32
        )
        mixed = mixed + jnp.einsum(
            "rkgbt,rtkd->rbkgd", tree_weights, tree_values, preferred_element_type=jnp.float32
        )
        attended = mixed.reshape(own_rows, head_cols).astype(jnp.bfloat16)
        partial_out = jnp.dot(
            lax.all_gather(attended, "dp", axis=0, tiled=True),
            w_out,
            preferred_element_type=jnp.float32,
        )
        share_sums = lax.psum_scatter(
            partial_out.astype(jnp.bfloat16), "tensor", scatter_dimension=1, tiled=True
        ).astype(jnp.float32)
        residual = lax.dynamic_slice_in_dim(flat_state, tensor_index * share_cols, share_cols, 1)
        fresh_share = (residual + share_sums).astype(jnp.bfloat16)
        if tree_level + 1 < DEPTHS:
            gathered = lax.all_gather(fresh_share, "tensor", axis=1, tiled=True)
            previous = gathered.reshape(request_count, BRANCH, feat_cols)
        results.append(fresh_share.reshape(request_count, BRANCH, share_cols))
    return jnp.stack(results, axis=1)


def solution(mesh):
    return jax.shard_map(
        shards,
        mesh=mesh,
        in_specs=(
            P("groups", "dp"),
            P("groups", None, None, "dp"),
            P("groups", None, None),
            P(("groups", "dp")),
            P(("groups", "dp"), None, None, "tensor"),
            P("dp"),
            P("dp", "tensor"),
            P("dp", None, "tensor"),
            P("tensor", "dp"),
        ),
        out_specs=P("groups", None, None, ("dp", "tensor")),
        check_vma=False,
    )
```

profile of v0, /device:TPU:0, one launch (start us, length us, event | category | flops | bytes accessed | tf_op | source)
XLA Modules:
  0.0 381.4 jit_solution(6987603568505349397)
XLA Ops:
  18.4 8.3 %psum.28 = f32[128]{0:T(128)S(1)} all-reduce(f32[128]{0:T(128)S(1)} %reduce_sum.117), channel_id=1, replica_groups=mesh['groups'=2,'tensor'=4,'dp'=4] {'dp'}, use_global_device_ids=true, to_apply=%region_2.0 | all-reduce | flops 128 | bytes 1024 | tf_op jit(solution)/shard_map/psum | solution.py:81
  32.2 6.1 %reduce-scatter.9.cloned.1.call-done = bf16[32,768]{1,0:T(8,128)(2,1)} async-done(((bf16[128,768]{1,0:T(8,128)(2,1)}), bf16[32,768]{1,0:T(8,128)(2,1)}) %reduce-scatter.9.cloned.1.call-update) | async-done | bytes 49168 | tf_op jit(solution)/shard_map/reduce_scatter | solution.py:83
  40.6 5.4 %all_gather.21 = bf16[128,512]{1,0:T(8,128)(2,1)S(1)} all-gather(bf16[32,512]{1,0:T(8,128)(2,1)S(1)} %fusion.34), channel_id=1, replica_groups=mesh['groups'=2,'tensor'=4,'dp'=4] {'dp'}, dimensions={0}, use_global_device_ids=true | all-gather | bytes 163840 | tf_op jit(solution)/shard_map/all_gather | solution.py:129
  51.5 25.8 %reduce-scatter.11.cloned.1.call-done = bf16[128,1024]{1,0:T(8,128)(2,1)} async-done(((bf16[128,4096]{1,0:T(8,128)(2,1)}), bf16[128,1024]{1,0:T(8,128)(2,1)}) %reduce-scatter.11.cloned.1.call-update) | async-done | bytes 262160 | tf_op jit(solution)/shard_map/reduce_scatter | solution.py:133
  79.4 26.4 %all-gather.4.cloned.1.call-done = bf16[128,4096]{1,0:T(8,128)(2,1)} async-done(((bf16[128,1024]{1,0:T(8,128)(2,1)}), bf16[128,4096]{1,0:T(8,128)(2,1)}) %all-gather.4.cloned.1.call-update) | async-done | bytes 1048592 | tf_op jit(solution)/shard_map/all_gather | solution.py:139
  105.8 5.0 %gather_fusion = bf16[128,4096]{1,0:T(8,128)(2,1)} fusion(bf16[16,8,4096]{2,1,0:T(8,128)(2,1)} %bitcast.414, s32[128]{0:T(128)S(1)} %reshape.800), kind=kCustom, calls=%fused_computation.clone | custom fusion | bytes 2098176 | tf_op jit(solution)/shard_map/jit(take_along_axis)/gather | solution.py:76
  112.9 4.5 %convolution_convert_fusion.6 = bf16[128,768]{1,0:T(8,128)(2,1)} fusion(bf16[4096,768]{1,0:T(8,128)(2,1)} %copy-done, f32[128,4096]{1,0:T(8,128)S(1)} %get-tuple-element.110, f32[4096]{0:T(1024)S(1)} %convert_element_type.206), kind=kOutput, calls=%fused_computation.35 | convolution fusion | flops 806453248 | bytes 8601600 | tf_op jit(solution)/shard_map/dot_general | solution.py:84
  117.5 6.4 %psum.29 = f32[128]{0:T(128)S(1)} all-reduce(f32[128]{0:T(128)S(1)} %reduce_sum.121), channel_id=1, replica_groups=mesh['groups'=2,'tensor'=4,'dp'=4] {'dp'}, use_global_device_ids=true, to_apply=%region_10.12 | all-reduce | flops 128 | bytes 1024 | tf_op jit(solution)/shard_map/psum | solution.py:81
  124.0 12.7 %reduce-scatter.13.cloned.1.call-done = bf16[32,768]{1,0:T(8,128)(2,1)} async-done(((bf16[128,768]{1,0:T(8,128)(2,1)}), bf16[32,768]{1,0:T(8,128)(2,1)}) %reduce-scatter.13.cloned.1.call-update) | async-done | bytes 49168 | tf_op jit(solution)/shard_map/reduce_scatter | solution.py:83
  139.1 5.4 %all_gather.23 = bf16[128,512]{1,0:T(8,128)(2,1)S(1)} all-gather(bf16[32,512]{1,0:T(8,128)(2,1)S(1)} %fusion.33), channel_id=1, replica_groups=mesh['groups'=2,'tensor'=4,'dp'=4] {'dp'}, dimensions={0}, use_global_device_ids=true | all-gather | bytes 163840 | tf_op jit(solution)/shard_map/all_gather | solution.py:129
  148.5 27.3 %reduce-scatter.15.cloned.1.call-done = bf16[128,1024]{1,0:T(8,128)(2,1)} async-done(((bf16[128,4096]{1,0:T(8,128)(2,1)}), bf16[128,1024]{1,0:T(8,128)(2,1)}) %reduce-scatter.15.cloned.1.call-update) | async-done | bytes 262160 | tf_op jit(solution)/shard_map/reduce_scatter | solution.py:133
  178.0 26.3 %all-gather.6.cloned.1.call-done = bf16[128,4096]{1,0:T(8,128)(2,1)} async-done(((bf16[128,1024]{1,0:T(8,128)(2,1)}), bf16[128,4096]{1,0:T(8,128)(2,1)}) %all-gather.6.cloned.1.call-update) | async-done | bytes 1048592 | tf_op jit(solution)/shard_map/all_gather | solution.py:139
  204.3 4.9 %gather_fusion.2 = bf16[128,4096]{1,0:T(8,128)(2,1)} fusion(bf16[16,8,4096]{2,1,0:T(8,128)(2,1)} %bitcast.416, s32[128]{0:T(128)S(1)} %reshape.809), kind=kCustom, calls=%fused_computation.2.clone | custom fusion | bytes 2098176 | tf_op jit(solution)/shard_map/jit(take_along_axis)/gather | solution.py:76
  211.3 4.5 %convolution_convert_fusion.5 = bf16[128,768]{1,0:T(8,128)(2,1)} fusion(bf16[4096,768]{1,0:T(8,128)(2,1)} %copy-done, f32[128,4096]{1,0:T(8,128)S(1)} %get-tuple-element.108, f32[4096]{0:T(1024)S(1)} %convert_element_type.206), kind=kOutput, calls=%fused_computation.34 | convolution fusion | flops 806453248 | bytes 8601600 | tf_op jit(solution)/shard_map/dot_general | solution.py:84
  216.0 6.4 %psum.30 = f32[128]{0:T(128)S(1)} all-reduce(f32[128]{0:T(128)S(1)} %reduce_sum.125), channel_id=1, replica_groups=mesh['groups'=2,'tensor'=4,'dp'=4] {'dp'}, use_global_device_ids=true, to_apply=%region_18.21 | all-reduce | flops 128 | bytes 1024 | tf_op jit(solution)/shard_map/psum | solution.py:81
  222.5 12.8 %reduce-scatter.17.cloned.1.call-done = bf16[32,768]{1,0:T(8,128)(2,1)} async-done(((bf16[128,768]{1,0:T(8,128)(2,1)}), bf16[32,768]{1,0:T(8,128)(2,1)}) %reduce-scatter.17.cloned.1.call-update) | async-done | bytes 49168 | tf_op jit(solution)/shard_map/reduce_scatter | solution.py:83
  237.7 5.4 %all_gather.25 = bf16[128,512]{1,0:T(8,128)(2,1)S(1)} all-gather(bf16[32,512]{1,0:T(8,128)(2,1)S(1)} %fusion.32), channel_id=1, replica_groups=mesh['groups'=2,'tensor'=4,'dp'=4] {'dp'}, dimensions={0}, use_global_device_ids=true | all-gather | bytes 163840 | tf_op jit(solution)/shard_map/all_gather | solution.py:129
  247.1 27.3 %reduce-scatter.19.cloned.1.call-done = bf16[128,1024]{1,0:T(8,128)(2,1)} async-done(((bf16[128,4096]{1,0:T(8,128)(2,1)}), bf16[128,1024]{1,0:T(8,128)(2,1)}) %reduce-scatter.19.cloned.1.call-update) | async-done | bytes 262160 | tf_op jit(solution)/shard_map/reduce_scatter | solution.py:133
  276.4 26.4 %all-gather.8.cloned.1.call-done = bf16[128,4096]{1,0:T(8,128)(2,1)} async-done(((bf16[128,1024]{1,0:T(8,128)(2,1)}), bf16[128,4096]{1,0:T(8,128)(2,1)}) %all-gather.8.cloned.1.call-update) | async-done | bytes 1048592 | tf_op jit(solution)/shard_map/all_gather | solution.py:139
  302.8 4.8 %gather_fusion.5 = bf16[128,4096]{1,0:T(8,128)(2,1)} fusion(bf16[16,8,4096]{2,1,0:T(8,128)(2,1)} %bitcast.415, s32[128]{0:T(128)S(1)} %reshape.823), kind=kCustom, calls=%fused_computation.3.clone | custom fusion | bytes 2098176 | tf_op jit(solution)/shard_map/jit(take_along_axis)/gather | solution.py:76
  314.3 6.4 %psum.31 = f32[128]{0:T(128)S(1)} all-reduce(f32[128]{0:T(128)S(1)} %reduce_sum.129), channel_id=1, replica_groups=mesh['groups'=2,'tensor'=4,'dp'=4] {'dp'}, use_global_device_ids=true, to_apply=%region_26.29 | all-reduce | flops 128 | bytes 1024 | tf_op jit(solution)/shard_map/psum | solution.py:81
  320.8 12.8 %reduce-scatter.21.cloned.1.call-done = bf16[32,768]{1,0:T(8,128)(2,1)} async-done(((bf16[128,768]{1,0:T(8,128)(2,1)}), bf16[32,768]{1,0:T(8,128)(2,1)}) %reduce-scatter.21.cloned.1.call-update) | async-done | bytes 49168 | tf_op jit(solution)/shard_map/reduce_scatter | solution.py:83
  336.0 5.4 %all_gather.27 = bf16[128,512]{1,0:T(8,128)(2,1)S(1)} all-gather(bf16[32,512]{1,0:T(8,128)(2,1)S(1)} %fusion.31), channel_id=1, replica_groups=mesh['groups'=2,'tensor'=4,'dp'=4] {'dp'}, dimensions={0}, use_global_device_ids=true | all-gather | bytes 163840 | tf_op jit(solution)/shard_map/all_gather | solution.py:129
  345.4 27.3 %reduce-scatter.23.cloned.1.call-done = bf16[128,1024]{1,0:T(8,128)(2,1)} async-done(((bf16[128,4096]{1,0:T(8,128)(2,1)}), bf16[128,1024]{1,0:T(8,128)(2,1)}) %reduce-scatter.23.cloned.1.call-update) | async-done | bytes 262160 | tf_op jit(solution)/shard_map/reduce_scatter | solution.py:133
  (160 shorter events, 63.6 us)
Async XLA Ops:
  6.5 2.6 copy-start.8
  6.5 2.6 copy-start.6
  6.5 2.9 copy-start.5
  6.5 31.7 %reduce-scatter.9.cloned.1.call-start = ((), (), s32[]{:S(2)}) async-start(), calls=%async_computation.8 | async-start | bytes 245760 | tf_op jit(solution)/shard_map/reduce_scatter | solution.py:83
  9.8 2.7 copy-start
  12.5 4.7 %copy-start.7 = (s32[16,3,8]{0,2,1:T(8,128)S(1)}, s32[16,3,8]{0,2,1:T(8,128)}, u32[]{:S(2)}) copy-start(s32[16,3,8]{0,2,1:T(8,128)} %param.31) | copy-start | bytes 4612
  15.6 61.8 %reduce-scatter.11.cloned.1.call-start = ((), (), s32[]{:S(2)}) async-start(), calls=%async_computation.9 | async-start | bytes 1310720 | tf_op jit(solution)/shard_map/reduce_scatter | solution.py:133
  29.5 2.4 copy-start.9
  29.5 9.6 %copy-start.1 = (bf16[4,2,512,128]{3,2,1,0:T(8,128)(2,1)S(1)}, bf16[4,2,512,128]{3,2,1,0:T(8,128)(2,1)}, u32[]{:S(2)}) copy-start(bf16[4,2,512,128]{3,2,1,0:T(8,128)(2,1)} %param.33) | copy-start | bytes 3145732
  50.0 55.8 %all-gather.4.cloned.1.call-start = ((), (), s32[]{:S(2)}) async-start(), calls=%async_computation.10 | async-start | bytes 1310720 | tf_op jit(solution)/shard_map/all_gather | solution.py:139
  79.1 57.7 %reduce-scatter.13.cloned.1.call-start = ((), (), s32[]{:S(2)}) async-start(), calls=%async_computation.11 | async-start | bytes 245760 | tf_op jit(solution)/shard_map/reduce_scatter | solution.py:83
  117.4 58.4 %reduce-scatter.15.cloned.1.call-start = ((), (), s32[]{:S(2)}) async-start(), calls=%async_computation.12 | async-start | bytes 1310720 | tf_op jit(solution)/shard_map/reduce_scatter | solution.py:133
  148.5 55.8 %all-gather.6.cloned.1.call-start = ((), (), s32[]{:S(2)}) async-start(), calls=%async_computation.13 | async-start | bytes 1310720 | tf_op jit(solution)/shard_map/all_gather | solution.py:139
  177.5 57.7 %reduce-scatter.17.cloned.1.call-start = ((), (), s32[]{:S(2)}) async-start(), calls=%async_computation.14 | async-start | bytes 245760 | tf_op jit(solution)/shard_map/reduce_scatter | solution.py:83
  215.8 58.5 %reduce-scatter.19.cloned.1.call-start = ((), (), s32[]{:S(2)}) async-start(), calls=%async_computation.15 | async-start | bytes 1310720 | tf_op jit(solution)/shard_map/reduce_scatter | solution.py:133
  247.0 55.8 %all-gather.8.cloned.1.call-start = ((), (), s32[]{:S(2)}) async-start(), calls=%async_computation.16 | async-start | bytes 1310720 | tf_op jit(solution)/shard_map/all_gather | solution.py:139
  276.1 57.6 %reduce-scatter.21.cloned.1.call-start = ((), (), s32[]{:S(2)}) async-start(), calls=%async_computation.17 | async-start | bytes 245760 | tf_op jit(solution)/shard_map/reduce_scatter | solution.py:83
  314.2 58.5 %reduce-scatter.23.cloned.1.call-start = ((), (), s32[]{:S(2)}) async-start(), calls=%async_computation.18 | async-start | bytes 1310720 | tf_op jit(solution)/shard_map/reduce_scatter | solution.py:133
  345.3 28.4 %copy-start.2 = (bf16[128,1024]{1,0:T(8,128)(2,1)S(1)}, bf16[128,1024]{1,0:T(8,128)(2,1)}, u32[]{:S(2)}) copy-start(bf16[128,1024]{1,0:T(8,128)(2,1)} %add_convert_fusion.3) | copy-start | bytes 786436
  345.3 28.4 %copy-start.3 = (bf16[128,1024]{1,0:T(8,128)(2,1)S(1)}, bf16[128,1024]{1,0:T(8,128)(2,1)}, u32[]{:S(2)}) copy-start(bf16[128,1024]{1,0:T(8,128)(2,1)} %add_convert_fusion.2) | copy-start | bytes 786436
  345.3 28.4 %copy-start.4 = (bf16[128,1024]{1,0:T(8,128)(2,1)S(1)}, bf16[128,1024]{1,0:T(8,128)(2,1)}, u32[]{:S(2)}) copy-start(bf16[128,1024]{1,0:T(8,128)(2,1)} %add_convert_fusion.1) | copy-start | bytes 786436
Sparse Core Ops, SparseCore 0:
  15.7 22.5 reduce-scatter.8
  50.1 27.1 reduce-scatter.10
  79.2 26.5 all-gather.3
  117.5 19.1 reduce-scatter.12
  148.6 27.1 reduce-scatter.14
  177.7 26.5 all-gather.5
  215.9 19.2 reduce-scatter.16
  247.2 27.1 reduce-scatter.18
  276.2 26.5 all-gather.7
  314.3 19.2 reduce-scatter.20
  345.5 27.1 reduce-scatter.22
where the time goes:
time: 383 us; the launch traced here: 381 us
  waiting for transfers between devices  231 us (60%)
  blocking collectives  49.3 us (13%)
  matrix products  36.4 us (10%)
  local copies, waits for them, and re-layouts  27.5 us (7%)
  other arithmetic  22.6 us (6%)
  between operations  13.6 us (4%)
    reduce_scatter x4, waiting for transfers between devices, shards(): lax.psum_scatter(partial_out.astype(jnp.bfloat16), 'tensor', scatter_dime...  108 us
    all_gather x3, waiting for transfers between devices, shards(): gathered = lax.all_gather(fresh_share, 'tensor', axis=1, tiled=True)  79.1 us
    reduce_scatter x4, waiting for transfers between devices, shards(): lax.psum_scatter(jnp.dot(scaled, weights, preferred_element_type=jnp.floa...  44.3 us
    psum x4, blocking collectives, shards(): total_sums = lax.psum(square_sums, 'dp')  27.6 us
    all_gather x4, blocking collectives, shards(): lax.all_gather(attended, 'dp', axis=0, tiled=True)  21.7 us
    dot_general x4, matrix products, shards(): jnp.dot(scaled, weights, preferred_element_type=jnp.float32)  16.4 us
    dot_general x4, matrix products, shards(): jnp.dot(lax.all_gather(attended, 'dp', axis=0, tiled=True), w_out, prefer...  15.7 us
    gather x9, local copies, waits for them, and re-layouts, shards(): jnp.take_along_axis(previous, parents[:, tree_level - 1][:, :, None], axi...  15.2 us
  transfers between devices with their start and end apart: 11, of which 11 were waited for; matrix products, arithmetic and copies ran while one was open for 3% of the time, Pallas kernels for 0%

commit v1 on v0

v1 whole, which is shorter than its diff:
```python
import functools

import jax
import jax.numpy as jnp
from jax import lax
from jax.experimental import pallas as pl
from jax.experimental.pallas import tpu as pltpu
from jax.sharding import PartitionSpec as P

HD = 128
BATCHES = 2
EPSILON = 1e-05
MASKED = -1e30
LANES = 128
VMEM_BYTES = 40 * 1024 * 1024


def swap(x, axis, step):
    size = lax.axis_size(axis)
    return lax.ppermute(x, axis, [(i, i ^ step) for i in range(size)])


def parent_rows(index_ref, features):
    rows, width = index_ref.shape[0], features.shape[0]
    column = lax.broadcasted_iota(jnp.int32, (rows, width), 1)
    chosen = jnp.where(column == index_ref[...], 1.0, 0.0).astype(jnp.bfloat16)
    return jnp.dot(chosen, features, preferred_element_type=jnp.float32)


def embed_rows(places_ref, embed_ref):
    dp, _, per_block = embed_ref.shape[:3]
    blocks = []
    for step in range(dp):
        for request in range(per_block):
            block = embed_ref[places_ref[step], 0, request, 0]
            blocks.append(block.astype(jnp.float32))
    return jnp.concatenate(blocks, axis=0)


def project_kernel(pieces, dp, share_ref, places_ref, index_ref, *refs):
    features = refs[:pieces]
    embed_ref, gain_ref, query_ref, keyval_ref = refs[pieces : pieces + 4]
    out_refs = refs[pieces + 4 : pieces + 4 + dp]
    held_ref, total_ref, square_ref = refs[pieces + 4 + dp :]
    step = pl.program_id(0)
    head_cols = query_ref.shape[1]

    if pieces == 1:
        held_ref[...] = features[0][...]
    else:
        for piece in range(pieces):

            @pl.when(step == piece)
            def _():
                held_ref[...] = features[piece][...]

    state = parent_rows(index_ref, held_ref[...]) + embed_rows(places_ref, embed_ref)
    squares = jnp.sum(state * state, axis=1, keepdims=True)
    scaled = (state * gain_ref[...].astype(jnp.float32)).astype(jnp.bfloat16)
    query = jnp.dot(scaled, query_ref[...], preferred_element_type=jnp.float32)
    keyval = jnp.dot(scaled, keyval_ref[...], preferred_element_type=jnp.float32)

    @pl.when(step == 0)
    def _():
        total_ref[:, :head_cols] = query
        total_ref[:, head_cols:] = keyval
        square_ref[...] = squares

    @pl.when(step > 0)
    def _():
        total_ref[:, :head_cols] += query
        total_ref[:, head_cols:] += keyval
        square_ref[...] += squares

    @pl.when(step == pl.num_programs(0) - 1)
    def _():
        width = total_ref.shape[1]
        rows = out_refs[0].shape[0]
        lane = lax.broadcasted_iota(jnp.int32, (rows, LANES), 1)
        for block in range(dp):
            span = slice(block * rows, (block + 1) * rows)
            high = square_ref[span, :].astype(jnp.bfloat16).astype(jnp.float32)
            low = square_ref[span, :] - high
            tail = jnp.where(lane == 0, high, jnp.where(lane == 1, low, 0.0))
            out_refs[block][:, :width] = total_ref[span, :].astype(jnp.bfloat16)
            out_refs[block][:, width:] = tail.astype(jnp.bfloat16)


def attend_kernel(
    dp, earlier, head_cols, model_width, base, length_ref, *refs
):
    parts = refs[:dp]
    mask_ref, cache_ref = refs[dp : dp + 2]
    earlier_refs = refs[dp + 2 : dp + 2 + earlier]
    out_ref, fresh_ref = refs[dp + 2 + earlier :]
    total = parts[0][...].astype(jnp.float32)
    for part in parts[1:]:
        total = total + part[...].astype(jnp.float32)
    width = head_cols + fresh_ref.shape[1]
    squares = jnp.sum(total[:, width:], axis=1, keepdims=True)
    inv_rms = lax.rsqrt(squares / model_width + EPSILON)
    projected = (total[:, :width] * inv_rms).astype(jnp.bfloat16).astype(jnp.float32)
    fresh = projected[:, head_cols:]
    fresh_ref[...] = fresh
    per_block, _, cache, kv_cols = cache_ref.shape[1:]
    branch = total.shape[0] // per_block
    kv_heads = kv_cols // HD
    group = head_cols // HD // kv_heads
    positions = mask_ref.shape[1]
    tree = [ref[...] for ref in earlier_refs] + [fresh]
    blank = jnp.zeros((positions - branch * len(tree), HD), jnp.float32)
    column = lax.broadcasted_iota(jnp.int32, (group * branch, cache), 1)
    across = (((1,), (1,)), ((), ()))
    outs = []
    for request in range(per_block):
        span = slice(request * branch, (request + 1) * branch)
        valid = column < length_ref[base + request]
        allowed = jnp.concatenate([mask_ref[span, :]] * group, axis=0) > 0.5
        heads = []
        for kv in range(kv_heads):
            first = kv * group
            queries = jnp.concatenate(
                [
                    projected[span, (first + g) * HD : (first + g + 1) * HD]
                    for g in range(group)
                ],
                axis=0,
            ).astype(jnp.bfloat16)
            key_cols = slice(kv * HD, (kv + 1) * HD)
            value_cols = slice(kv_cols + kv * HD, kv_cols + (kv + 1) * HD)
            filler = [blank] if blank.shape[0] else []
            tree_keys = jnp.concatenate(
                [level[span, key_cols] for level in tree] + filler, axis=0
            ).astype(jnp.bfloat16)
            tree_values = jnp.concatenate(
                [level[span, value_cols] for level in tree] + filler, axis=0
            ).astype(jnp.bfloat16)
            keys = cache_ref[0, request, 0, :, key_cols]
            values = cache_ref[0, request, 1, :, key_cols]
            scale = HD**-0.5
            near = lax.dot_general(
                queries, keys, across, preferred_element_type=jnp.float32
            )
            far = lax.dot_general(
                queries, tree_keys, across, preferred_element_type=jnp.float32
            )
            near = jnp.where(valid, near * scale, MASKED)
            far = jnp.where(allowed, far * scale, MASKED)
            top = jnp.maximum(
                jnp.max(near, axis=1, keepdims=True), jnp.max(far, axis=1, keepdims=True)
            )
            near = jnp.exp(near - top)
            far = jnp.exp(far - top)
            below = jnp.sum(near, axis=1, keepdims=True) + jnp.sum(far, axis=1, keepdims=True)
            mixed = jnp.dot(
                (near / below).astype(jnp.bfloat16), values, preferred_element_type=jnp.float32
            ) + jnp.dot(
                (far / below).astype(jnp.bfloat16), tree_values, preferred_element_type=jnp.float32
            )
            heads += [mixed[g * branch : (g + 1) * branch] for g in range(group)]
        outs.append(jnp.concatenate(heads, axis=1))
    out_ref[...] = jnp.concatenate(outs, axis=0).astype(jnp.bfloat16)


def output_kernel(dp, weights, has_alias, info_ref, index_ref, *refs):
    attended = refs[:dp]
    weight_refs = refs[dp : dp + len(weights)]
    feature_ref, embed_ref = refs[dp + len(weights) : dp + len(weights) + 2]
    rest = refs[dp + len(weights) + 2 + has_alias :]
    fresh_ref, out_ref, gathered_ref = rest
    rows = attended[0].shape[0]
    for step in range(dp):
        gathered_ref[step * rows : (step + 1) * rows, :] = attended[step][...]
    fresh = parent_rows(index_ref, feature_ref[...]) + embed_rows(info_ref, embed_ref)
    for weight_ref, (start, side) in zip(weight_refs, weights):
        depth = weight_ref.shape[0]
        if side is None:
            left = gathered_ref[:, start : start + depth]
        else:
            offset = pl.multiple_of(start + info_ref[dp + side], LANES)
            left = gathered_ref[:, pl.ds(offset, depth)]
        fresh = fresh + jnp.dot(left, weight_ref[...], preferred_element_type=jnp.float32)
    fresh_ref[...] = fresh.astype(jnp.bfloat16)
    per_block, branch = out_ref.shape[2], out_ref.shape[4]
    for step in range(dp):
        for request in range(per_block):
            start = (step * per_block + request) * branch
            out_ref[info_ref[step], 0, request, 0] = fresh[start : start + branch].astype(
                jnp.bfloat16
            )


def project(level, batch, share_ids, places, index, pieces, embeds, gain, w_query, w_keyval):
    dp, _, per_block, _, branch, feat_cols = embeds.shape
    steps = share_ids.shape[0]
    cols = feat_cols // steps
    head_cols, kv_cols = w_query.shape[1], w_keyval.shape[1]
    rows = per_block * branch
    if len(pieces) == 1:
        piece_specs = [
            pl.BlockSpec((pieces[0].shape[0], cols), lambda k, s, p: (0, s[k])),
        ]
    else:
        piece_specs = [pl.BlockSpec(x.shape, lambda k, s, p: (0, 0)) for x in pieces]
    width = head_cols + kv_cols + LANES
    out_shape = [jax.ShapeDtypeStruct((rows, width), jnp.bfloat16)] * dp
    body = functools.partial(project_kernel, len(pieces), dp)
    return pl.pallas_call(
        body,
        grid_spec=pltpu.PrefetchScalarGridSpec(
            num_scalar_prefetch=2,
            grid=(steps,),
            in_specs=[pl.BlockSpec(index.shape, lambda k, s, p: (0, 0))]
            + piece_specs
            + [
                pl.BlockSpec(
                    (dp, 1, per_block, 1, branch, cols),
                    lambda k, s, p: (0, batch, 0, level, 0, s[k]),
                ),
                pl.BlockSpec((1, cols), lambda k, s, p: (0, s[k])),
                pl.BlockSpec((cols, head_cols), lambda k, s, p: (s[k], 0)),
                pl.BlockSpec((cols, kv_cols), lambda k, s, p: (s[k], 0)),
            ],
            out_specs=[pl.BlockSpec((rows, width), lambda k, s, p: (0, 0))] * dp,
            scratch_shapes=[
                pltpu.VMEM((pieces[0].shape[0], cols), jnp.bfloat16),
                pltpu.VMEM((dp * rows, head_cols + kv_cols), jnp.float32),
                pltpu.VMEM((dp * rows, 1), jnp.float32),
            ],
        ),
        out_shape=out_shape,
        compiler_params=pltpu.CompilerParams(vmem_limit_bytes=VMEM_BYTES),
        cost_estimate=pl.CostEstimate(
            flops=2 * dp * rows * feat_cols * (head_cols + kv_cols),
            bytes_accessed=2 * feat_cols * (head_cols + kv_cols + 2 * dp * rows),
            transcendentals=0,
        ),
        name="project",
    )(share_ids, places, index, *pieces, embeds, gain, w_query, w_keyval)


def attend(batch, model_width, head_cols, lengths, parts, mask, cache, earlier):
    rows, width = parts[0].shape
    fresh_cols = width - LANES - head_cols
    per_block = cache.shape[1]
    whole = lambda x: pl.BlockSpec(x.shape, lambda i, n: (0,) * x.ndim)
    cache_shape = (1,) + cache.shape[1:]
    return pl.pallas_call(
        functools.partial(
            attend_kernel,
            len(parts),
            len(earlier),
            head_cols,
            model_width,
            batch * per_block,
        ),
        grid_spec=pltpu.PrefetchScalarGridSpec(
            num_scalar_prefetch=1,
            grid=(1,),
            in_specs=[whole(x) for x in parts]
            + [whole(mask), pl.BlockSpec(cache_shape, lambda i, n: (batch, 0, 0, 0, 0))]
            + [whole(x) for x in earlier],
            out_specs=[
                pl.BlockSpec((rows, head_cols), lambda i, n: (0, 0)),
                pl.BlockSpec((rows, fresh_cols), lambda i, n: (0, 0)),
            ],
        ),
        out_shape=[
            jax.ShapeDtypeStruct((rows, head_cols), jnp.bfloat16),
            jax.ShapeDtypeStruct((rows, fresh_cols), jnp.float32),
        ],
        compiler_params=pltpu.CompilerParams(vmem_limit_bytes=VMEM_BYTES),
        cost_estimate=pl.CostEstimate(
            flops=4 * rows * head_cols * cache.shape[3],
            bytes_accessed=4 * cache.shape[3] * per_block * HD * 8,
            transcendentals=rows * head_cols * 4,
        ),
        name="attend",
    )(lengths, *parts, mask, cache, *earlier)


def output(level, batch, info, index, attended, weights, features, embeds, held, share_cols):
    dp, batches, per_block, depths, branch, _ = embeds.shape
    rows = dp * per_block * branch
    block = min(2 * LANES, share_cols)
    steps = share_cols // block
    full = lambda x: pl.BlockSpec(x.shape, lambda j, s: (0, 0))
    local = features.shape[1] == share_cols
    base = dp + 2
    if local:
        feature_map = lambda j, s: (0, j)
    else:
        feature_map = lambda j, s: (0, s[base] * steps + j)
    arrays = [w for w, _, _ in weights]
    places = [(start, side) for _, start, side in weights]
    out_shape = jax.ShapeDtypeStruct(
        (dp, batches, per_block, depths, branch, share_cols), jnp.bfloat16
    )
    in_specs = (
        [full(index)]
        + [full(x) for x in attended]
        + [pl.BlockSpec((w.shape[0], block), lambda j, s: (0, j)) for w in arrays]
        + [
            pl.BlockSpec((features.shape[0], block), feature_map),
            pl.BlockSpec(
                (dp, 1, per_block, 1, branch, block),
                lambda j, s: (0, batch, 0, level, 0, s[base] * steps + j),
            ),
        ]
    )
    operands = [info, index, *attended, *arrays, features, embeds]
    aliases = {}
    if held is not None:
        in_specs.append(pl.BlockSpec(memory_space=pl.ANY))
        aliases = {len(operands): 1}
        operands.append(held)
    depth = sum(w.shape[0] for w in arrays)
    return pl.pallas_call(
        functools.partial(output_kernel, dp, places, int(held is not None)),
        grid_spec=pltpu.PrefetchScalarGridSpec(
            num_scalar_prefetch=1,
            grid=(steps,),
            in_specs=in_specs,
            out_specs=[
                pl.BlockSpec((rows, block), lambda j, s: (0, j)),
                pl.BlockSpec(
                    (dp, 1, per_block, 1, branch, block),
                    lambda j, s: (0, batch, 0, level, 0, j),
                ),
            ],
            scratch_shapes=[pltpu.VMEM((rows, depth), jnp.bfloat16)],
        ),
        out_shape=[jax.ShapeDtypeStruct((rows, share_cols), jnp.bfloat16), out_shape],
        input_output_aliases=aliases,
        compiler_params=pltpu.CompilerParams(vmem_limit_bytes=VMEM_BYTES),
        cost_estimate=pl.CostEstimate(
            flops=2 * rows * depth * share_cols,
            bytes_accessed=2 * depth * share_cols,
            transcendentals=0,
        ),
        name="output",
    )(*operands)


def tree_masks(own_parents, depths, branch):
    columns = jnp.arange(branch, dtype=jnp.int32)
    masks = []
    for level in range(depths):
        current = jnp.broadcast_to(columns, own_parents.shape[:2] + (branch,))
        blocks = [columns == current[..., None]]
        for upper in range(level, 0, -1):
            above = own_parents[:, :, upper - 1]
            current = jnp.sum(
                jnp.where(current[..., None] == columns, above[:, :, None, :], 0), axis=3
            )
            blocks.append(columns == current[..., None])
        blocks = blocks[::-1]
        blank = jnp.zeros(blocks[0].shape, bool)
        blocks += [blank] * (depths - len(blocks))
        joined = jnp.concatenate(blocks, axis=3).astype(jnp.float32)
        masks.append(joined.reshape(own_parents.shape[0], -1, depths * branch))
    return masks


def shards(
    root_features,
    branch_embeds,
    parents,
    cache_lengths,
    cache_kv,
    norm_gain,
    w_query,
    w_keyval,
    w_out,
):
    requests, depths, branch, feat_cols = branch_embeds.shape
    dp, tensor, groups = (lax.axis_size(name) for name in ("dp", "tensor", "groups"))
    dp_index, tensor_index, group_index = (
        lax.axis_index(name).astype(jnp.int32) for name in ("dp", "tensor", "groups")
    )
    local = requests // dp
    batches = BATCHES
    per_block = local // batches
    share_cols = feat_cols // tensor
    head_cols = w_query.shape[1]
    head_rows = w_out.shape[0]
    by_swaps = tensor == 4 and groups == 2

    if by_swaps:
        half = head_rows // 2
        own = lax.dynamic_slice(w_out, (0, tensor_index * share_cols), (head_rows, share_cols))
        weights = [(own, 0, None)]
        for step in (3, 2, 1):
            sent = lax.dynamic_slice(
                w_out,
                (group_index * half, (tensor_index ^ step) * share_cols),
                (half, share_cols),
            )
            arrived = swap(sent, "tensor", step)
            weights.append((arrived, step * head_rows, 0))
            weights.append((swap(arrived, "groups", 1), step * head_rows, 1))
    else:
        half = 0
        spread = lax.all_to_all(w_out, "tensor", 1, 0, tiled=True)
        weights = [(spread, 0, None)]

    embeds = branch_embeds.reshape(dp, batches, per_block, depths, branch, feat_cols)
    gain = norm_gain.reshape(1, feat_cols)
    keyval = w_keyval.reshape(feat_cols, -1)
    cache = cache_kv.reshape((batches, per_block) + cache_kv.shape[1:])
    places = jnp.stack([dp_index ^ step for step in range(dp)])
    info = jnp.concatenate(
        [
            places,
            jnp.stack([group_index * half, (1 - group_index) * half, tensor_index]),
        ]
    )
    if by_swaps:
        share_ids = jnp.stack([tensor_index ^ step for step in range(tensor)])
    else:
        share_ids = jnp.zeros((1,), jnp.int32)
    root_ids = jnp.arange(4 if by_swaps else 1, dtype=jnp.int32)

    split = parents.reshape(dp, batches, per_block, depths - 1, branch)
    ordered = jnp.stack(
        [lax.dynamic_index_in_dim(split, dp_index ^ step, 0, False) for step in range(dp)]
    )
    slot = (
        jnp.arange(dp, dtype=jnp.int32)[:, None] * per_block
        + jnp.arange(per_block, dtype=jnp.int32)[None, :]
    )
    rows = dp * per_block * branch
    indices = []
    for level in range(depths):
        row = []
        for batch in range(batches):
            if level == 0:
                request = (
                    places[:, None] * local
                    + batch * per_block
                    + jnp.arange(per_block, dtype=jnp.int32)[None, :]
                )
                place = jnp.broadcast_to(request[:, :, None], (dp, per_block, branch))
            else:
                place = slot[:, :, None] * branch + ordered[:, batch, :, level - 1]
            row.append(place.reshape(rows, 1))
        indices.append(row)
    masks = tree_masks(ordered[0], depths, branch)

    earlier = [[] for _ in range(batches)]
    shares = [root_features] * batches
    gathered = [[root_features]] * batches
    held = None
    for level in range(depths):
        attended = []
        for batch in range(batches):
            sums = project(
                level,
                batch,
                root_ids if level == 0 else share_ids,
                places,
                indices[level][batch],
                gathered[batch],
                embeds,
                gain,
                w_query,
                keyval,
            )
            parts = [sums[0]] + [swap(sums[step], "dp", step) for step in range(1, dp)]
            mixed, fresh = attend(
                batch,
                feat_cols * dp,
                head_cols,
                cache_lengths,
                parts,
                masks[level][batch],
                cache,
                earlier[batch],
            )
            earlier[batch] = earlier[batch] + [fresh]
            if by_swaps:
                heads = [mixed] + [swap(mixed, "tensor", step) for step in range(1, tensor)]
                joined = jnp.concatenate(heads, axis=1)
            else:
                joined = lax.all_gather(mixed, "tensor", axis=1, tiled=True)
            attended.append([joined] + [swap(joined, "dp", step) for step in range(1, dp)])
        for batch in range(batches):
            shares[batch], held = output(
                level,
                batch,
                info,
                indices[level][batch],
                attended[batch],
                weights,
                shares[batch],
                embeds,
                held,
                share_cols,
            )
            if level + 1 == depths:
                continue
            own = shares[batch]
            if by_swaps:
                far = swap(own, "tensor", 3)
                gathered[batch] = [own, swap(own, "tensor", 1), swap(far, "tensor", 1), far]
            else:
                gathered[batch] = [lax.all_gather(own, "tensor", axis=1, tiled=True)]
    return held.reshape(requests, depths, branch, share_cols)


def solution(mesh):
    return jax.shard_map(
        shards,
        mesh=mesh,
        in_specs=(
            P("groups", "dp"),
            P("groups", None, None, "dp"),
            P("groups", None, None),
            P(("groups", "dp")),
            P(("groups", "dp"), None, None, "tensor"),
            P("dp"),
            P("dp", "tensor"),
            P("dp", None, "tensor"),
            P("tensor", "dp"),
        ),
        out_specs=P("groups", None, None, ("dp", "tensor")),
        check_vma=False,
    )
```

time: 383 us -> 313 us (0.82)
  waiting for transfers between devices: 231 us -> 73.3 us
  starting transfers between devices: 0.6 us -> 93.1 us
  Pallas kernels: 0 us -> 84.6 us
  blocking collectives: 49.3 us -> 0 us
  matrix products: 36.4 us -> 0 us
  local copies, waits for them, and re-layouts: 27.5 us -> 56.2 us
  other arithmetic: 22.6 us -> 3.19 us
  between operations: 13.6 us -> 1.3 us
    reduce_scatter x8 -> x0, waiting for transfers between devices: 152 us -> none  [the longest x4 108 us: shards(): lax.psum_scatter(partial_out.astype(jnp.bfloat16), 'tensor', scatter_dime...]
    ppermute x0 -> x96, starting transfers between devices: none -> 93.1 us  [swap(): return lax.ppermute(x, axis, [(i, i ^ step) for i in range(size)])]
    pallas_call x0 -> x24, Pallas kernels: none -> 84.6 us  [the longest x8 38.2 us: output(): pl.pallas_call(functools.partial(output_kernel, dp, places, int(held is n...]
    all_gather x3 -> x0, waiting for transfers between devices: 79.1 us -> none  [shards(): gathered = lax.all_gather(fresh_share, 'tensor', axis=1, tiled=True)]
    ppermute x0 -> x96, waiting for transfers between devices: none -> 73.3 us  [swap(): return lax.ppermute(x, axis, [(i, i ^ step) for i in range(size)])]
    dot_general x24 -> x0, matrix products: 36.4 us -> none  [the longest x4 16.4 us: shards(): jnp.dot(scaled, weights, preferred_element_type=jnp.float32)]
    unnamed x21 -> x236, local copies, waits for them, and re-layouts: 5.56 us -> 41.8 us
    psum x4 -> x0, blocking collectives: 27.6 us -> none  [shards(): total_sums = lax.psum(square_sums, 'dp')]
  transfers between devices with their start and end apart: 11 -> 96, of which waited for: 11 -> 18; matrix products, arithmetic and copies ran while one was open for 3% -> 6% of each run, Pallas kernels for 0% -> 24%
where the time goes in v1:
time: 313 us; the launch traced here: 312 us
  starting transfers between devices  93.1 us (30%)
  Pallas kernels  84.6 us (27%)
  waiting for transfers between devices  73.3 us (23%)
  local copies, waits for them, and re-layouts  56.2 us (18%)
  other arithmetic  3.19 us (1%)
    ppermute x96, starting transfers between devices, swap(): return lax.ppermute(x, axis, [(i, i ^ step) for i in range(size)])  93.1 us
    ppermute x96, waiting for transfers between devices, swap(): return lax.ppermute(x, axis, [(i, i ^ step) for i in range(size)])  73.3 us
    unnamed x236, local copies, waits for them, and re-layouts  41.8 us
    pallas_call x8, Pallas kernels, output(): pl.pallas_call(functools.partial(output_kernel, dp, places, int(held is n...  38.2 us
    pallas_call x8, Pallas kernels, project(): pl.pallas_call(body, grid_spec=pltpu.PrefetchScalarGridSpec(num_scalar_pr...  33.4 us
    pallas_call x8, Pallas kernels, attend(): pl.pallas_call(functools.partial(attend_kernel, len(parts), len(earlier),...  13 us
  transfers between devices with their start and end apart: 96, of which 18 were waited for; matrix products, arithmetic and copies ran while one was open for 6% of the time, Pallas kernels for 24%

profile of v1, /device:TPU:0, one launch (start us, length us, event | category | flops | bytes accessed | tf_op | source)
XLA Modules:
  0.0 311.7 jit_solution(2473631634892425783)
XLA Ops:
  47.6 6.5 %collective-permute-done.18 = bf16[16,512]{1,0:T(8,128)(2,1)S(1)} collective-permute-done((bf16[16,512]{1,0:T(8,128)(2,1)S(1)}, bf16[16,512]{1,0:T(8,128)(2,1)S(1)}, u32[]{:S(2)}, u32[]{:S(2)}) %collective-permute-start.18) | collective-permute-done | bytes 16416 | tf_op jit(solution)/shard_map/ppermute | solution.py:20
  54.4 11.5 %collective-permute-done.19 = bf16[16,512]{1,0:T(8,128)(2,1)S(1)} collective-permute-done((bf16[16,512]{1,0:T(8,128)(2,1)S(1)}, bf16[16,512]{1,0:T(8,128)(2,1)S(1)}, u32[]{:S(2)}, u32[]{:S(2)}) %collective-permute-start.19) | collective-permute-done | bytes 16416 | tf_op jit(solution)/shard_map/ppermute | solution.py:20
  74.3 3.8 %collective-permute-done.5 = bf16[16,512]{1,0:T(8,128)(2,1)S(1)} collective-permute-done((bf16[16,512]{1,0:T(8,128)(2,1)S(1)}, bf16[16,512]{1,0:T(8,128)(2,1)S(1)}, u32[]{:S(2)}, u32[]{:S(2)}) %collective-permute-start.5) | collective-permute-done | bytes 16416 | tf_op jit(solution)/shard_map/ppermute | solution.py:20
  85.0 7.2 %collective-permute-done.12.refs_8_ = bf16[256,1024]{1,0:T(8,128)(2,1)S(1)} collective-permute-done((bf16[256,1024]{1,0:T(8,128)(2,1)}, bf16[256,1024]{1,0:T(8,128)(2,1)S(1)}, u32[]{:S(2)}, u32[]{:S(2)}) %collective-permute-start.12) | collective-permute-done | bytes 524320 | tf_op jit(solution)/shard_map/ppermute | solution.py:20
  92.3 9.6 %collective-permute-done.14.refs_10_ = bf16[256,1024]{1,0:T(8,128)(2,1)S(1)} collective-permute-done((bf16[256,1024]{1,0:T(8,128)(2,1)}, bf16[256,1024]{1,0:T(8,128)(2,1)S(1)}, u32[]{:S(2)}, u32[]{:S(2)}) %collective-permute-start.14) | collective-permute-done | bytes 524320 | tf_op jit(solution)/shard_map/ppermute | solution.py:20
  104.0 4.8 %output.8 = (bf16[64,1024]{1,0:T(8,128)(2,1)S(1)}, bf16[4,2,2,4,8,1024]{5,4,3,2,1,0:T(8,128)(2,1)}) custom-call(s32[7]{0:T(128)S(1)} %concatenate.51.info_ref, s32[64,1]{1,0:T(8,128)S(1)} %reshape.306.index_ref, bf16[16,2048]{1,0:T(8,128)(2,1)S(1)} %constant_dynamic-update-slice_fusion.4.refs_0_, bf16[16,2048]{1,0:T(8,128)(2,1)S(1)} %collective-permute-done.21.refs_1_, ...), custom_call_target="tpu_custom_call" | custom-call | flops 268435456 | bytes 4194304 | tf_op jit(solution)/shard_map/output/pallas_call | solution.py:318
  124.5 4.8 %output.9 = (bf16[64,1024]{1,0:T(8,128)(2,1)S(1)}, bf16[4,2,2,4,8,1024]{5,4,3,2,1,0:T(8,128)(2,1)}) custom-call(s32[7]{0:T(128)S(1)} %copy-done.62, s32[64,1]{1,0:T(8,128)S(1)} %copy-done.40, bf16[16,2048]{1,0:T(8,128)(2,1)S(1)} %copy-done.52, bf16[16,2048]{1,0:T(8,128)(2,1)} %collective-permute-done.6.refs_1_, ...), custom_call_target="tpu_custom_call", output_to_operand_aliasing={{1}: (15, {})} | custom-call | flops 268435456 | bytes 4194304 | tf_op jit(solution)/shard_map/output/pallas_call | solution.py:318
  133.6 4.1 %collective-permute-done.25.refs_3_ = bf16[64,1024]{1,0:T(8,128)(2,1)} collective-permute-done((bf16[64,1024]{1,0:T(8,128)(2,1)S(1)}, bf16[64,1024]{1,0:T(8,128)(2,1)}, u32[]{:S(2)}, u32[]{:S(2)}) %collective-permute-start.25) | collective-permute-done | bytes 131104 | tf_op jit(solution)/shard_map/ppermute | solution.py:20
  143.9 4.1 %project.11 = (bf16[16,896]{1,0:T(8,128)(2,1)S(1)}, bf16[16,896]{1,0:T(8,128)(2,1)S(1)}, bf16[16,896]{1,0:T(8,128)(2,1)S(1)}, bf16[16,896]{1,0:T(8,128)(2,1)S(1)}) custom-call(s32[4]{0:T(128)S(1)} %pad_add_fusion.1.share_ref, s32[4]{0:T(128)S(1)} %copy-done.58, s32[64,1]{1,0:T(8,128)S(1)} %copy.63.index_ref, ...), custom_call_target="tpu_custom_call" | custom-call | flops 402653184 | bytes 7340032 | tf_op jit(solution)/shard_map/project/pallas_call | solution.py:208
  150.1 4.5 %project.10 = (bf16[16,896]{1,0:T(8,128)(2,1)S(1)}, bf16[16,896]{1,0:T(8,128)(2,1)S(1)}, bf16[16,896]{1,0:T(8,128)(2,1)S(1)}, bf16[16,896]{1,0:T(8,128)(2,1)S(1)}) custom-call(s32[4]{0:T(128)S(1)} %pad_add_fusion.1.share_ref, s32[4]{0:T(128)S(1)} %copy-done.58, s32[64,1]{1,0:T(8,128)S(1)} %copy.64.index_ref, ...), custom_call_target="tpu_custom_call" | custom-call | flops 402653184 | bytes 7340032 | tf_op jit(solution)/shard_map/project/pallas_call | solution.py:208
  174.6 4.8 %output.10 = (bf16[64,1024]{1,0:T(8,128)(2,1)S(1)}, bf16[4,2,2,4,8,1024]{5,4,3,2,1,0:T(8,128)(2,1)}) custom-call(s32[7]{0:T(128)S(1)} %copy-done.63, s32[64,1]{1,0:T(8,128)S(1)} %copy-done.44, bf16[16,2048]{1,0:T(8,128)(2,1)S(1)} %constant_dynamic-update-slice_fusion.12.refs_0_, ...), custom_call_target="tpu_custom_call", output_to_operand_aliasing={{1}: (15, {})} | custom-call | flops 268435456 | bytes 4194304 | tf_op jit(solution)/shard_map/output/pallas_call | solution.py:318
  181.4 4.8 %output.11 = (bf16[64,1024]{1,0:T(8,128)(2,1)S(1)}, bf16[4,2,2,4,8,1024]{5,4,3,2,1,0:T(8,128)(2,1)}) custom-call(s32[7]{0:T(128)S(1)} %copy-done.63, s32[64,1]{1,0:T(8,128)S(1)} %copy-done.42, bf16[16,2048]{1,0:T(8,128)(2,1)S(1)} %constant_dynamic-update-slice_fusion.8.refs_0_, ...), custom_call_target="tpu_custom_call", output_to_operand_aliasing={{1}: (15, {})} | custom-call | flops 268435456 | bytes 4194304 | tf_op jit(solution)/shard_map/output/pallas_call | solution.py:318
  190.1 4.3 %collective-permute-done.49.refs_3_ = bf16[64,1024]{1,0:T(8,128)(2,1)} collective-permute-done((bf16[64,1024]{1,0:T(8,128)(2,1)S(1)}, bf16[64,1024]{1,0:T(8,128)(2,1)}, u32[]{:S(2)}, u32[]{:S(2)}) %collective-permute-start.49) | collective-permute-done | bytes 131104 | tf_op jit(solution)/shard_map/ppermute | solution.py:20
  196.5 5.5 %collective-permute-done.62.refs_2_ = bf16[64,1024]{1,0:T(8,128)(2,1)} collective-permute-done((bf16[64,1024]{1,0:T(8,128)(2,1)}, bf16[64,1024]{1,0:T(8,128)(2,1)}, u32[]{:S(2)}, u32[]{:S(2)}) %collective-permute-start.62) | collective-permute-done | bytes 131104 | tf_op jit(solution)/shard_map/ppermute | solution.py:20
  207.7 4.1 %project.13 = (bf16[16,896]{1,0:T(8,128)(2,1)S(1)}, bf16[16,896]{1,0:T(8,128)(2,1)S(1)}, bf16[16,896]{1,0:T(8,128)(2,1)S(1)}, bf16[16,896]{1,0:T(8,128)(2,1)S(1)}) custom-call(s32[4]{0:T(128)S(1)} %copy-done.79, s32[4]{0:T(128)S(1)} %copy-done.59, s32[64,1]{1,0:T(8,128)S(1)} %copy.67.index_ref, bf16[64,1024]{1,0:T(8,128)(2,1)S(1)} %get-tuple-element.99.refs_0_.refs_11_, ...), custom_call_target="tpu_custom_call" | custom-call | flops 402653184 | bytes 7340032 | tf_op jit(solution)/shard_map/project/pallas_call | solution.py:208
  213.9 4.8 %project.12 = (bf16[16,896]{1,0:T(8,128)(2,1)S(1)}, bf16[16,896]{1,0:T(8,128)(2,1)S(1)}, bf16[16,896]{1,0:T(8,128)(2,1)S(1)}, bf16[16,896]{1,0:T(8,128)(2,1)S(1)}) custom-call(s32[4]{0:T(128)S(1)} %copy-done.80, s32[4]{0:T(128)S(1)} %copy-done.59, s32[64,1]{1,0:T(8,128)S(1)} %copy.68.index_ref, bf16[64,1024]{1,0:T(8,128)(2,1)S(1)} %get-tuple-element.92.refs_0_.refs_11_, ...), custom_call_target="tpu_custom_call" | custom-call | flops 402653184 | bytes 7340032 | tf_op jit(solution)/shard_map/project/pallas_call | solution.py:208
  238.2 4.8 %output.12 = (bf16[64,1024]{1,0:T(8,128)(2,1)S(1)}, bf16[4,2,2,4,8,1024]{5,4,3,2,1,0:T(8,128)(2,1)}) custom-call(s32[7]{0:T(128)S(1)} %copy-done.64, s32[64,1]{1,0:T(8,128)S(1)} %copy.67.index_ref, bf16[16,2048]{1,0:T(8,128)(2,1)S(1)} %constant_dynamic-update-slice_fusion.20.refs_0_, ...), custom_call_target="tpu_custom_call", output_to_operand_aliasing={{1}: (15, {})} | custom-call | flops 268435456 | bytes 4194304 | tf_op jit(solution)/shard_map/output/pallas_call | solution.py:318
  244.9 4.8 %output.13 = (bf16[64,1024]{1,0:T(8,128)(2,1)S(1)}, bf16[4,2,2,4,8,1024]{5,4,3,2,1,0:T(8,128)(2,1)}) custom-call(s32[7]{0:T(128)S(1)} %copy-done.64, s32[64,1]{1,0:T(8,128)S(1)} %copy.68.index_ref, bf16[16,2048]{1,0:T(8,128)(2,1)S(1)} %constant_dynamic-update-slice_fusion.16.refs_0_, ...), custom_call_target="tpu_custom_call", output_to_operand_aliasing={{1}: (15, {})} | custom-call | flops 268435456 | bytes 4194304 | tf_op jit(solution)/shard_map/output/pallas_call | solution.py:318
  253.7 4.2 %collective-permute-done.73.refs_3_ = bf16[64,1024]{1,0:T(8,128)(2,1)} collective-permute-done((bf16[64,1024]{1,0:T(8,128)(2,1)S(1)}, bf16[64,1024]{1,0:T(8,128)(2,1)}, u32[]{:S(2)}, u32[]{:S(2)}) %collective-permute-start.73) | collective-permute-done | bytes 131104 | tf_op jit(solution)/shard_map/ppermute | solution.py:20
  259.9 5.5 %collective-permute-done.86.refs_2_ = bf16[64,1024]{1,0:T(8,128)(2,1)} collective-permute-done((bf16[64,1024]{1,0:T(8,128)(2,1)}, bf16[64,1024]{1,0:T(8,128)(2,1)}, u32[]{:S(2)}, u32[]{:S(2)}) %collective-permute-start.86) | collective-permute-done | bytes 131104 | tf_op jit(solution)/shard_map/ppermute | solution.py:20
  271.1 4.1 %project.15 = (bf16[16,896]{1,0:T(8,128)(2,1)S(1)}, bf16[16,896]{1,0:T(8,128)(2,1)S(1)}, bf16[16,896]{1,0:T(8,128)(2,1)S(1)}, bf16[16,896]{1,0:T(8,128)(2,1)S(1)}) custom-call(s32[4]{0:T(128)S(1)} %copy-done.81, s32[4]{0:T(128)S(1)} %copy-done.60, s32[64,1]{1,0:T(8,128)S(1)} %copy.71.index_ref, bf16[64,1024]{1,0:T(8,128)(2,1)S(1)} %get-tuple-element.115.refs_0_.refs_11_, ...), custom_call_target="tpu_custom_call" | custom-call | flops 402653184 | bytes 7340032 | tf_op jit(solution)/shard_map/project/pallas_call | solution.py:208
  277.3 4.7 %project.14 = (bf16[16,896]{1,0:T(8,128)(2,1)S(1)}, bf16[16,896]{1,0:T(8,128)(2,1)S(1)}, bf16[16,896]{1,0:T(8,128)(2,1)S(1)}, bf16[16,896]{1,0:T(8,128)(2,1)S(1)}) custom-call(s32[4]{0:T(128)S(1)} %copy-done.82, s32[4]{0:T(128)S(1)} %copy-done.60, s32[64,1]{1,0:T(8,128)S(1)} %copy.72.index_ref, bf16[64,1024]{1,0:T(8,128)(2,1)S(1)} %get-tuple-element.108.refs_0_.refs_11_, ...), custom_call_target="tpu_custom_call" | custom-call | flops 402653184 | bytes 7340032 | tf_op jit(solution)/shard_map/project/pallas_call | solution.py:208
  302.1 4.8 %output.14 = (bf16[64,1024]{1,0:T(8,128)(2,1)}, bf16[4,2,2,4,8,1024]{5,4,3,2,1,0:T(8,128)(2,1)}) custom-call(s32[7]{0:T(128)S(1)} %copy-done.65, s32[64,1]{1,0:T(8,128)S(1)} %copy.71.index_ref, bf16[16,2048]{1,0:T(8,128)(2,1)S(1)} %constant_dynamic-update-slice_fusion.28.refs_0_, ...), custom_call_target="tpu_custom_call", output_to_operand_aliasing={{1}: (15, {})} | custom-call | flops 268435456 | bytes 4194304 | tf_op jit(solution)/shard_map/output/pallas_call | solution.py:318
  306.9 4.8 %output.15 = (bf16[64,1024]{1,0:T(8,128)(2,1)}, bf16[4,2,2,4,8,1024]{5,4,3,2,1,0:T(8,128)(2,1)}) custom-call(s32[7]{0:T(128)S(1)} %copy-done.65, s32[64,1]{1,0:T(8,128)S(1)} %copy.72.index_ref, bf16[16,2048]{1,0:T(8,128)(2,1)S(1)} %constant_dynamic-update-slice_fusion.24.refs_0_, ...), custom_call_target="tpu_custom_call", output_to_operand_aliasing={{1}: (15, {})} | custom-call | flops 268435456 | bytes 4194304 | tf_op jit(solution)/shard_map/output/pallas_call | solution.py:318
  (489 shorter events, 183.6 us)
Async XLA Ops:
  9.8 21.0 %collective-permute-start.15 = (bf16[16,896]{1,0:T(8,128)(2,1)S(1)}, bf16[16,896]{1,0:T(8,128)(2,1)S(1)}, u32[]{:S(2)}, u32[]{:S(2)}) collective-permute-start(bf16[16,896]{1,0:T(8,128)(2,1)S(1)} %get-tuple-element.71), channel_id=1, source_target_pairs={{0,1},{1,0},{2,3},{3,2},{4,5},{5,4},{6,7},{7,6},{8,9},{9,8},{10,11... | collective-permute-start | bytes 86024 | tf_op jit(solution)/shard_map/ppermute | solution.py:20
  10.3 21.1 %collective-permute-start.16 = (bf16[16,896]{1,0:T(8,128)(2,1)S(1)}, bf16[16,896]{1,0:T(8,128)(2,1)S(1)}, u32[]{:S(2)}, u32[]{:S(2)}) collective-permute-start(bf16[16,896]{1,0:T(8,128)(2,1)S(1)} %get-tuple-element.72), channel_id=1, source_target_pairs={{0,2},{1,3},{2,0},{3,1},{4,6},{5,7},{6,4},{7,5},{8,10},{9,11},{10,... | collective-permute-start | bytes 86024 | tf_op jit(solution)/shard_map/ppermute | solution.py:20
  12.8 19.9 %collective-permute-start.17 = (bf16[16,896]{1,0:T(8,128)(2,1)}, bf16[16,896]{1,0:T(8,128)(2,1)S(1)}, u32[]{:S(2)}, u32[]{:S(2)}) collective-permute-start(bf16[16,896]{1,0:T(8,128)(2,1)} %get-tuple-element.73), channel_id=1, source_target_pairs={{0,3},{1,2},{2,1},{3,0},{4,7},{5,6},{6,5},{7,4},{8,11},{9,10},{10,... | collective-permute-start | bytes 86024 | tf_op jit(solution)/shard_map/ppermute | solution.py:20
  15.4 50.5 %collective-permute-start.9 = (bf16[256,1024]{1,0:T(8,128)(2,1)}, bf16[256,1024]{1,0:T(8,128)(2,1)}, u32[]{:S(2)}, u32[]{:S(2)}) collective-permute-start(bf16[256,1024]{1,0:T(8,128)(2,1)} %get-tuple-element.133), channel_id=1, source_target_pairs={{0,12},{4,8},{8,4},{12,0},{1,13},{5,9},{9,5},{13,1},{2,14},{6,10},... | collective-permute-start | bytes 1572872 | tf_op jit(solution)/shard_map/ppermute | solution.py:20
  19.3 48.2 %collective-permute-start.11 = (bf16[256,1024]{1,0:T(8,128)(2,1)}, bf16[256,1024]{1,0:T(8,128)(2,1)}, u32[]{:S(2)}, u32[]{:S(2)}) collective-permute-start(bf16[256,1024]{1,0:T(8,128)(2,1)} %get-tuple-element.134), channel_id=1, source_target_pairs={{0,8},{4,12},{8,0},{12,4},{1,9},{5,13},{9,1},{13,5},{2,10},{6,14},... | collective-permute-start | bytes 1572872 | tf_op jit(solution)/shard_map/ppermute | solution.py:20
  30.8 37.2 %collective-permute-start.13 = (bf16[256,1024]{1,0:T(8,128)(2,1)}, bf16[256,1024]{1,0:T(8,128)(2,1)}, u32[]{:S(2)}, u32[]{:S(2)}) collective-permute-start(bf16[256,1024]{1,0:T(8,128)(2,1)} %get-tuple-element.132), channel_id=1, source_target_pairs={{0,4},{4,0},{8,12},{12,8},{1,5},{5,1},{9,13},{13,9},{2,6},{6,2},{1... | collective-permute-start | bytes 1572872 | tf_op jit(solution)/shard_map/ppermute | solution.py:20
  39.0 15.1 %collective-permute-start.18 = (bf16[16,512]{1,0:T(8,128)(2,1)S(1)}, bf16[16,512]{1,0:T(8,128)(2,1)S(1)}, u32[]{:S(2)}, u32[]{:S(2)}) collective-permute-start(bf16[16,512]{1,0:T(8,128)(2,1)S(1)} %get-tuple-element.74), channel_id=1, source_target_pairs={{0,4},{4,0},{8,12},{12,8},{1,5},{5,1},{9,13},{13,9},{2,6},{6,2},{1... | collective-permute-start | bytes 49160 | tf_op jit(solution)/shard_map/ppermute | solution.py:20
  40.5 25.4 %collective-permute-start.19 = (bf16[16,512]{1,0:T(8,128)(2,1)S(1)}, bf16[16,512]{1,0:T(8,128)(2,1)S(1)}, u32[]{:S(2)}, u32[]{:S(2)}) collective-permute-start(bf16[16,512]{1,0:T(8,128)(2,1)S(1)} %get-tuple-element.74), channel_id=1, source_target_pairs={{0,8},{4,12},{8,0},{12,4},{1,9},{5,13},{9,1},{13,5},{2,10},{6,14},... | collective-permute-start | bytes 49160 | tf_op jit(solution)/shard_map/ppermute | solution.py:20
  54.2 15.4 %collective-permute-start.20 = (bf16[16,512]{1,0:T(8,128)(2,1)S(1)}, bf16[16,512]{1,0:T(8,128)(2,1)S(1)}, u32[]{:S(2)}, u32[]{:S(2)}) collective-permute-start(bf16[16,512]{1,0:T(8,128)(2,1)S(1)} %get-tuple-element.74), channel_id=1, source_target_pairs={{0,12},{4,8},{8,4},{12,0},{1,13},{5,9},{9,5},{13,1},{2,14},{6,10},... | collective-permute-start | bytes 49160 | tf_op jit(solution)/shard_map/ppermute | solution.py:20
  65.9 18.6 %collective-permute-start.10 = (bf16[256,1024]{1,0:T(8,128)(2,1)}, bf16[256,1024]{1,0:T(8,128)(2,1)S(1)}, u32[]{:S(2)}, u32[]{:S(2)}) collective-permute-start(bf16[256,1024]{1,0:T(8,128)(2,1)} %collective-permute-done.9.refs_5_), channel_id=1, source_target_pairs={{0,16},{16,0},{1,17},{17,1},{2,18},{18,2},{3,19},{19,3},{4,20},{20... | collective-permute-start | bytes 1572872 | tf_op jit(solution)/shard_map/ppermute | solution.py:20
  67.5 24.8 %collective-permute-start.12 = (bf16[256,1024]{1,0:T(8,128)(2,1)}, bf16[256,1024]{1,0:T(8,128)(2,1)S(1)}, u32[]{:S(2)}, u32[]{:S(2)}) collective-permute-start(bf16[256,1024]{1,0:T(8,128)(2,1)} %collective-permute-done.11.refs_7_), channel_id=1, source_target_pairs={{0,16},{16,0},{1,17},{17,1},{2,18},{18,2},{3,19},{19,3},{4,20},{20... | collective-permute-start | bytes 1572872 | tf_op jit(solution)/shard_map/ppermute | solution.py:20
  68.0 33.9 %collective-permute-start.14 = (bf16[256,1024]{1,0:T(8,128)(2,1)}, bf16[256,1024]{1,0:T(8,128)(2,1)S(1)}, u32[]{:S(2)}, u32[]{:S(2)}) collective-permute-start(bf16[256,1024]{1,0:T(8,128)(2,1)} %collective-permute-done.13.refs_9_), channel_id=1, source_target_pairs={{0,16},{16,0},{1,17},{17,1},{2,18},{18,2},{3,19},{19,3},{4,20},{20... | collective-permute-start | bytes 1572872 | tf_op jit(solution)/shard_map/ppermute | solution.py:20
  82.3 34.5 %collective-permute-start.6 = (bf16[16,2048]{1,0:T(8,128)(2,1)S(1)}, bf16[16,2048]{1,0:T(8,128)(2,1)}, u32[]{:S(2)}, u32[]{:S(2)}) collective-permute-start(bf16[16,2048]{1,0:T(8,128)(2,1)S(1)} %constant_dynamic-update-slice_fusion.refs_0_), channel_id=1, source_target_pairs={{0,1},{1,0},{2,3},{3,2},{4,5},{5,4},{6,7},{7,6},{8,9},{9,8},{10,11... | collective-permute-start | bytes 196616 | tf_op jit(solution)/shard_map/ppermute | solution.py:20
  83.8 33.1 %collective-permute-start.7 = (bf16[16,2048]{1,0:T(8,128)(2,1)S(1)}, bf16[16,2048]{1,0:T(8,128)(2,1)}, u32[]{:S(2)}, u32[]{:S(2)}) collective-permute-start(bf16[16,2048]{1,0:T(8,128)(2,1)S(1)} %constant_dynamic-update-slice_fusion.refs_0_), channel_id=1, source_target_pairs={{0,2},{1,3},{2,0},{3,1},{4,6},{5,7},{6,4},{7,5},{8,10},{9,11},{10,... | collective-permute-start | bytes 196616 | tf_op jit(solution)/shard_map/ppermute | solution.py:20
  84.5 32.4 %collective-permute-start.8 = (bf16[16,2048]{1,0:T(8,128)(2,1)S(1)}, bf16[16,2048]{1,0:T(8,128)(2,1)}, u32[]{:S(2)}, u32[]{:S(2)}) collective-permute-start(bf16[16,2048]{1,0:T(8,128)(2,1)S(1)} %constant_dynamic-update-slice_fusion.refs_0_), channel_id=1, source_target_pairs={{0,3},{1,2},{2,1},{3,0},{4,7},{5,6},{6,5},{7,4},{8,11},{9,10},{10,... | collective-permute-start | bytes 196616 | tf_op jit(solution)/shard_map/ppermute | solution.py:20
  108.8 21.9 %collective-permute-start.37 = (bf16[64,1024]{1,0:T(8,128)(2,1)S(1)}, bf16[64,1024]{1,0:T(8,128)(2,1)}, u32[]{:S(2)}, u32[]{:S(2)}) collective-permute-start(bf16[64,1024]{1,0:T(8,128)(2,1)S(1)} %get-tuple-element.83.refs_0_.refs_11_), channel_id=1, source_target_pairs={{0,12},{4,8},{8,4},{12,0},{1,13},{5,9},{9,5},{13,1},{2,14},{6,10},... | collective-permute-start | bytes 393224 | tf_op jit(solution)/shard_map/ppermute | solution.py:20
  116.0 21.8 %collective-permute-start.36 = (bf16[64,1024]{1,0:T(8,128)(2,1)S(1)}, bf16[64,1024]{1,0:T(8,128)(2,1)}, u32[]{:S(2)}, u32[]{:S(2)}) collective-permute-start(bf16[64,1024]{1,0:T(8,128)(2,1)S(1)} %get-tuple-element.83.refs_0_.refs_11_), channel_id=1, source_target_pairs={{0,4},{4,0},{8,12},{12,8},{1,5},{5,1},{9,13},{13,9},{2,6},{6,2},{1... | collective-permute-start | bytes 393224 | tf_op jit(solution)/shard_map/ppermute | solution.py:20
  131.8 18.3 %collective-permute-start.24 = (bf16[64,1024]{1,0:T(8,128)(2,1)S(1)}, bf16[64,1024]{1,0:T(8,128)(2,1)S(1)}, u32[]{:S(2)}, u32[]{:S(2)}) collective-permute-start(bf16[64,1024]{1,0:T(8,128)(2,1)S(1)} %get-tuple-element.76.refs_0_.refs_11_), channel_id=1, source_target_pairs={{0,4},{4,0},{8,12},{12,8},{1,5},{5,1},{9,13},{13,9},{2,6},{6,2},{1... | collective-permute-start | bytes 393224 | tf_op jit(solution)/shard_map/ppermute | solution.py:20
  137.7 12.4 %collective-permute-start.26 = (bf16[64,1024]{1,0:T(8,128)(2,1)}, bf16[64,1024]{1,0:T(8,128)(2,1)S(1)}, u32[]{:S(2)}, u32[]{:S(2)}) collective-permute-start(bf16[64,1024]{1,0:T(8,128)(2,1)} %collective-permute-done.25.refs_3_), channel_id=1, source_target_pairs={{0,4},{4,0},{8,12},{12,8},{1,5},{5,1},{9,13},{13,9},{2,6},{6,2},{1... | collective-permute-start | bytes 393224 | tf_op jit(solution)/shard_map/ppermute | solution.py:20
  188.0 25.8 %collective-permute-start.48 = (bf16[64,1024]{1,0:T(8,128)(2,1)S(1)}, bf16[64,1024]{1,0:T(8,128)(2,1)}, u32[]{:S(2)}, u32[]{:S(2)}) collective-permute-start(bf16[64,1024]{1,0:T(8,128)(2,1)S(1)} %get-tuple-element.92.refs_0_.refs_11_), channel_id=1, source_target_pairs={{0,4},{4,0},{8,12},{12,8},{1,5},{5,1},{9,13},{13,9},{2,6},{6,2},{1... | collective-permute-start | bytes 393224 | tf_op jit(solution)/shard_map/ppermute | solution.py:20
  190.1 11.9 %collective-permute-start.62 = (bf16[64,1024]{1,0:T(8,128)(2,1)}, bf16[64,1024]{1,0:T(8,128)(2,1)}, u32[]{:S(2)}, u32[]{:S(2)}) collective-permute-start(bf16[64,1024]{1,0:T(8,128)(2,1)} %collective-permute-done.61.refs_3_), channel_id=1, source_target_pairs={{0,4},{4,0},{8,12},{12,8},{1,5},{5,1},{9,13},{13,9},{2,6},{6,2},{1... | collective-permute-start | bytes 393224 | tf_op jit(solution)/shard_map/ppermute | solution.py:20
  194.5 19.4 %collective-permute-start.50 = (bf16[64,1024]{1,0:T(8,128)(2,1)}, bf16[64,1024]{1,0:T(8,128)(2,1)}, u32[]{:S(2)}, u32[]{:S(2)}) collective-permute-start(bf16[64,1024]{1,0:T(8,128)(2,1)} %collective-permute-done.49.refs_3_), channel_id=1, source_target_pairs={{0,4},{4,0},{8,12},{12,8},{1,5},{5,1},{9,13},{13,9},{2,6},{6,2},{1... | collective-permute-start | bytes 393224 | tf_op jit(solution)/shard_map/ppermute | solution.py:20
  251.6 25.7 %collective-permute-start.72 = (bf16[64,1024]{1,0:T(8,128)(2,1)S(1)}, bf16[64,1024]{1,0:T(8,128)(2,1)}, u32[]{:S(2)}, u32[]{:S(2)}) collective-permute-start(bf16[64,1024]{1,0:T(8,128)(2,1)S(1)} %get-tuple-element.108.refs_0_.refs_11_), channel_id=1, source_target_pairs={{0,4},{4,0},{8,12},{12,8},{1,5},{5,1},{9,13},{13,9},{2,6},{6,2},{1... | collective-permute-start | bytes 393224 | tf_op jit(solution)/shard_map/ppermute | solution.py:20
  257.9 19.4 %collective-permute-start.74 = (bf16[64,1024]{1,0:T(8,128)(2,1)}, bf16[64,1024]{1,0:T(8,128)(2,1)}, u32[]{:S(2)}, u32[]{:S(2)}) collective-permute-start(bf16[64,1024]{1,0:T(8,128)(2,1)} %collective-permute-done.73.refs_3_), channel_id=1, source_target_pairs={{0,4},{4,0},{8,12},{12,8},{1,5},{5,1},{9,13},{13,9},{2,6},{6,2},{1... | collective-permute-start | bytes 393224 | tf_op jit(solution)/shard_map/ppermute | solution.py:20
  (177 other events, 1843.3 us)

commit v2 on v1

v2 whole, which is shorter than its diff:
```python
import functools

import jax
import jax.numpy as jnp
from jax import lax
from jax.experimental import pallas as pl
from jax.experimental.pallas import tpu as pltpu
from jax.sharding import PartitionSpec as P

HD = 128
BATCHES = 1
CHUNKS = 2
EPSILON = 1e-05
MASKED = -1e30
LANES = 128
VMEM_BYTES = 20 * 1024 * 1024


def swap(x, axis, step):
    size = lax.axis_size(axis)
    return lax.ppermute(x, axis, [(i, i ^ step) for i in range(size)])


def parent_rows(index_ref, features):
    rows, width = index_ref.shape[0], features.shape[0]
    column = lax.broadcasted_iota(jnp.int32, (rows, width), 1)
    chosen = jnp.where(column == index_ref[...], 1.0, 0.0).astype(jnp.bfloat16)
    return jnp.dot(chosen, features, preferred_element_type=jnp.float32)


def embed_rows(places_ref, embed_ref, batch, level, columns):
    dp, _, per_block = embed_ref.shape[:3]
    blocks = []
    for step in range(dp):
        for request in range(per_block):
            block = embed_ref[places_ref[step], batch, request, level, :, columns]
            blocks.append(block.astype(jnp.float32))
    return jnp.concatenate(blocks, axis=0)


def cut_kernel(half, info_ref, weight_ref, *refs):
    outs, sems = refs[:-1], refs[-1]
    share = outs[0].shape[1]
    copies = []
    for place, out_ref in enumerate(outs):
        step, start, depth = half[place]
        row = start if step == 0 else pl.multiple_of(start + info_ref[0], 16)
        column = pl.multiple_of((info_ref[1] ^ step) * share, LANES)
        copies.append(
            pltpu.make_async_copy(
                weight_ref.at[pl.ds(row, depth), pl.ds(column, share)],
                out_ref,
                sems.at[place],
            )
        )
    for copy in copies:
        copy.start()
    for copy in copies:
        copy.wait()


def cut(info, w_out, plan, share):
    shapes = [(depth, share) for _, _, depth in plan]
    return pl.pallas_call(
        functools.partial(cut_kernel, plan),
        grid_spec=pltpu.PrefetchScalarGridSpec(
            num_scalar_prefetch=1,
            grid=(1,),
            in_specs=[pl.BlockSpec(memory_space=pl.ANY)],
            out_specs=[pl.BlockSpec(memory_space=pl.ANY) for _ in shapes],
            scratch_shapes=[pltpu.SemaphoreType.DMA((len(shapes),))],
        ),
        out_shape=[jax.ShapeDtypeStruct(shape, w_out.dtype) for shape in shapes],
        compiler_params=pltpu.CompilerParams(vmem_limit_bytes=VMEM_BYTES),
        name="cut",
    )(info, w_out)


def load_kernel(*refs):
    count = len(refs) // 2
    sources, held, sems = refs[:count], refs[count : 2 * count], refs[-1]
    copies = [
        pltpu.make_async_copy(source, target, sems.at[place])
        for place, (source, target) in enumerate(zip(sources, held))
    ]
    for copy in copies:
        copy.start()
    for copy in copies:
        copy.wait()


def load(*arrays):
    return pl.pallas_call(
        load_kernel,
        in_specs=[pl.BlockSpec(memory_space=pl.ANY) for _ in arrays],
        out_specs=[pl.BlockSpec(memory_space=pltpu.VMEM) for _ in arrays],
        out_shape=[pltpu.VMEM(x.shape, x.dtype) for x in arrays],
        scratch_shapes=[pltpu.SemaphoreType.DMA((len(arrays),))],
        compiler_params=pltpu.CompilerParams(vmem_limit_bytes=VMEM_BYTES),
        name="load",
    )(*arrays)


def project_kernel(level, batch, pieces, steps, dp, share_ref, places_ref, index_ref, *refs):
    features = refs[:pieces]
    embed_ref, gain_ref, query_ref, keyval_ref = refs[pieces : pieces + 4]
    out_refs = refs[pieces + 4 : pieces + 4 + dp]
    cols = query_ref.shape[0] // steps
    query = keyval = squares = None
    for step in range(steps):
        offset = pl.multiple_of(share_ref[step] * cols, LANES)
        columns = pl.ds(offset, cols)
        held = features[step][...] if pieces == steps else features[0][:, columns]
        state = parent_rows(index_ref, held) + embed_rows(
            places_ref, embed_ref, batch, level, columns
        )
        square = jnp.sum(state * state, axis=1, keepdims=True)
        gain = gain_ref[:, columns].astype(jnp.float32)
        scaled = (state * gain).astype(jnp.bfloat16)
        first = jnp.dot(scaled, query_ref[columns, :], preferred_element_type=jnp.float32)
        second = jnp.dot(scaled, keyval_ref[columns, :], preferred_element_type=jnp.float32)
        query = first if step == 0 else query + first
        keyval = second if step == 0 else keyval + second
        squares = square if step == 0 else squares + square
    head_cols = query.shape[1]
    width = head_cols + keyval.shape[1]
    rows = out_refs[0].shape[0]
    lane = lax.broadcasted_iota(jnp.int32, (rows, LANES), 1)
    for block in range(dp):
        span = slice(block * rows, (block + 1) * rows)
        high = squares[span].astype(jnp.bfloat16).astype(jnp.float32)
        low = squares[span] - high
        tail = jnp.where(lane == 0, high, jnp.where(lane == 1, low, 0.0))
        out_refs[block][:, :head_cols] = query[span].astype(jnp.bfloat16)
        out_refs[block][:, head_cols:width] = keyval[span].astype(jnp.bfloat16)
        out_refs[block][:, width:] = tail.astype(jnp.bfloat16)


def attend_kernel(
    dp, earlier, head_cols, model_width, base, branch, length_ref, *refs
):
    parts = refs[:dp]
    mask_ref, cache_ref = refs[dp : dp + 2]
    earlier_refs = refs[dp + 2 : dp + 2 + earlier]
    out_ref, fresh_ref = refs[dp + 2 + earlier :]
    total = parts[0][...].astype(jnp.float32)
    for part in parts[1:]:
        total = total + part[...].astype(jnp.float32)
    width = head_cols + fresh_ref.shape[1]
    squares = jnp.sum(total[:, width:], axis=1, keepdims=True)
    inv_rms = lax.rsqrt(squares / model_width + EPSILON)
    projected = (total[:, :width] * inv_rms).astype(jnp.bfloat16).astype(jnp.float32)
    fresh = projected[:, head_cols:]
    fresh_ref[...] = fresh
    _, _, cache, kv_cols = cache_ref.shape
    per_block = total.shape[0] // branch
    kv_heads = kv_cols // HD
    group = head_cols // HD // kv_heads
    positions = mask_ref.shape[1]
    tree = [ref[...] for ref in earlier_refs] + [fresh]
    blank = jnp.zeros((positions - branch * len(tree), HD), jnp.float32)
    column = lax.broadcasted_iota(jnp.int32, (group * branch, cache), 1)
    across = (((1,), (1,)), ((), ()))
    outs = []
    for request in range(per_block):
        span = slice(request * branch, (request + 1) * branch)
        valid = column < length_ref[base + request]
        allowed = jnp.concatenate([mask_ref[span, :]] * group, axis=0) > 0.5
        heads = []
        for kv in range(kv_heads):
            first = kv * group
            queries = jnp.concatenate(
                [
                    projected[span, (first + g) * HD : (first + g + 1) * HD]
                    for g in range(group)
                ],
                axis=0,
            ).astype(jnp.bfloat16)
            key_cols = slice(kv * HD, (kv + 1) * HD)
            value_cols = slice(kv_cols + kv * HD, kv_cols + (kv + 1) * HD)
            filler = [blank] if blank.shape[0] else []
            tree_keys = jnp.concatenate(
                [level[span, key_cols] for level in tree] + filler, axis=0
            ).astype(jnp.bfloat16)
            tree_values = jnp.concatenate(
                [level[span, value_cols] for level in tree] + filler, axis=0
            ).astype(jnp.bfloat16)
            keys = cache_ref[base + request, 0, :, key_cols]
            values = cache_ref[base + request, 1, :, key_cols]
            scale = HD**-0.5
            near = lax.dot_general(
                queries, keys, across, preferred_element_type=jnp.float32
            )
            far = lax.dot_general(
                queries, tree_keys, across, preferred_element_type=jnp.float32
            )
            near = jnp.where(valid, near * scale, MASKED)
            far = jnp.where(allowed, far * scale, MASKED)
            top = jnp.maximum(
                jnp.max(near, axis=1, keepdims=True), jnp.max(far, axis=1, keepdims=True)
            )
            near = jnp.exp(near - top)
            far = jnp.exp(far - top)
            below = jnp.sum(near, axis=1, keepdims=True) + jnp.sum(far, axis=1, keepdims=True)
            mixed = jnp.dot(
                (near / below).astype(jnp.bfloat16), values, preferred_element_type=jnp.float32
            ) + jnp.dot(
                (far / below).astype(jnp.bfloat16), tree_values, preferred_element_type=jnp.float32
            )
            heads += [mixed[g * branch : (g + 1) * branch] for g in range(group)]
        outs.append(jnp.concatenate(heads, axis=1))
    out_ref[...] = jnp.concatenate(outs, axis=0).astype(jnp.bfloat16)


def output_kernel(level, batch, dp, weights, keep, info_ref, index_ref, *refs):
    attended = refs[:dp]
    weight_refs = refs[dp : dp + len(weights)]
    feature_ref, embed_ref = refs[dp + len(weights) : dp + len(weights) + 2]
    rest = refs[dp + len(weights) + 2 :]
    fresh_ref, gathered_ref = rest[0], rest[-1]
    rows = attended[0].shape[0]
    share = fresh_ref.shape[1]
    for step in range(dp):
        gathered_ref[step * rows : (step + 1) * rows, :] = attended[step][...]
    spans = []
    for weight_ref, (start, side) in zip(weight_refs, weights):
        depth = weight_ref.shape[0]
        if side is not None:
            start = pl.multiple_of(start + info_ref[dp + side], LANES)
        spans.append(pl.ds(start, depth))
        if keep:
            rest[1][spans[-1], :] = weight_ref[...]
    if keep:
        weight_refs, spans = [rest[1]], [slice(None)]
    offset = pl.multiple_of(info_ref[dp + 2] * share, LANES)
    block = min(2 * LANES, share)
    for start in range(0, share, block):
        if feature_ref.shape[1] == share:
            held = feature_ref[:, start : start + block]
        else:
            held = feature_ref[:, pl.ds(offset + start, block)]
        fresh = parent_rows(index_ref, held) + embed_rows(
            info_ref, embed_ref, batch, level, pl.ds(offset + start, block)
        )
        for weight_ref, span in zip(weight_refs, spans):
            fresh = fresh + jnp.dot(
                gathered_ref[:, span],
                weight_ref[:, start : start + block],
                preferred_element_type=jnp.float32,
            )
        fresh_ref[:, start : start + block] = fresh.astype(jnp.bfloat16)


def store_kernel(info_ref, fresh_ref, *refs):
    out_ref = refs[-1]
    dp, per_block, branch = out_ref.shape[0], out_ref.shape[2], out_ref.shape[4]
    fresh = fresh_ref[...].astype(jnp.float32)
    for step in range(dp):
        for request in range(per_block):
            start = (step * per_block + request) * branch
            block = fresh[start : start + branch].astype(jnp.bfloat16)
            out_ref[info_ref[step], 0, request, 0] = block


def full(x):
    return pl.BlockSpec(x.shape, lambda i, *_: (0,) * x.ndim)


def project(level, batch, share_ids, places, index, pieces, embeds, gain, w_query, keyval):
    dp, _, per_block, _, branch, feat_cols = embeds.shape
    steps = share_ids.shape[0]
    head_cols, kv_cols = w_query.shape[1], keyval.shape[1]
    rows = per_block * branch
    width = head_cols + kv_cols + LANES
    operands = [index, *pieces, embeds, gain, w_query, keyval]
    return pl.pallas_call(
        functools.partial(project_kernel, level, batch, len(pieces), steps, dp),
        grid_spec=pltpu.PrefetchScalarGridSpec(
            num_scalar_prefetch=2,
            grid=(),
            in_specs=[pl.BlockSpec(memory_space=pltpu.VMEM)] * len(operands),
            out_specs=[pl.BlockSpec(memory_space=pltpu.VMEM)] * dp,
        ),
        out_shape=[jax.ShapeDtypeStruct((rows, width), jnp.bfloat16)] * dp,
        compiler_params=pltpu.CompilerParams(vmem_limit_bytes=VMEM_BYTES),
        cost_estimate=pl.CostEstimate(
            flops=2 * dp * rows * feat_cols * (head_cols + kv_cols),
            bytes_accessed=4 * dp * rows * feat_cols,
            transcendentals=0,
        ),
        name="project",
    )(share_ids, places, *operands)


def attend(batch, per_block, model_width, head_cols, lengths, parts, mask, cache, earlier):
    rows, width = parts[0].shape
    fresh_cols = width - LANES - head_cols
    operands = [*parts, mask, cache, *earlier]
    return pl.pallas_call(
        functools.partial(
            attend_kernel,
            len(parts),
            len(earlier),
            head_cols,
            model_width,
            batch * per_block,
            rows // per_block,
        ),
        grid_spec=pltpu.PrefetchScalarGridSpec(
            num_scalar_prefetch=1,
            grid=(),
            in_specs=[pl.BlockSpec(memory_space=pltpu.VMEM)] * len(operands),
            out_specs=[pl.BlockSpec(memory_space=pltpu.VMEM)] * 2,
        ),
        out_shape=[
            jax.ShapeDtypeStruct((rows, head_cols), jnp.bfloat16),
            jax.ShapeDtypeStruct((rows, fresh_cols), jnp.float32),
        ],
        compiler_params=pltpu.CompilerParams(vmem_limit_bytes=VMEM_BYTES),
        cost_estimate=pl.CostEstimate(
            flops=4 * rows * head_cols * cache.shape[2],
            bytes_accessed=4 * cache.shape[2] * per_block * HD,
            transcendentals=rows * head_cols * 4,
        ),
        name="attend",
    )(lengths, *operands)


def output(level, batch, info, index, attended, weights, features, embeds, share_cols):
    dp, _, per_block, _, branch, _ = embeds.shape
    rows = dp * per_block * branch
    arrays = [w for w, _, _ in weights]
    places = [(start, side) for _, start, side in weights]
    depth = sum(w.shape[0] for w in arrays)
    keep = len(weights) > 1
    operands = [index, *attended, *arrays, features, embeds]
    out_shape = [jax.ShapeDtypeStruct((rows, share_cols), jnp.bfloat16)]
    if keep:
        out_shape.append(pltpu.VMEM((depth, share_cols), jnp.bfloat16))
    return pl.pallas_call(
        functools.partial(output_kernel, level, batch, dp, places, keep),
        grid_spec=pltpu.PrefetchScalarGridSpec(
            num_scalar_prefetch=1,
            grid=(),
            in_specs=[pl.BlockSpec(memory_space=pltpu.VMEM)] * len(operands),
            out_specs=[pl.BlockSpec(memory_space=pltpu.VMEM)] * len(out_shape),
            scratch_shapes=[pltpu.VMEM((rows, depth), jnp.bfloat16)],
        ),
        out_shape=out_shape,
        compiler_params=pltpu.CompilerParams(vmem_limit_bytes=VMEM_BYTES),
        cost_estimate=pl.CostEstimate(
            flops=2 * rows * depth * share_cols,
            bytes_accessed=2 * rows * depth,
            transcendentals=0,
        ),
        name="output",
    )(info, *operands)


def store(level, batch, shape, info, fresh, held):
    dp, _, per_block, _, branch, share_cols = shape
    operands = [info, fresh]
    in_specs = [full(fresh)]
    aliases = {}
    if held is not None:
        in_specs.append(pl.BlockSpec(memory_space=pl.ANY))
        aliases = {2: 0}
        operands.append(held)
    return pl.pallas_call(
        store_kernel,
        grid_spec=pltpu.PrefetchScalarGridSpec(
            num_scalar_prefetch=1,
            grid=(1,),
            in_specs=in_specs,
            out_specs=pl.BlockSpec(
                (dp, 1, per_block, 1, branch, share_cols),
                lambda i, s: (0, batch, 0, level, 0, 0),
            ),
        ),
        out_shape=jax.ShapeDtypeStruct(shape, jnp.bfloat16),
        input_output_aliases=aliases,
        compiler_params=pltpu.CompilerParams(vmem_limit_bytes=VMEM_BYTES),
        cost_estimate=pl.CostEstimate(
            flops=0, bytes_accessed=4 * fresh.size, transcendentals=0
        ),
        name="store",
    )(*operands)


def tree_masks(own_parents, depths, branch):
    columns = jnp.arange(branch, dtype=jnp.int32)
    masks = []
    for level in range(depths):
        current = jnp.broadcast_to(columns, own_parents.shape[:2] + (branch,))
        blocks = [columns == current[..., None]]
        for upper in range(level, 0, -1):
            above = own_parents[:, :, upper - 1]
            current = jnp.sum(
                jnp.where(current[..., None] == columns, above[:, :, None, :], 0), axis=3
            )
            blocks.append(columns == current[..., None])
        blocks = blocks[::-1]
        blank = jnp.zeros(blocks[0].shape, bool)
        blocks += [blank] * (depths - len(blocks))
        joined = jnp.concatenate(blocks, axis=3).astype(jnp.float32)
        masks.append(joined.reshape(own_parents.shape[0], -1, depths * branch))
    return masks


def shards(
    root_features,
    branch_embeds,
    parents,
    cache_lengths,
    cache_kv,
    norm_gain,
    w_query,
    w_keyval,
    w_out,
):
    requests, depths, branch, feat_cols = branch_embeds.shape
    dp, tensor, groups = (lax.axis_size(name) for name in ("dp", "tensor", "groups"))
    dp_index, tensor_index, group_index = (
        lax.axis_index(name).astype(jnp.int32) for name in ("dp", "tensor", "groups")
    )
    local = requests // dp
    batches = BATCHES
    per_block = local // batches
    share_cols = feat_cols // tensor
    head_cols = w_query.shape[1]
    head_rows = w_out.shape[0]
    by_swaps = tensor == 4 and groups == 2

    if by_swaps:
        half = head_rows // 2
        depth = half // CHUNKS
        plan = [(0, 0, head_rows)]
        for chunk in range(CHUNKS):
            plan += [(step, chunk * depth, depth) for step in (3, 2, 1)]
        cuts = cut(
            jnp.stack([group_index * half, tensor_index]), w_out, tuple(plan), share_cols
        )
        weights = [(cuts[0], 0, None)]
        for (step, start, _), sent in zip(plan[1:], cuts[1:]):
            arrived = swap(sent, "tensor", step)
            weights.append((arrived, step * head_rows + start, 0))
            weights.append((swap(arrived, "groups", 1), step * head_rows + start, 1))
    else:
        half = 0
        spread = lax.all_to_all(w_out, "tensor", 1, 0, tiled=True)
        weights = [(load(spread)[0], 0, None)]

    embeds = branch_embeds.reshape(dp, batches, per_block, depths, branch, feat_cols)
    gain = norm_gain.reshape(1, feat_cols)
    keyval = w_keyval.reshape(feat_cols, -1)
    w_query, keyval, embeds, cache_kv = load(w_query, keyval, embeds, cache_kv)
    places = jnp.stack([dp_index ^ step for step in range(dp)])
    info = jnp.concatenate(
        [
            places,
            jnp.stack([group_index * half, (1 - group_index) * half, tensor_index]),
        ]
    )
    if by_swaps:
        share_ids = jnp.stack([tensor_index ^ step for step in range(tensor)])
    else:
        share_ids = jnp.zeros((1,), jnp.int32)

    split = parents.reshape(dp, batches, per_block, depths - 1, branch)
    ordered = jnp.stack(
        [lax.dynamic_index_in_dim(split, dp_index ^ step, 0, False) for step in range(dp)]
    )
    slot = (
        jnp.arange(dp, dtype=jnp.int32)[:, None] * per_block
        + jnp.arange(per_block, dtype=jnp.int32)[None, :]
    )
    rows = dp * per_block * branch
    indices = []
    for level in range(depths):
        row = []
        for batch in range(batches):
            if level == 0:
                request = (
                    places[:, None] * local
                    + batch * per_block
                    + jnp.arange(per_block, dtype=jnp.int32)[None, :]
                )
                place = jnp.broadcast_to(request[:, :, None], (dp, per_block, branch))
            else:
                place = slot[:, :, None] * branch + ordered[:, batch, :, level - 1]
            row.append(place.reshape(rows, 1))
        indices.append(row)
    masks = tree_masks(ordered[0], depths, branch)

    earlier = [[] for _ in range(batches)]
    shares = [root_features] * batches
    gathered = [[root_features]] * batches
    held = None
    for level in range(depths):
        attended = []
        for batch in range(batches):
            sums = project(
                level,
                batch,
                share_ids,
                places,
                indices[level][batch],
                gathered[batch],
                embeds,
                gain,
                w_query,
                keyval,
            )
            parts = [sums[0]] + [swap(sums[step], "dp", step) for step in range(1, dp)]
            mixed, fresh = attend(
                batch,
                per_block,
                feat_cols * dp,
                head_cols,
                cache_lengths,
                parts,
                masks[level][batch],
                cache_kv,
                earlier[batch],
            )
            earlier[batch] = earlier[batch] + [fresh]
            if by_swaps:
                heads = [mixed] + [swap(mixed, "tensor", step) for step in range(1, tensor)]
                joined = jnp.concatenate(heads, axis=1)
            else:
                joined = lax.all_gather(mixed, "tensor", axis=1, tiled=True)
            attended.append([joined] + [swap(joined, "dp", step) for step in range(1, dp)])
        for batch in range(batches):
            shares[batch], *kept = output(
                level,
                batch,
                info,
                indices[level][batch],
                attended[batch],
                weights,
                shares[batch],
                embeds,
                share_cols,
            )
            if kept:
                weights = [(kept[0], 0, None)]
            held = store(
                level, batch, embeds.shape[:-1] + (share_cols,), info, shares[batch], held
            )
            if level + 1 == depths:
                continue
            own = shares[batch]
            if by_swaps:
                far = swap(own, "tensor", 3)
                gathered[batch] = [own, swap(own, "tensor", 1), swap(far, "tensor", 1), far]
            else:
                gathered[batch] = [lax.all_gather(own, "tensor", axis=1, tiled=True)]
    return held.reshape(requests, depths, branch, share_cols)


def solution(mesh):
    return jax.shard_map(
        shards,
        mesh=mesh,
        in_specs=(
            P("groups", "dp"),
            P("groups", None, None, "dp"),
            P("groups", None, None),
            P(("groups", "dp")),
            P(("groups", "dp"), None, None, "tensor"),
            P("dp"),
            P("dp", "tensor"),
            P("dp", None, "tensor"),
            P("tensor", "dp"),
        ),
        out_specs=P("groups", None, None, ("dp", "tensor")),
        check_vma=False,
    )
```

time: 313 us -> 288 us (0.920)
  Pallas kernels: 84.6 us -> 41.4 us
  waiting for transfers between devices: 73.3 us -> 108 us
  starting transfers between devices: 93.1 us -> 66.6 us
  other arithmetic: 3.19 us -> 8.86 us
  local copies, waits for them, and re-layouts: 56.2 us -> 60.7 us
    pallas_call x16 -> x14, Pallas kernels: 71.6 us -> 31.6 us  [the longest x4 14.1 us: project(): pl.pallas_call(functools.partial(project_kernel, level, batch, len(pieces...]
    ppermute x96 -> x57, waiting for transfers between devices: 73.3 us -> 108 us  [swap(): return lax.ppermute(x, axis, [(i, i ^ step) for i in range(size)])]
    ppermute x96 -> x57, starting transfers between devices: 93.1 us -> 66.6 us  [swap(): return lax.ppermute(x, axis, [(i, i ^ step) for i in range(size)])]
    unnamed x236 -> x164, local copies, waits for them, and re-layouts: 41.8 us -> 50 us
    eq x0 -> x6, local copies, waits for them, and re-layouts: none -> 4.7 us  [the longest x3 2.7 us: tree_masks(): blocks.append(columns == current[..., None])]
    dynamic_slice x2 -> x0, local copies, waits for them, and re-layouts: 3.84 us -> none  [the longest x1 2.55 us: shards(): lax.dynamic_slice(w_out, (group_index * half, (tensor_index ^ step) * sha...]
    pallas_call x8 -> x4, Pallas kernels: 13 us -> 9.8 us  [attend(): pl.pallas_call(functools.partial(attend_kernel, len(parts), len(earlier),...]
  transfers between devices with their start and end apart: 96 -> 57, of which waited for: 18 -> 33; matrix products, arithmetic and copies ran while one was open for 6% -> 7% of each run, Pallas kernels for 24% -> 3%
where the time goes in v2:
time: 288 us; the launch traced here: 286 us
  waiting for transfers between devices  108 us (38%)
  starting transfers between devices  66.6 us (23%)
  local copies, waits for them, and re-layouts  60.7 us (21%)
  Pallas kernels  41.4 us (14%)
  other arithmetic  8.86 us (3%)
    ppermute x57, waiting for transfers between devices, swap(): return lax.ppermute(x, axis, [(i, i ^ step) for i in range(size)])  108 us
    ppermute x57, starting transfers between devices, swap(): return lax.ppermute(x, axis, [(i, i ^ step) for i in range(size)])  66.6 us
    unnamed x164, local copies, waits for them, and re-layouts  50 us
    pallas_call x4, Pallas kernels, project(): pl.pallas_call(functools.partial(project_kernel, level, batch, len(pieces...  14.1 us
    pallas_call x4, Pallas kernels, attend(): pl.pallas_call(functools.partial(attend_kernel, len(parts), len(earlier),...  9.8 us
    pallas_call x4, Pallas kernels, output(): pl.pallas_call(functools.partial(output_kernel, level, batch, dp, places,...  9.1 us
    pallas_call x4, Pallas kernels, store(): pl.pallas_call(store_kernel, grid_spec=pltpu.PrefetchScalarGridSpec(num_s...  6 us
  transfers between devices with their start and end apart: 57, of which 33 were waited for; matrix products, arithmetic and copies ran while one was open for 7% of the time, Pallas kernels for 3%

profile of v2, /device:TPU:0, one launch (start us, length us, event | category | flops | bytes accessed | tf_op | source)
XLA Modules:
  0.0 286.4 jit_solution(10901624872978860318)
XLA Ops:
  7.5 3.3 %project.4 = (bf16[32,896]{1,0:T(8,128)(2,1)S(1)}, bf16[32,896]{1,0:T(8,128)(2,1)}, bf16[32,896]{1,0:T(8,128)(2,1)}, bf16[32,896]{1,0:T(8,128)(2,1)}) custom-call(s32[4]{0:T(128)S(1)} %get-tuple-element.100.share_ref, s32[4]{0:T(128)S(1)} %get-tuple-element.83.places_ref, s32[128,1]{1,0:T(8,128)S(1)} %reshape.339.index_ref, bf16[16,4096]{1,0:T(8,128)(2,1)S(1)} %copy-done.25, ...), custom_call_target="tpu_custom_call" | custom-call | flops 805306368 | bytes 2097152 | tf_op jit(solution)/shard_map/project/pallas_call | solution.py:276
  20.8 3.8 %collective-permute-start.9 = (bf16[128,1024]{1,0:T(8,128)(2,1)}, bf16[128,1024]{1,0:T(8,128)(2,1)S(1)}, u32[]{:S(2)}, u32[]{:S(2)}) collective-permute-start(bf16[128,1024]{1,0:T(8,128)(2,1)} %get-tuple-element.51), channel_id=1, source_target_pairs={{0,12},{4,8},{8,4},{12,0},{1,13},{5,9},{9,5},{13,1},{2,14},{6,10},... | collective-permute-start | bytes 786440 | tf_op jit(solution)/shard_map/ppermute | solution.py:21
  35.9 3.0 %attend.4 = (bf16[32,512]{1,0:T(8,128)(2,1)S(1)}, f32[32,256]{1,0:T(8,128)S(1)}) custom-call(s32[4]{0:T(128)S(1)} %copy-done.57, bf16[32,896]{1,0:T(8,128)(2,1)S(1)} %copy-done.42, bf16[32,896]{1,0:T(8,128)(2,1)S(1)} %copy-done.44, bf16[32,896]{1,0:T(8,128)(2,1)} %collective-permute-done.1.refs_2_, bf16[32,896]{1,0:T(8,128)(2,1)} %collective-permute-done.2.refs_3_, ...), custom_call_target="tpu_custom_call" | custom-call | flops 33554432 | bytes 1048576 | tf_op jit(solution)/shard_map/attend/pallas_call | solution.py:299
  44.3 5.7 %collective-permute-done.4 = bf16[32,512]{1,0:T(8,128)(2,1)S(1)} collective-permute-done((bf16[32,512]{1,0:T(8,128)(2,1)S(1)}, bf16[32,512]{1,0:T(8,128)(2,1)S(1)}, u32[]{:S(2)}, u32[]{:S(2)}) %collective-permute-start.4) | collective-permute-done | bytes 32800 | tf_op jit(solution)/shard_map/ppermute | solution.py:21
  68.4 2.7 collective-permute-done.15.refs_11_
  72.6 9.6 %collective-permute-done.17.refs_13_ = bf16[128,1024]{1,0:T(8,128)(2,1)} collective-permute-done((bf16[128,1024]{1,0:T(8,128)(2,1)}, bf16[128,1024]{1,0:T(8,128)(2,1)}, u32[]{:S(2)}, u32[]{:S(2)}) %collective-permute-start.17) | collective-permute-done | bytes 262176 | tf_op jit(solution)/shard_map/ppermute | solution.py:21
  87.8 4.0 %collective-permute-done.16.refs_12_ = bf16[128,1024]{1,0:T(8,128)(2,1)} collective-permute-done((bf16[128,1024]{1,0:T(8,128)(2,1)}, bf16[128,1024]{1,0:T(8,128)(2,1)}, u32[]{:S(2)}, u32[]{:S(2)}) %collective-permute-start.16) | collective-permute-done | bytes 262176 | tf_op jit(solution)/shard_map/ppermute | solution.py:21
  91.8 5.6 %collective-permute-done.18.refs_14_ = bf16[128,1024]{1,0:T(8,128)(2,1)} collective-permute-done((bf16[128,1024]{1,0:T(8,128)(2,1)}, bf16[128,1024]{1,0:T(8,128)(2,1)}, u32[]{:S(2)}, u32[]{:S(2)}) %collective-permute-start.18) | collective-permute-done | bytes 262176 | tf_op jit(solution)/shard_map/ppermute | solution.py:21
  97.4 3.0 %collective-permute-done.20.refs_16_ = bf16[128,1024]{1,0:T(8,128)(2,1)S(1)} collective-permute-done((bf16[128,1024]{1,0:T(8,128)(2,1)}, bf16[128,1024]{1,0:T(8,128)(2,1)S(1)}, u32[]{:S(2)}, u32[]{:S(2)}) %collective-permute-start.20) | collective-permute-done | bytes 262176 | tf_op jit(solution)/shard_map/ppermute | solution.py:21
  111.0 3.3 %output.4 = (bf16[128,1024]{1,0:T(8,128)(2,1)S(1)}, bf16[2048,1024]{1,0:T(8,128)(2,1)S(1)}) custom-call(s32[7]{0:T(128)S(1)} %concatenate.45.info_ref, s32[128,1]{1,0:T(8,128)S(1)} %reshape.339.index_ref, bf16[32,2048]{1,0:T(8,128)(2,1)S(1)} %copy-done.32, bf16[32,2048]{1,0:T(8,128)(2,1)S(1)} %copy-done.34, bf16[32,2048]{1,0:T(8,128)(2,1)S(1)} %copy-done.36, ...), custom_call_target="tpu_custom_call" | custom-call | flops 536870912 | bytes 524288 | tf_op jit(solution)/shard_map/output/pallas_call | solution.py:340
  121.4 5.8 %collective-permute-done.22.refs_3_ = bf16[128,1024]{1,0:T(8,128)(2,1)} collective-permute-done((bf16[128,1024]{1,0:T(8,128)(2,1)S(1)}, bf16[128,1024]{1,0:T(8,128)(2,1)}, u32[]{:S(2)}, u32[]{:S(2)}) %collective-permute-start.22) | collective-permute-done | bytes 262176 | tf_op jit(solution)/shard_map/ppermute | solution.py:21
  127.2 2.8 collective-permute-start.23
  132.8 3.6 %collective-permute-done.23.refs_2_ = bf16[128,1024]{1,0:T(8,128)(2,1)} collective-permute-done((bf16[128,1024]{1,0:T(8,128)(2,1)}, bf16[128,1024]{1,0:T(8,128)(2,1)}, u32[]{:S(2)}, u32[]{:S(2)}) %collective-permute-start.23) | collective-permute-done | bytes 262176 | tf_op jit(solution)/shard_map/ppermute | solution.py:21
  140.8 3.5 %project.5 = (bf16[32,896]{1,0:T(8,128)(2,1)S(1)}, bf16[32,896]{1,0:T(8,128)(2,1)S(1)}, bf16[32,896]{1,0:T(8,128)(2,1)S(1)}, bf16[32,896]{1,0:T(8,128)(2,1)S(1)}) custom-call(s32[4]{0:T(128)S(1)} %get-tuple-element.100.share_ref, s32[4]{0:T(128)S(1)} %get-tuple-element.83.places_ref, s32[128,1]{1,0:T(8,128)S(1)} %copy.47.index_ref, ...), custom_call_target="tpu_custom_call" | custom-call | flops 805306368 | bytes 2097152 | tf_op jit(solution)/shard_map/project/pallas_call | solution.py:276
  161.6 4.4 %collective-permute-done.31.refs_2_ = bf16[32,2048]{1,0:T(8,128)(2,1)S(1)} collective-permute-done((bf16[32,2048]{1,0:T(8,128)(2,1)S(1)}, bf16[32,2048]{1,0:T(8,128)(2,1)S(1)}, u32[]{:S(2)}, u32[]{:S(2)}) %collective-permute-start.31) | collective-permute-done | bytes 131104 | tf_op jit(solution)/shard_map/ppermute | solution.py:21
  172.9 8.8 %collective-permute-done.34.refs_3_ = bf16[128,1024]{1,0:T(8,128)(2,1)} collective-permute-done((bf16[128,1024]{1,0:T(8,128)(2,1)S(1)}, bf16[128,1024]{1,0:T(8,128)(2,1)}, u32[]{:S(2)}, u32[]{:S(2)}) %collective-permute-start.34) | collective-permute-done | bytes 262176 | tf_op jit(solution)/shard_map/ppermute | solution.py:21
  181.6 3.2 %collective-permute-start.35 = (bf16[128,1024]{1,0:T(8,128)(2,1)}, bf16[128,1024]{1,0:T(8,128)(2,1)}, u32[]{:S(2)}, u32[]{:S(2)}) collective-permute-start(bf16[128,1024]{1,0:T(8,128)(2,1)} %collective-permute-done.34.refs_3_), channel_id=1, source_target_pairs={{0,4},{4,0},{8,12},{12,8},{1,5},{5,1},{9,13},{13,9},{2,6},{6,2},{1... | collective-permute-start | bytes 786440 | tf_op jit(solution)/shard_map/ppermute | solution.py:21
  186.7 5.5 %collective-permute-done.35.refs_2_ = bf16[128,1024]{1,0:T(8,128)(2,1)} collective-permute-done((bf16[128,1024]{1,0:T(8,128)(2,1)}, bf16[128,1024]{1,0:T(8,128)(2,1)}, u32[]{:S(2)}, u32[]{:S(2)}) %collective-permute-start.35) | collective-permute-done | bytes 262176 | tf_op jit(solution)/shard_map/ppermute | solution.py:21
  197.8 3.5 %project.6 = (bf16[32,896]{1,0:T(8,128)(2,1)S(1)}, bf16[32,896]{1,0:T(8,128)(2,1)S(1)}, bf16[32,896]{1,0:T(8,128)(2,1)S(1)}, bf16[32,896]{1,0:T(8,128)(2,1)S(1)}) custom-call(s32[4]{0:T(128)S(1)} %copy-done.55, s32[4]{0:T(128)S(1)} %copy-done.52, s32[128,1]{1,0:T(8,128)S(1)} %copy.49.index_ref, bf16[128,1024]{1,0:T(8,128)(2,1)S(1)} %output.5.refs_0_.refs_5_.fresh_ref, ...), custom_call_target="tpu_custom_call" | custom-call | flops 805306368 | bytes 2097152 | tf_op jit(solution)/shard_map/project/pallas_call | solution.py:276
  218.6 4.4 %collective-permute-done.43.refs_2_ = bf16[32,2048]{1,0:T(8,128)(2,1)S(1)} collective-permute-done((bf16[32,2048]{1,0:T(8,128)(2,1)S(1)}, bf16[32,2048]{1,0:T(8,128)(2,1)S(1)}, u32[]{:S(2)}, u32[]{:S(2)}) %collective-permute-start.43) | collective-permute-done | bytes 131104 | tf_op jit(solution)/shard_map/ppermute | solution.py:21
  229.4 9.2 %collective-permute-done.46.refs_3_ = bf16[128,1024]{1,0:T(8,128)(2,1)} collective-permute-done((bf16[128,1024]{1,0:T(8,128)(2,1)}, bf16[128,1024]{1,0:T(8,128)(2,1)}, u32[]{:S(2)}, u32[]{:S(2)}) %collective-permute-start.46) | collective-permute-done | bytes 262176 | tf_op jit(solution)/shard_map/ppermute | solution.py:21
  243.6 5.5 %collective-permute-done.47.refs_2_ = bf16[128,1024]{1,0:T(8,128)(2,1)} collective-permute-done((bf16[128,1024]{1,0:T(8,128)(2,1)}, bf16[128,1024]{1,0:T(8,128)(2,1)}, u32[]{:S(2)}, u32[]{:S(2)}) %collective-permute-start.47) | collective-permute-done | bytes 262176 | tf_op jit(solution)/shard_map/ppermute | solution.py:21
  254.7 3.8 %project.7 = (bf16[32,896]{1,0:T(8,128)(2,1)S(1)}, bf16[32,896]{1,0:T(8,128)(2,1)S(1)}, bf16[32,896]{1,0:T(8,128)(2,1)S(1)}, bf16[32,896]{1,0:T(8,128)(2,1)S(1)}) custom-call(s32[4]{0:T(128)S(1)} %copy-done.56, s32[4]{0:T(128)S(1)} %copy-done.53, s32[128,1]{1,0:T(8,128)S(1)} %copy.51.index_ref, bf16[128,1024]{1,0:T(8,128)(2,1)} %output.6.refs_0_.refs_5_.fresh_ref, ...), custom_call_target="tpu_custom_call" | custom-call | flops 805306368 | bytes 2097152 | tf_op jit(solution)/shard_map/project/pallas_call | solution.py:276
  260.5 2.7 collective-permute-done.49.refs_2_
  (320 shorter events, 175.2 us)
Async XLA Ops:
  11.4 21.6 %collective-permute-start = (bf16[32,896]{1,0:T(8,128)(2,1)}, bf16[32,896]{1,0:T(8,128)(2,1)S(1)}, u32[]{:S(2)}, u32[]{:S(2)}) collective-permute-start(bf16[32,896]{1,0:T(8,128)(2,1)} %get-tuple-element.45), channel_id=1, source_target_pairs={{0,1},{1,0},{2,3},{3,2},{4,5},{5,4},{6,7},{7,6},{8,9},{9,8},{10,11... | collective-permute-start | bytes 172040 | tf_op jit(solution)/shard_map/ppermute | solution.py:21
  11.9 21.7 %collective-permute-start.1 = (bf16[32,896]{1,0:T(8,128)(2,1)}, bf16[32,896]{1,0:T(8,128)(2,1)}, u32[]{:S(2)}, u32[]{:S(2)}) collective-permute-start(bf16[32,896]{1,0:T(8,128)(2,1)} %get-tuple-element.46), channel_id=1, source_target_pairs={{0,2},{1,3},{2,0},{3,1},{4,6},{5,7},{6,4},{7,5},{8,10},{9,11},{10,... | collective-permute-start | bytes 172040 | tf_op jit(solution)/shard_map/ppermute | solution.py:21
  14.4 19.3 %collective-permute-start.2 = (bf16[32,896]{1,0:T(8,128)(2,1)}, bf16[32,896]{1,0:T(8,128)(2,1)}, u32[]{:S(2)}, u32[]{:S(2)}) collective-permute-start(bf16[32,896]{1,0:T(8,128)(2,1)} %get-tuple-element.47), channel_id=1, source_target_pairs={{0,3},{1,2},{2,1},{3,0},{4,7},{5,6},{6,5},{7,4},{8,11},{9,10},{10,... | collective-permute-start | bytes 172040 | tf_op jit(solution)/shard_map/ppermute | solution.py:21
  20.8 40.2 %collective-permute-start.9 = (bf16[128,1024]{1,0:T(8,128)(2,1)}, bf16[128,1024]{1,0:T(8,128)(2,1)S(1)}, u32[]{:S(2)}, u32[]{:S(2)}) collective-permute-start(bf16[128,1024]{1,0:T(8,128)(2,1)} %get-tuple-element.51), channel_id=1, source_target_pairs={{0,12},{4,8},{8,4},{12,0},{1,13},{5,9},{9,5},{13,1},{2,14},{6,10},... | collective-permute-start | bytes 786440 | tf_op jit(solution)/shard_map/ppermute | solution.py:21
  24.6 37.6 %collective-permute-start.11 = (bf16[128,1024]{1,0:T(8,128)(2,1)}, bf16[128,1024]{1,0:T(8,128)(2,1)}, u32[]{:S(2)}, u32[]{:S(2)}) collective-permute-start(bf16[128,1024]{1,0:T(8,128)(2,1)} %get-tuple-element.52), channel_id=1, source_target_pairs={{0,8},{4,12},{8,0},{12,4},{1,9},{5,13},{9,1},{13,5},{2,10},{6,14},... | collective-permute-start | bytes 786440 | tf_op jit(solution)/shard_map/ppermute | solution.py:21
  39.7 10.4 %collective-permute-start.4 = (bf16[32,512]{1,0:T(8,128)(2,1)S(1)}, bf16[32,512]{1,0:T(8,128)(2,1)S(1)}, u32[]{:S(2)}, u32[]{:S(2)}) collective-permute-start(bf16[32,512]{1,0:T(8,128)(2,1)S(1)} %get-tuple-element.49), channel_id=1, source_target_pairs={{0,8},{4,12},{8,0},{12,4},{1,9},{5,13},{9,1},{13,5},{2,10},{6,14},... | collective-permute-start | bytes 98312 | tf_op jit(solution)/shard_map/ppermute | solution.py:21
  54.7 13.2 %collective-permute-start.13 = (bf16[128,1024]{1,0:T(8,128)(2,1)}, bf16[128,1024]{1,0:T(8,128)(2,1)}, u32[]{:S(2)}, u32[]{:S(2)}) collective-permute-start(bf16[128,1024]{1,0:T(8,128)(2,1)} %copy-done.64), channel_id=1, source_target_pairs={{0,4},{4,0},{8,12},{12,8},{1,5},{5,1},{9,13},{13,9},{2,6},{6,2},{1... | collective-permute-start | bytes 786440 | tf_op jit(solution)/shard_map/ppermute | solution.py:21
  57.2 13.9 %collective-permute-start.15 = (bf16[128,1024]{1,0:T(8,128)(2,1)}, bf16[128,1024]{1,0:T(8,128)(2,1)}, u32[]{:S(2)}, u32[]{:S(2)}) collective-permute-start(bf16[128,1024]{1,0:T(8,128)(2,1)} %copy-done.63), channel_id=1, source_target_pairs={{0,12},{4,8},{8,4},{12,0},{1,13},{5,9},{9,5},{13,1},{2,14},{6,10},... | collective-permute-start | bytes 786440 | tf_op jit(solution)/shard_map/ppermute | solution.py:21
  60.3 21.9 %collective-permute-start.17 = (bf16[128,1024]{1,0:T(8,128)(2,1)}, bf16[128,1024]{1,0:T(8,128)(2,1)}, u32[]{:S(2)}, u32[]{:S(2)}) collective-permute-start(bf16[128,1024]{1,0:T(8,128)(2,1)} %copy-done.62), channel_id=1, source_target_pairs={{0,8},{4,12},{8,0},{12,4},{1,9},{5,13},{9,1},{13,5},{2,10},{6,14},... | collective-permute-start | bytes 786440 | tf_op jit(solution)/shard_map/ppermute | solution.py:21
  61.0 22.8 %collective-permute-start.19 = (bf16[128,1024]{1,0:T(8,128)(2,1)}, bf16[128,1024]{1,0:T(8,128)(2,1)}, u32[]{:S(2)}, u32[]{:S(2)}) collective-permute-start(bf16[128,1024]{1,0:T(8,128)(2,1)} %copy-done.61), channel_id=1, source_target_pairs={{0,4},{4,0},{8,12},{12,8},{1,5},{5,1},{9,13},{13,9},{2,6},{6,2},{1... | collective-permute-start | bytes 786440 | tf_op jit(solution)/shard_map/ppermute | solution.py:21
  62.2 22.0 %collective-permute-start.10 = (bf16[128,1024]{1,0:T(8,128)(2,1)S(1)}, bf16[128,1024]{1,0:T(8,128)(2,1)}, u32[]{:S(2)}, u32[]{:S(2)}) collective-permute-start(bf16[128,1024]{1,0:T(8,128)(2,1)S(1)} %collective-permute-done.9.refs_5_), channel_id=1, source_target_pairs={{0,16},{16,0},{1,17},{17,1},{2,18},{18,2},{3,19},{19,3},{4,20},{20... | collective-permute-start | bytes 786440 | tf_op jit(solution)/shard_map/ppermute | solution.py:21
  67.9 19.9 %collective-permute-start.12 = (bf16[128,1024]{1,0:T(8,128)(2,1)}, bf16[128,1024]{1,0:T(8,128)(2,1)}, u32[]{:S(2)}, u32[]{:S(2)}) collective-permute-start(bf16[128,1024]{1,0:T(8,128)(2,1)} %collective-permute-done.11.refs_7_), channel_id=1, source_target_pairs={{0,16},{16,0},{1,17},{17,1},{2,18},{18,2},{3,19},{19,3},{4,20},{20... | collective-permute-start | bytes 786440 | tf_op jit(solution)/shard_map/ppermute | solution.py:21
  71.1 16.7 %collective-permute-start.14 = (bf16[128,1024]{1,0:T(8,128)(2,1)}, bf16[128,1024]{1,0:T(8,128)(2,1)}, u32[]{:S(2)}, u32[]{:S(2)}) collective-permute-start(bf16[128,1024]{1,0:T(8,128)(2,1)} %collective-permute-done.13.refs_9_), channel_id=1, source_target_pairs={{0,16},{16,0},{1,17},{17,1},{2,18},{18,2},{3,19},{19,3},{4,20},{20... | collective-permute-start | bytes 786440 | tf_op jit(solution)/shard_map/ppermute | solution.py:21
  82.2 9.6 %collective-permute-start.16 = (bf16[128,1024]{1,0:T(8,128)(2,1)}, bf16[128,1024]{1,0:T(8,128)(2,1)}, u32[]{:S(2)}, u32[]{:S(2)}) collective-permute-start(bf16[128,1024]{1,0:T(8,128)(2,1)} %collective-permute-done.15.refs_11_), channel_id=1, source_target_pairs={{0,16},{16,0},{1,17},{17,1},{2,18},{18,2},{3,19},{19,3},{4,20},{20... | collective-permute-start | bytes 786440 | tf_op jit(solution)/shard_map/ppermute | solution.py:21
  83.7 13.7 %collective-permute-start.18 = (bf16[128,1024]{1,0:T(8,128)(2,1)}, bf16[128,1024]{1,0:T(8,128)(2,1)}, u32[]{:S(2)}, u32[]{:S(2)}) collective-permute-start(bf16[128,1024]{1,0:T(8,128)(2,1)} %collective-permute-done.17.refs_13_), channel_id=1, source_target_pairs={{0,16},{16,0},{1,17},{17,1},{2,18},{18,2},{3,19},{19,3},{4,20},{20... | collective-permute-start | bytes 786440 | tf_op jit(solution)/shard_map/ppermute | solution.py:21
  84.3 16.2 %collective-permute-start.20 = (bf16[128,1024]{1,0:T(8,128)(2,1)}, bf16[128,1024]{1,0:T(8,128)(2,1)S(1)}, u32[]{:S(2)}, u32[]{:S(2)}) collective-permute-start(bf16[128,1024]{1,0:T(8,128)(2,1)} %collective-permute-done.19.refs_15_), channel_id=1, source_target_pairs={{0,16},{16,0},{1,17},{17,1},{2,18},{18,2},{3,19},{19,3},{4,20},{20... | collective-permute-start | bytes 786440 | tf_op jit(solution)/shard_map/ppermute | solution.py:21
  116.3 10.8 %collective-permute-start.22 = (bf16[128,1024]{1,0:T(8,128)(2,1)S(1)}, bf16[128,1024]{1,0:T(8,128)(2,1)}, u32[]{:S(2)}, u32[]{:S(2)}) collective-permute-start(bf16[128,1024]{1,0:T(8,128)(2,1)S(1)} %get-tuple-element.57.refs_0_.refs_5_.fresh_ref), channel_id=1, source_target_pairs={{0,12},{4,8},{8,4},{12,0},{1,13},{5,9},{9,5},{13,1},{2,14},{6,10},... | collective-permute-start | bytes 786440 | tf_op jit(solution)/shard_map/ppermute | solution.py:21
  120.9 12.0 %collective-permute-start.21 = (bf16[128,1024]{1,0:T(8,128)(2,1)S(1)}, bf16[128,1024]{1,0:T(8,128)(2,1)}, u32[]{:S(2)}, u32[]{:S(2)}) collective-permute-start(bf16[128,1024]{1,0:T(8,128)(2,1)S(1)} %get-tuple-element.57.refs_0_.refs_5_.fresh_ref), channel_id=1, source_target_pairs={{0,4},{4,0},{8,12},{12,8},{1,5},{5,1},{9,13},{13,9},{2,6},{6,2},{1... | collective-permute-start | bytes 786440 | tf_op jit(solution)/shard_map/ppermute | solution.py:21
  170.4 11.2 %collective-permute-start.34 = (bf16[128,1024]{1,0:T(8,128)(2,1)S(1)}, bf16[128,1024]{1,0:T(8,128)(2,1)}, u32[]{:S(2)}, u32[]{:S(2)}) collective-permute-start(bf16[128,1024]{1,0:T(8,128)(2,1)S(1)} %output.5.refs_0_.refs_5_.fresh_ref), channel_id=1, source_target_pairs={{0,12},{4,8},{8,4},{12,0},{1,13},{5,9},{9,5},{13,1},{2,14},{6,10},... | collective-permute-start | bytes 786440 | tf_op jit(solution)/shard_map/ppermute | solution.py:21
  172.9 13.8 %collective-permute-start.33 = (bf16[128,1024]{1,0:T(8,128)(2,1)S(1)}, bf16[128,1024]{1,0:T(8,128)(2,1)}, u32[]{:S(2)}, u32[]{:S(2)}) collective-permute-start(bf16[128,1024]{1,0:T(8,128)(2,1)S(1)} %output.5.refs_0_.refs_5_.fresh_ref), channel_id=1, source_target_pairs={{0,4},{4,0},{8,12},{12,8},{1,5},{5,1},{9,13},{13,9},{2,6},{6,2},{1... | collective-permute-start | bytes 786440 | tf_op jit(solution)/shard_map/ppermute | solution.py:21
  181.6 10.5 %collective-permute-start.35 = (bf16[128,1024]{1,0:T(8,128)(2,1)}, bf16[128,1024]{1,0:T(8,128)(2,1)}, u32[]{:S(2)}, u32[]{:S(2)}) collective-permute-start(bf16[128,1024]{1,0:T(8,128)(2,1)} %collective-permute-done.34.refs_3_), channel_id=1, source_target_pairs={{0,4},{4,0},{8,12},{12,8},{1,5},{5,1},{9,13},{13,9},{2,6},{6,2},{1... | collective-permute-start | bytes 786440 | tf_op jit(solution)/shard_map/ppermute | solution.py:21
  227.2 11.4 %collective-permute-start.46 = (bf16[128,1024]{1,0:T(8,128)(2,1)}, bf16[128,1024]{1,0:T(8,128)(2,1)}, u32[]{:S(2)}, u32[]{:S(2)}) collective-permute-start(bf16[128,1024]{1,0:T(8,128)(2,1)} %output.6.refs_0_.refs_5_.fresh_ref), channel_id=1, source_target_pairs={{0,12},{4,8},{8,4},{12,0},{1,13},{5,9},{9,5},{13,1},{2,14},{6,10},... | collective-permute-start | bytes 786440 | tf_op jit(solution)/shard_map/ppermute | solution.py:21
  229.4 14.2 %collective-permute-start.45 = (bf16[128,1024]{1,0:T(8,128)(2,1)}, bf16[128,1024]{1,0:T(8,128)(2,1)}, u32[]{:S(2)}, u32[]{:S(2)}) collective-permute-start(bf16[128,1024]{1,0:T(8,128)(2,1)} %output.6.refs_0_.refs_5_.fresh_ref), channel_id=1, source_target_pairs={{0,4},{4,0},{8,12},{12,8},{1,5},{5,1},{9,13},{13,9},{2,6},{6,2},{1... | collective-permute-start | bytes 786440 | tf_op jit(solution)/shard_map/ppermute | solution.py:21
  238.6 10.5 %collective-permute-start.47 = (bf16[128,1024]{1,0:T(8,128)(2,1)}, bf16[128,1024]{1,0:T(8,128)(2,1)}, u32[]{:S(2)}, u32[]{:S(2)}) collective-permute-start(bf16[128,1024]{1,0:T(8,128)(2,1)} %collective-permute-done.46.refs_3_), channel_id=1, source_target_pairs={{0,4},{4,0},{8,12},{12,8},{1,5},{5,1},{9,13},{13,9},{2,6},{6,2},{1... | collective-permute-start | bytes 786440 | tf_op jit(solution)/shard_map/ppermute | solution.py:21
  (108 other events, 979.0 us)

commit v3 on v2

--- a/solution.py
+++ b/solution.py
@@ -21,11 +21,8 @@
     return lax.ppermute(x, axis, [(i, i ^ step) for i in range(size)])
 
 
-def parent_rows(index_ref, features):
-    rows, width = index_ref.shape[0], features.shape[0]
-    column = lax.broadcasted_iota(jnp.int32, (rows, width), 1)
-    chosen = jnp.where(column == index_ref[...], 1.0, 0.0).astype(jnp.bfloat16)
-    return jnp.dot(chosen, features, preferred_element_type=jnp.float32)
+def parent_rows(chosen_ref, features):
+    return jnp.dot(chosen_ref[...], features, preferred_element_type=jnp.float32)
 
 
 def embed_rows(places_ref, embed_ref, batch, level, columns):
@@ -38,14 +35,14 @@
     return jnp.concatenate(blocks, axis=0)
 
 
-def cut_kernel(half, info_ref, weight_ref, *refs):
+def cut_kernel(plan, dp, info_ref, weight_ref, *refs):
     outs, sems = refs[:-1], refs[-1]
     share = outs[0].shape[1]
     copies = []
     for place, out_ref in enumerate(outs):
-        step, start, depth = half[place]
-        row = start if step == 0 else pl.multiple_of(start + info_ref[0], 16)
-        column = pl.multiple_of((info_ref[1] ^ step) * share, LANES)
+        step, start, depth = plan[place]
+        row = start if step == 0 else pl.multiple_of(start + info_ref[dp], 16)
+        column = pl.multiple_of((info_ref[dp + 2] ^ step) * share, LANES)
         copies.append(
             pltpu.make_async_copy(
                 weight_ref.at[pl.ds(row, depth), pl.ds(column, share)],
@@ -59,10 +56,10 @@
         copy.wait()
 
 
-def cut(info, w_out, plan, share):
+def cut(info, w_out, plan, share, dp):
     shapes = [(depth, share) for _, _, depth in plan]
     return pl.pallas_call(
-        functools.partial(cut_kernel, plan),
+        functools.partial(cut_kernel, plan, dp),
         grid_spec=pltpu.PrefetchScalarGridSpec(
             num_scalar_prefetch=1,
             grid=(1,),
@@ -76,12 +73,15 @@
     )(info, w_out)
 
 
-def load_kernel(*refs):
-    count = len(refs) // 2
-    sources, held, sems = refs[:count], refs[count : 2 * count], refs[-1]
+def load_kernel(parts, info_ref, source_ref, held_ref, sems):
+    depth = source_ref.shape[0] // parts
     copies = [
-        pltpu.make_async_copy(source, target, sems.at[place])
-        for place, (source, target) in enumerate(zip(sources, held))
+        pltpu.make_async_copy(
+            source_ref.at[pl.ds(part * depth, depth)],
+            held_ref.at[pl.ds(part * depth, depth)],
+            sems.at[part],
+        )
+        for part in range(parts)
     ]
     for copy in copies:
         copy.start()
@@ -89,30 +89,100 @@
         copy.wait()
 
 
-def load(*arrays):
+def load(info, x):
+    parts = 4
     return pl.pallas_call(
-        load_kernel,
-        in_specs=[pl.BlockSpec(memory_space=pl.ANY) for _ in arrays],
-        out_specs=[pl.BlockSpec(memory_space=pltpu.VMEM) for _ in arrays],
-        out_shape=[pltpu.VMEM(x.shape, x.dtype) for x in arrays],
-        scratch_shapes=[pltpu.SemaphoreType.DMA((len(arrays),))],
+        functools.partial(load_kernel, parts),
+        in_specs=[pl.BlockSpec(memory_space=pltpu.SMEM), pl.BlockSpec(memory_space=pl.ANY)],
+        out_specs=pl.BlockSpec(memory_space=pltpu.VMEM),
+        out_shape=pltpu.VMEM(x.shape, x.dtype),
+        scratch_shapes=[pltpu.SemaphoreType.DMA((parts,))],
         compiler_params=pltpu.CompilerParams(vmem_limit_bytes=VMEM_BYTES),
         name="load",
-    )(*arrays)
-
-
-def project_kernel(level, batch, pieces, steps, dp, share_ref, places_ref, index_ref, *refs):
+    )(info, x)
+
+
+def prepare_kernel(batch, batches, dp, levels, branch, info_ref, parents_ref, *refs):
+    root_ref, chosen_refs = refs[0], refs[1 : levels]
+    mask_refs, table_ref = refs[levels : 2 * levels], refs[2 * levels]
+    rows, requests = root_ref.shape
+    local = requests // dp
+    per_block = local // batches
+    own = per_block * branch
+    for level in range(levels):
+        width = requests if level == 0 else rows
+        line = lax.broadcasted_iota(jnp.int32, (branch, width), 0)
+        column = lax.broadcasted_iota(jnp.int32, (branch, width), 1)
+        for step in range(dp):
+            for slot in range(per_block):
+                request = info_ref[step] * local + batch * per_block + slot
+                first = (step * per_block + slot) * branch
+                if level == 0:
+                    place = request
+                else:
+                    place = jnp.zeros((branch, width), jnp.int32)
+                    for node in range(branch):
+                        up = parents_ref[request, level - 1, node] + first
+                        place = jnp.where(line == node, up, place)
+                table_ref[first : first + branch, :width] = jnp.where(
+                    column == place, 1.0, 0.0
+                )
+        chosen = table_ref[:, :width].astype(jnp.bfloat16)
+        if level == 0:
+            root_ref[...] = chosen
+        else:
+            chosen_refs[level - 1][...] = chosen
+    ups = [ref[:own, :own] for ref in chosen_refs]
+    line = lax.broadcasted_iota(jnp.int32, (own, own), 0)
+    column = lax.broadcasted_iota(jnp.int32, (own, own), 1)
+    for level in range(levels):
+        current = jnp.where(line == column, 1.0, 0.0)
+        blocks = [current]
+        for upper in range(level, 0, -1):
+            current = jnp.dot(
+                current.astype(jnp.bfloat16), ups[upper - 1], preferred_element_type=jnp.float32
+            )
+            blocks.insert(0, current)
+        for place in range(levels):
+            span = slice(place * own, (place + 1) * own)
+            if place < len(blocks):
+                mask_refs[level][:, span] = blocks[place]
+            else:
+                mask_refs[level][:, span] = jnp.zeros((own, own), jnp.float32)
+
+
+def prepare(batch, batches, info, parents, dp, levels, branch):
+    requests = parents.shape[0]
+    own = requests // dp // batches * branch
+    rows = dp * own
+    half, single = jnp.bfloat16, jnp.float32
+    out_shape = [jax.ShapeDtypeStruct((rows, requests), half)]
+    out_shape += [jax.ShapeDtypeStruct((rows, rows), half)] * (levels - 1)
+    out_shape += [jax.ShapeDtypeStruct((own, levels * own), single)] * levels
+    outs = pl.pallas_call(
+        functools.partial(prepare_kernel, batch, batches, dp, levels, branch),
+        in_specs=[pl.BlockSpec(memory_space=pltpu.SMEM)] * 2,
+        out_specs=[pl.BlockSpec(memory_space=pltpu.VMEM)] * len(out_shape),
+        out_shape=out_shape,
+        scratch_shapes=[pltpu.VMEM((rows, max(rows, requests)), jnp.float32)],
+        compiler_params=pltpu.CompilerParams(vmem_limit_bytes=VMEM_BYTES),
+        name="prepare",
+    )(info, parents)
+    return outs[:levels], outs[levels:]
+
+
+def project_kernel(level, batch, pieces, steps, dp, info_ref, index_ref, *refs):
     features = refs[:pieces]
     embed_ref, gain_ref, query_ref, keyval_ref = refs[pieces : pieces + 4]
     out_refs = refs[pieces + 4 : pieces + 4 + dp]
     cols = query_ref.shape[0] // steps
     query = keyval = squares = None
     for step in range(steps):
-        offset = pl.multiple_of(share_ref[step] * cols, LANES)
+        offset = pl.multiple_of(info_ref[dp + 3 + step] * cols, LANES)
         columns = pl.ds(offset, cols)
         held = features[step][...] if pieces == steps else features[0][:, columns]
         state = parent_rows(index_ref, held) + embed_rows(
-            places_ref, embed_ref, batch, level, columns
+            info_ref, embed_ref, batch, level, columns
         )
         square = jnp.sum(state * state, axis=1, keepdims=True)
         gain = gain_ref[:, columns].astype(jnp.float32)
@@ -149,67 +219,68 @@
     width = head_cols + fresh_ref.shape[1]
     squares = jnp.sum(total[:, width:], axis=1, keepdims=True)
     inv_rms = lax.rsqrt(squares / model_width + EPSILON)
-    projected = (total[:, :width] * inv_rms).astype(jnp.bfloat16).astype(jnp.float32)
+    projected = (total[:, :width] * inv_rms).astype(jnp.bfloat16)
     fresh = projected[:, head_cols:]
     fresh_ref[...] = fresh
     _, _, cache, kv_cols = cache_ref.shape
-    per_block = total.shape[0] // branch
+    rows = total.shape[0]
+    per_block = rows // branch
     kv_heads = kv_cols // HD
     group = head_cols // HD // kv_heads
-    positions = mask_ref.shape[1]
     tree = [ref[...] for ref in earlier_refs] + [fresh]
-    blank = jnp.zeros((positions - branch * len(tree), HD), jnp.float32)
-    column = lax.broadcasted_iota(jnp.int32, (group * branch, cache), 1)
+    filler = mask_ref.shape[1] - rows * len(tree)
+    tree += [jnp.zeros((filler, fresh.shape[1]), jnp.bfloat16)] if filler else []
+    tree = jnp.concatenate(tree, axis=0)
+    allowed = jnp.concatenate([mask_ref[...]] * group, axis=0) > 0.5
+    column = lax.broadcasted_iota(jnp.int32, (branch, cache), 1)
+    valid = [column < length_ref[base + request] for request in range(per_block)]
     across = (((1,), (1,)), ((), ()))
-    outs = []
-    for request in range(per_block):
-        span = slice(request * branch, (request + 1) * branch)
-        valid = column < length_ref[base + request]
-        allowed = jnp.concatenate([mask_ref[span, :]] * group, axis=0) > 0.5
-        heads = []
-        for kv in range(kv_heads):
-            first = kv * group
-            queries = jnp.concatenate(
-                [
-                    projected[span, (first + g) * HD : (first + g + 1) * HD]
-                    for g in range(group)
-                ],
-                axis=0,
-            ).astype(jnp.bfloat16)
-            key_cols = slice(kv * HD, (kv + 1) * HD)
-            value_cols = slice(kv_cols + kv * HD, kv_cols + (kv + 1) * HD)
-            filler = [blank] if blank.shape[0] else []
-            tree_keys = jnp.concatenate(
-                [level[span, key_cols] for level in tree] + filler, axis=0
-            ).astype(jnp.bfloat16)
-            tree_values = jnp.concatenate(
-                [level[span, value_cols] for level in tree] + filler, axis=0
-            ).astype(jnp.bfloat16)
+    scale = HD**-0.5
+    for kv in range(kv_heads):
+        first = kv * group
+        queries = jnp.concatenate(
+            [projected[:, (first + g) * HD : (first + g + 1) * HD] for g in range(group)], axis=0
+        )
+        key_cols = slice(kv * HD, (kv + 1) * HD)
+        value_cols = slice(kv_cols + kv * HD, kv_cols + (kv + 1) * HD)
+        far = lax.dot_general(
+            queries, tree[:, key_cols], across, preferred_element_type=jnp.float32
+        )
+        far = jnp.where(allowed, far * scale, MASKED)
+        found = []
+        for request in range(per_block):
             keys = cache_ref[base + request, 0, :, key_cols]
+            scores = lax.dot_general(queries, keys, across, preferred_element_type=jnp.float32)
+            found.append(scores)
+        blocks = []
+        for g in range(group):
+            for request in range(per_block):
+                start = g * rows + request * branch
+                block = found[request][start : start + branch] * scale
+                blocks.append(jnp.where(valid[request], block, MASKED))
+        near = jnp.concatenate(blocks, axis=0)
+        top = jnp.maximum(
+            jnp.max(near, axis=1, keepdims=True), jnp.max(far, axis=1, keepdims=True)
+        )
+        near = jnp.exp(near - top)
+        far = jnp.exp(far - top)
+        below = jnp.sum(near, axis=1, keepdims=True) + jnp.sum(far, axis=1, keepdims=True)
+        near = (near / below).astype(jnp.bfloat16)
+        far = (far / below).astype(jnp.bfloat16)
+        mixed = jnp.dot(far, tree[:, value_cols], preferred_element_type=jnp.float32)
+        found = []
+        for request in range(per_block):
             values = cache_ref[base + request, 1, :, key_cols]
-            scale = HD**-0.5
-            near = lax.dot_general(
-                queries, keys, across, preferred_element_type=jnp.float32
-            )
-            far = lax.dot_general(
-                queries, tree_keys, across, preferred_element_type=jnp.float32
-            )
-            near = jnp.where(valid, near * scale, MASKED)
-            far = jnp.where(allowed, far * scale, MASKED)
-            top = jnp.maximum(
-                jnp.max(near, axis=1, keepdims=True), jnp.max(far, axis=1, keepdims=True)
-            )
-            near = jnp.exp(near - top)
-            far = jnp.exp(far - top)
-            below = jnp.sum(near, axis=1, keepdims=True) + jnp.sum(far, axis=1, keepdims=True)
-            mixed = jnp.dot(
-                (near / below).astype(jnp.bfloat16), values, preferred_element_type=jnp.float32
-            ) + jnp.dot(
-                (far / below).astype(jnp.bfloat16), tree_values, preferred_element_type=jnp.float32
-            )
-            heads += [mixed[g * branch : (g + 1) * branch] for g in range(group)]
-        outs.append(jnp.concatenate(heads, axis=1))
-    out_ref[...] = jnp.concatenate(outs, axis=0).astype(jnp.bfloat16)
+            found.append(jnp.dot(near, values, preferred_element_type=jnp.float32))
+        for g in range(group):
+            blocks = []
+            for request in range(per_block):
+                start = g * rows + request * branch
+                blocks.append(
+                    found[request][start : start + branch] + mixed[start : start + branch]
+                )
+            block = jnp.concatenate(blocks, axis=0).astype(jnp.bfloat16)
+            out_ref[:, (first + g) * HD : (first + g + 1) * HD] = block
 
 
 def output_kernel(level, batch, dp, weights, keep, info_ref, index_ref, *refs):
@@ -266,9 +337,8 @@
     return pl.BlockSpec(x.shape, lambda i, *_: (0,) * x.ndim)
 
 
-def project(level, batch, share_ids, places, index, pieces, embeds, gain, w_query, keyval):
+def project(level, batch, steps, info, index, pieces, embeds, gain, w_query, keyval):
     dp, _, per_block, _, branch, feat_cols = embeds.shape
-    steps = share_ids.shape[0]
     head_cols, kv_cols = w_query.shape[1], keyval.shape[1]
     rows = per_block * branch
     width = head_cols + kv_cols + LANES
@@ -276,7 +346,7 @@
     return pl.pallas_call(
         functools.partial(project_kernel, level, batch, len(pieces), steps, dp),
         grid_spec=pltpu.PrefetchScalarGridSpec(
-            num_scalar_prefetch=2,
+            num_scalar_prefetch=1,
             grid=(),
             in_specs=[pl.BlockSpec(memory_space=pltpu.VMEM)] * len(operands),
             out_specs=[pl.BlockSpec(memory_space=pltpu.VMEM)] * dp,
@@ -289,7 +359,7 @@
             transcendentals=0,
         ),
         name="project",
-    )(share_ids, places, *operands)
+    )(info, *operands)
 
 
 def attend(batch, per_block, model_width, head_cols, lengths, parts, mask, cache, earlier):
@@ -314,7 +384,7 @@
         ),
         out_shape=[
             jax.ShapeDtypeStruct((rows, head_cols), jnp.bfloat16),
-            jax.ShapeDtypeStruct((rows, fresh_cols), jnp.float32),
+            jax.ShapeDtypeStruct((rows, fresh_cols), jnp.bfloat16),
         ],
         compiler_params=pltpu.CompilerParams(vmem_limit_bytes=VMEM_BYTES),
         cost_estimate=pl.CostEstimate(
@@ -385,26 +455,6 @@
         ),
         name="store",
     )(*operands)
-
-
-def tree_masks(own_parents, depths, branch):
-    columns = jnp.arange(branch, dtype=jnp.int32)
-    masks = []
-    for level in range(depths):
-        current = jnp.broadcast_to(columns, own_parents.shape[:2] + (branch,))
-        blocks = [columns == current[..., None]]
-        for upper in range(level, 0, -1):
-            above = own_parents[:, :, upper - 1]
-            current = jnp.sum(
-                jnp.where(current[..., None] == columns, above[:, :, None, :], 0), axis=3
-            )
-            blocks.append(columns == current[..., None])
-        blocks = blocks[::-1]
-        blank = jnp.zeros(blocks[0].shape, bool)
-        blocks += [blank] * (depths - len(blocks))
-        joined = jnp.concatenate(blocks, axis=3).astype(jnp.float32)
-        masks.append(joined.reshape(own_parents.shape[0], -1, depths * branch))
-    return masks
 
 
 def shards(
@@ -431,66 +481,39 @@
     head_rows = w_out.shape[0]
     by_swaps = tensor == 4 and groups == 2
 
+    half = head_rows // 2 if by_swaps else 0
+    steps = tensor if by_swaps else 1
+    info = [dp_index ^ step for step in range(dp)]
+    info += [group_index * half, (1 - group_index) * half, tensor_index]
+    info += [tensor_index ^ step for step in range(tensor)] if by_swaps else [0 * dp_index]
+    info = jnp.stack(info)
+
     if by_swaps:
-        half = head_rows // 2
         depth = half // CHUNKS
         plan = [(0, 0, head_rows)]
         for chunk in range(CHUNKS):
             plan += [(step, chunk * depth, depth) for step in (3, 2, 1)]
-        cuts = cut(
-            jnp.stack([group_index * half, tensor_index]), w_out, tuple(plan), share_cols
-        )
+        cuts = cut(info, w_out, tuple(plan), share_cols, dp)
         weights = [(cuts[0], 0, None)]
         for (step, start, _), sent in zip(plan[1:], cuts[1:]):
             arrived = swap(sent, "tensor", step)
             weights.append((arrived, step * head_rows + start, 0))
             weights.append((swap(arrived, "groups", 1), step * head_rows + start, 1))
     else:
-        half = 0
         spread = lax.all_to_all(w_out, "tensor", 1, 0, tiled=True)
-        weights = [(load(spread)[0], 0, None)]
-
+        weights = [(load(info, spread), 0, None)]
+
+    chosen, masks = [], []
+    for batch in range(batches):
+        made = prepare(batch, batches, info, parents, dp, depths, branch)
+        chosen.append(made[0])
+        masks.append(made[1])
     embeds = branch_embeds.reshape(dp, batches, per_block, depths, branch, feat_cols)
     gain = norm_gain.reshape(1, feat_cols)
     keyval = w_keyval.reshape(feat_cols, -1)
-    w_query, keyval, embeds, cache_kv = load(w_query, keyval, embeds, cache_kv)
-    places = jnp.stack([dp_index ^ step for step in range(dp)])
-    info = jnp.concatenate(
-        [
-            places,
-            jnp.stack([group_index * half, (1 - group_index) * half, tensor_index]),
-        ]
+    w_query, keyval, embeds, cache_kv = (
+        load(info, x) for x in (w_query, keyval, embeds, cache_kv)
     )
-    if by_swaps:
-        share_ids = jnp.stack([tensor_index ^ step for step in range(tensor)])
-    else:
-        share_ids = jnp.zeros((1,), jnp.int32)
-
-    split = parents.reshape(dp, batches, per_block, depths - 1, branch)
-    ordered = jnp.stack(
-        [lax.dynamic_index_in_dim(split, dp_index ^ step, 0, False) for step in range(dp)]
-    )
-    slot = (
-        jnp.arange(dp, dtype=jnp.int32)[:, None] * per_block
-        + jnp.arange(per_block, dtype=jnp.int32)[None, :]
-    )
-    rows = dp * per_block * branch
-    indices = []
-    for level in range(depths):
-        row = []
-        for batch in range(batches):
-            if level == 0:
-                request = (
-                    places[:, None] * local
-                    + batch * per_block
-                    + jnp.arange(per_block, dtype=jnp.int32)[None, :]
-                )
-                place = jnp.broadcast_to(request[:, :, None], (dp, per_block, branch))
-            else:
-                place = slot[:, :, None] * branch + ordered[:, batch, :, level - 1]
-            row.append(place.reshape(rows, 1))
-        indices.append(row)
-    masks = tree_masks(ordered[0], depths, branch)
 
     earlier = [[] for _ in range(batches)]
     shares = [root_features] * batches
@@ -502,9 +525,9 @@
             sums = project(
                 level,
                 batch,
-                share_ids,
-                places,
-                indices[level][batch],
+                steps,
+                info,
+                chosen[batch][level],
                 gathered[batch],
                 embeds,
                 gain,
@@ -519,7 +542,7 @@
                 head_cols,
                 cache_lengths,
                 parts,
-                masks[level][batch],
+                masks[batch][level],
                 cache_kv,
                 earlier[batch],
             )
@@ -535,7 +558,7 @@
                 level,
                 batch,
                 info,
-                indices[level][batch],
+                chosen[batch][level],
                 attended[batch],
                 weights,
                 shares[batch],

time: 288 us -> 238 us (0.83)
  local copies, waits for them, and re-layouts: 60.7 us -> 4.87 us
  waiting for transfers between devices: 108 us -> 135 us
  Pallas kernels: 41.4 us -> 30.4 us
  other arithmetic: 8.86 us -> 0 us
    unnamed x164 -> x26, local copies, waits for them, and re-layouts: 50 us -> 4.05 us
    ppermute x57, waiting for transfers between devices: 108 us -> 135 us  [swap(): return lax.ppermute(x, axis, [(i, i ^ step) for i in range(size)])]
    pallas_call x4, Pallas kernels: 14.1 us -> 8.23 us  [project(): pl.pallas_call(functools.partial(project_kernel, level, batch, len(pieces...]
    eq x6 -> x0, local copies, waits for them, and re-layouts: 4.7 us -> none  [the longest x3 2.7 us: tree_masks(): blocks.append(columns == current[..., None])]
    pallas_call x4, Pallas kernels: 9.8 us -> 5.6 us  [attend(): pl.pallas_call(functools.partial(attend_kernel, len(parts), len(earlier),...]
    pallas_call x4, Pallas kernels: 9.1 us -> 5.52 us  [output(): pl.pallas_call(functools.partial(output_kernel, level, batch, dp, places,...]
    pallas_call x2 -> x6, Pallas kernels: 2.44 us -> 5.99 us  [the longest x4 3.33 us: load(): pl.pallas_call(functools.partial(load_kernel, parts), in_specs=[pl.BlockS...]
    eq x5 -> x0, other arithmetic: 3.36 us -> none  [the longest x4 2.77 us: tree_masks(): blocks.append(columns == current[..., None])]
  transfers between devices with their start and end apart: 57 -> 57, of which waited for: 33 -> 35; matrix products, arithmetic and copies ran while one was open for 7% -> 0% of each run, Pallas kernels for 3% -> 3%
where the time goes in v3:
time: 238 us
  waiting for transfers between devices  135 us (57%)
  starting transfers between devices  66.7 us (28%)
  Pallas kernels  30.4 us (13%)
  local copies, waits for them, and re-layouts  4.87 us (2%)
    ppermute x57, waiting for transfers between devices, swap(): return lax.ppermute(x, axis, [(i, i ^ step) for i in range(size)])  135 us
    ppermute x57, starting transfers between devices, swap(): return lax.ppermute(x, axis, [(i, i ^ step) for i in range(size)])  66.7 us
    pallas_call x4, Pallas kernels, project(): pl.pallas_call(functools.partial(project_kernel, level, batch, len(pieces...  8.23 us
    pallas_call x4, Pallas kernels, attend(): pl.pallas_call(functools.partial(attend_kernel, len(parts), len(earlier),...  5.6 us
    pallas_call x4, Pallas kernels, output(): pl.pallas_call(functools.partial(output_kernel, level, batch, dp, places,...  5.52 us
    pallas_call x4, Pallas kernels, store(): pl.pallas_call(store_kernel, grid_spec=pltpu.PrefetchScalarGridSpec(num_s...  5.05 us
  transfers between devices with their start and end apart: 57, of which 35 were waited for; matrix products, arithmetic and copies ran while one was open for 0% of the time, Pallas kernels for 3%

profile of v3, /device:TPU:0, one launch (start us, length us, event | category | flops | bytes accessed | tf_op | source)
XLA Modules:
  0.0 237.5 jit_solution(7918356779844648210)
XLA Ops:
  15.3 3.9 %collective-permute-start.9 = (bf16[128,1024]{1,0:T(8,128)(2,1)S(1)}, bf16[128,1024]{1,0:T(8,128)(2,1)S(1)}, u32[]{:S(2)}, u32[]{:S(2)}) collective-permute-start(bf16[128,1024]{1,0:T(8,128)(2,1)S(1)} %get-tuple-element.56), channel_id=1, source_target_pairs={{0,12},{4,8},{8,4},{12,0},{1,13},{5,9},{9,5},{13,1},{2,14},{6,10},... | collective-permute-start | bytes 786440 | tf_op jit(solution)/shard_map/ppermute | solution.py:21
  25.9 7.1 %collective-permute-done.3 = bf16[32,512]{1,0:T(8,128)(2,1)S(1)} collective-permute-done((bf16[32,512]{1,0:T(8,128)(2,1)S(1)}, bf16[32,512]{1,0:T(8,128)(2,1)S(1)}, u32[]{:S(2)}, u32[]{:S(2)}) %collective-permute-start.3) | collective-permute-done | bytes 32800 | tf_op jit(solution)/shard_map/ppermute | solution.py:21
  33.0 11.8 %collective-permute-done.4 = bf16[32,512]{1,0:T(8,128)(2,1)S(1)} collective-permute-done((bf16[32,512]{1,0:T(8,128)(2,1)S(1)}, bf16[32,512]{1,0:T(8,128)(2,1)S(1)}, u32[]{:S(2)}, u32[]{:S(2)}) %collective-permute-start.4) | collective-permute-done | bytes 32800 | tf_op jit(solution)/shard_map/ppermute | solution.py:21
  46.7 3.9 %collective-permute-done.8.refs_3_ = bf16[32,2048]{1,0:T(8,128)(2,1)S(1)} collective-permute-done((bf16[32,2048]{1,0:T(8,128)(2,1)S(1)}, bf16[32,2048]{1,0:T(8,128)(2,1)S(1)}, u32[]{:S(2)}, u32[]{:S(2)}) %collective-permute-start.8) | collective-permute-done | bytes 131104 | tf_op jit(solution)/shard_map/ppermute | solution.py:21
  61.3 4.7 %collective-permute-done.15.refs_11_ = bf16[128,1024]{1,0:T(8,128)(2,1)S(1)} collective-permute-done((bf16[128,1024]{1,0:T(8,128)(2,1)S(1)}, bf16[128,1024]{1,0:T(8,128)(2,1)S(1)}, u32[]{:S(2)}, u32[]{:S(2)}) %collective-permute-start.15) | collective-permute-done | bytes 262176 | tf_op jit(solution)/shard_map/ppermute | solution.py:21
  67.6 10.6 %collective-permute-done.17.refs_13_ = bf16[128,1024]{1,0:T(8,128)(2,1)S(1)} collective-permute-done((bf16[128,1024]{1,0:T(8,128)(2,1)S(1)}, bf16[128,1024]{1,0:T(8,128)(2,1)S(1)}, u32[]{:S(2)}, u32[]{:S(2)}) %collective-permute-start.17) | collective-permute-done | bytes 262176 | tf_op jit(solution)/shard_map/ppermute | solution.py:21
  81.7 5.7 %collective-permute-done.16.refs_12_ = bf16[128,1024]{1,0:T(8,128)(2,1)S(1)} collective-permute-done((bf16[128,1024]{1,0:T(8,128)(2,1)S(1)}, bf16[128,1024]{1,0:T(8,128)(2,1)S(1)}, u32[]{:S(2)}, u32[]{:S(2)}) %collective-permute-start.16) | collective-permute-done | bytes 262176 | tf_op jit(solution)/shard_map/ppermute | solution.py:21
  87.4 5.6 %collective-permute-done.18.refs_14_ = bf16[128,1024]{1,0:T(8,128)(2,1)S(1)} collective-permute-done((bf16[128,1024]{1,0:T(8,128)(2,1)S(1)}, bf16[128,1024]{1,0:T(8,128)(2,1)S(1)}, u32[]{:S(2)}, u32[]{:S(2)}) %collective-permute-start.18) | collective-permute-done | bytes 262176 | tf_op jit(solution)/shard_map/ppermute | solution.py:21
  93.1 3.8 %collective-permute-done.20.refs_16_ = bf16[128,1024]{1,0:T(8,128)(2,1)S(1)} collective-permute-done((bf16[128,1024]{1,0:T(8,128)(2,1)S(1)}, bf16[128,1024]{1,0:T(8,128)(2,1)S(1)}, u32[]{:S(2)}, u32[]{:S(2)}) %collective-permute-start.20) | collective-permute-done | bytes 262176 | tf_op jit(solution)/shard_map/ppermute | solution.py:21
  101.0 8.6 %collective-permute-done.22.refs_3_ = bf16[128,1024]{1,0:T(8,128)(2,1)S(1)} collective-permute-done((bf16[128,1024]{1,0:T(8,128)(2,1)S(1)}, bf16[128,1024]{1,0:T(8,128)(2,1)S(1)}, u32[]{:S(2)}, u32[]{:S(2)}) %collective-permute-start.22) | collective-permute-done | bytes 262176 | tf_op jit(solution)/shard_map/ppermute | solution.py:21
  112.7 5.5 %collective-permute-done.23.refs_2_ = bf16[128,1024]{1,0:T(8,128)(2,1)S(1)} collective-permute-done((bf16[128,1024]{1,0:T(8,128)(2,1)S(1)}, bf16[128,1024]{1,0:T(8,128)(2,1)S(1)}, u32[]{:S(2)}, u32[]{:S(2)}) %collective-permute-start.23) | collective-permute-done | bytes 262176 | tf_op jit(solution)/shard_map/ppermute | solution.py:21
  122.2 2.9 %collective-permute-done.25.refs_2_ = bf16[32,896]{1,0:T(8,128)(2,1)S(1)} collective-permute-done((bf16[32,896]{1,0:T(8,128)(2,1)S(1)}, bf16[32,896]{1,0:T(8,128)(2,1)S(1)}, u32[]{:S(2)}, u32[]{:S(2)}) %collective-permute-start.25) | collective-permute-done | bytes 57376 | tf_op jit(solution)/shard_map/ppermute | solution.py:21
  131.3 2.8 %collective-permute-done.27 = bf16[32,512]{1,0:T(8,128)(2,1)S(1)} collective-permute-done((bf16[32,512]{1,0:T(8,128)(2,1)S(1)}, bf16[32,512]{1,0:T(8,128)(2,1)S(1)}, u32[]{:S(2)}, u32[]{:S(2)}) %collective-permute-start.27) | collective-permute-done | bytes 32800 | tf_op jit(solution)/shard_map/ppermute | solution.py:21
  136.0 3.9 %collective-permute-done.32.refs_3_ = bf16[32,2048]{1,0:T(8,128)(2,1)S(1)} collective-permute-done((bf16[32,2048]{1,0:T(8,128)(2,1)S(1)}, bf16[32,2048]{1,0:T(8,128)(2,1)S(1)}, u32[]{:S(2)}, u32[]{:S(2)}) %collective-permute-start.32) | collective-permute-done | bytes 131104 | tf_op jit(solution)/shard_map/ppermute | solution.py:21
  144.9 9.9 %collective-permute-done.34.refs_3_ = bf16[128,1024]{1,0:T(8,128)(2,1)S(1)} collective-permute-done((bf16[128,1024]{1,0:T(8,128)(2,1)S(1)}, bf16[128,1024]{1,0:T(8,128)(2,1)S(1)}, u32[]{:S(2)}, u32[]{:S(2)}) %collective-permute-start.34) | collective-permute-done | bytes 262176 | tf_op jit(solution)/shard_map/ppermute | solution.py:21
  154.9 3.5 %collective-permute-start.35 = (bf16[128,1024]{1,0:T(8,128)(2,1)S(1)}, bf16[128,1024]{1,0:T(8,128)(2,1)S(1)}, u32[]{:S(2)}, u32[]{:S(2)}) collective-permute-start(bf16[128,1024]{1,0:T(8,128)(2,1)S(1)} %collective-permute-done.34.refs_3_), channel_id=1, source_target_pairs={{0,4},{4,0},{8,12},{12,8},{1,5},{5,1},{9,13},{13,9},{2,6},{6,2},{1... | collective-permute-start | bytes 786440 | tf_op jit(solution)/shard_map/ppermute | solution.py:21
  158.6 5.8 %collective-permute-done.35.refs_2_ = bf16[128,1024]{1,0:T(8,128)(2,1)S(1)} collective-permute-done((bf16[128,1024]{1,0:T(8,128)(2,1)S(1)}, bf16[128,1024]{1,0:T(8,128)(2,1)S(1)}, u32[]{:S(2)}, u32[]{:S(2)}) %collective-permute-start.35) | collective-permute-done | bytes 262176 | tf_op jit(solution)/shard_map/ppermute | solution.py:21
  168.4 2.8 %collective-permute-done.37.refs_2_ = bf16[32,896]{1,0:T(8,128)(2,1)S(1)} collective-permute-done((bf16[32,896]{1,0:T(8,128)(2,1)S(1)}, bf16[32,896]{1,0:T(8,128)(2,1)S(1)}, u32[]{:S(2)}, u32[]{:S(2)}) %collective-permute-start.37) | collective-permute-done | bytes 57376 | tf_op jit(solution)/shard_map/ppermute | solution.py:21
  177.7 3.0 %collective-permute-done.39 = bf16[32,512]{1,0:T(8,128)(2,1)S(1)} collective-permute-done((bf16[32,512]{1,0:T(8,128)(2,1)S(1)}, bf16[32,512]{1,0:T(8,128)(2,1)S(1)}, u32[]{:S(2)}, u32[]{:S(2)}) %collective-permute-start.39) | collective-permute-done | bytes 32800 | tf_op jit(solution)/shard_map/ppermute | solution.py:21
  182.6 3.8 %collective-permute-done.44.refs_3_ = bf16[32,2048]{1,0:T(8,128)(2,1)S(1)} collective-permute-done((bf16[32,2048]{1,0:T(8,128)(2,1)S(1)}, bf16[32,2048]{1,0:T(8,128)(2,1)S(1)}, u32[]{:S(2)}, u32[]{:S(2)}) %collective-permute-start.44) | collective-permute-done | bytes 131104 | tf_op jit(solution)/shard_map/ppermute | solution.py:21
  192.0 9.0 %collective-permute-done.46.refs_3_ = bf16[128,1024]{1,0:T(8,128)(2,1)S(1)} collective-permute-done((bf16[128,1024]{1,0:T(8,128)(2,1)S(1)}, bf16[128,1024]{1,0:T(8,128)(2,1)S(1)}, u32[]{:S(2)}, u32[]{:S(2)}) %collective-permute-start.46) | collective-permute-done | bytes 262176 | tf_op jit(solution)/shard_map/ppermute | solution.py:21
  201.0 3.9 %collective-permute-start.47 = (bf16[128,1024]{1,0:T(8,128)(2,1)S(1)}, bf16[128,1024]{1,0:T(8,128)(2,1)S(1)}, u32[]{:S(2)}, u32[]{:S(2)}) collective-permute-start(bf16[128,1024]{1,0:T(8,128)(2,1)S(1)} %collective-permute-done.46.refs_3_), channel_id=1, source_target_pairs={{0,4},{4,0},{8,12},{12,8},{1,5},{5,1},{9,13},{13,9},{2,6},{6,2},{1... | collective-permute-start | bytes 786440 | tf_op jit(solution)/shard_map/ppermute | solution.py:21
  205.5 5.4 %collective-permute-done.47.refs_2_ = bf16[128,1024]{1,0:T(8,128)(2,1)S(1)} collective-permute-done((bf16[128,1024]{1,0:T(8,128)(2,1)S(1)}, bf16[128,1024]{1,0:T(8,128)(2,1)S(1)}, u32[]{:S(2)}, u32[]{:S(2)}) %collective-permute-start.47) | collective-permute-done | bytes 262176 | tf_op jit(solution)/shard_map/ppermute | solution.py:21
  214.9 2.8 %collective-permute-done.49.refs_2_ = bf16[32,896]{1,0:T(8,128)(2,1)S(1)} collective-permute-done((bf16[32,896]{1,0:T(8,128)(2,1)S(1)}, bf16[32,896]{1,0:T(8,128)(2,1)S(1)}, u32[]{:S(2)}, u32[]{:S(2)}) %collective-permute-start.49) | collective-permute-done | bytes 57376 | tf_op jit(solution)/shard_map/ppermute | solution.py:21
  (144 shorter events, 106.5 us)
Async XLA Ops:
  11.2 8.8 %collective-permute-start = (bf16[32,896]{1,0:T(8,128)(2,1)S(1)}, bf16[32,896]{1,0:T(8,128)(2,1)S(1)}, u32[]{:S(2)}, u32[]{:S(2)}) collective-permute-start(bf16[32,896]{1,0:T(8,128)(2,1)S(1)} %get-tuple-element.50), channel_id=1, source_target_pairs={{0,1},{1,0},{2,3},{3,2},{4,5},{5,4},{6,7},{7,6},{8,9},{9,8},{10,11... | collective-permute-start | bytes 172040 | tf_op jit(solution)/shard_map/ppermute | solution.py:21
  15.3 40.7 %collective-permute-start.9 = (bf16[128,1024]{1,0:T(8,128)(2,1)S(1)}, bf16[128,1024]{1,0:T(8,128)(2,1)S(1)}, u32[]{:S(2)}, u32[]{:S(2)}) collective-permute-start(bf16[128,1024]{1,0:T(8,128)(2,1)S(1)} %get-tuple-element.56), channel_id=1, source_target_pairs={{0,12},{4,8},{8,4},{12,0},{1,13},{5,9},{9,5},{13,1},{2,14},{6,10},... | collective-permute-start | bytes 786440 | tf_op jit(solution)/shard_map/ppermute | solution.py:21
  19.2 38.7 %collective-permute-start.11 = (bf16[128,1024]{1,0:T(8,128)(2,1)S(1)}, bf16[128,1024]{1,0:T(8,128)(2,1)S(1)}, u32[]{:S(2)}, u32[]{:S(2)}) collective-permute-start(bf16[128,1024]{1,0:T(8,128)(2,1)S(1)} %get-tuple-element.57), channel_id=1, source_target_pairs={{0,8},{4,12},{8,0},{12,4},{1,9},{5,13},{9,1},{13,5},{2,10},{6,14},... | collective-permute-start | bytes 786440 | tf_op jit(solution)/shard_map/ppermute | solution.py:21
  21.5 23.3 %collective-permute-start.5 = (bf16[32,512]{1,0:T(8,128)(2,1)S(1)}, bf16[32,512]{1,0:T(8,128)(2,1)S(1)}, u32[]{:S(2)}, u32[]{:S(2)}) collective-permute-start(bf16[32,512]{1,0:T(8,128)(2,1)S(1)} %get-tuple-element.54), channel_id=1, source_target_pairs={{0,12},{4,8},{8,4},{12,0},{1,13},{5,9},{9,5},{13,1},{2,14},{6,10},... | collective-permute-start | bytes 98312 | tf_op jit(solution)/shard_map/ppermute | solution.py:21
  23.4 21.4 %collective-permute-start.4 = (bf16[32,512]{1,0:T(8,128)(2,1)S(1)}, bf16[32,512]{1,0:T(8,128)(2,1)S(1)}, u32[]{:S(2)}, u32[]{:S(2)}) collective-permute-start(bf16[32,512]{1,0:T(8,128)(2,1)S(1)} %get-tuple-element.54), channel_id=1, source_target_pairs={{0,8},{4,12},{8,0},{12,4},{1,9},{5,13},{9,1},{13,5},{2,10},{6,14},... | collective-permute-start | bytes 98312 | tf_op jit(solution)/shard_map/ppermute | solution.py:21
  46.4 9.5 %collective-permute-start.6 = (bf16[32,2048]{1,0:T(8,128)(2,1)S(1)}, bf16[32,2048]{1,0:T(8,128)(2,1)S(1)}, u32[]{:S(2)}, u32[]{:S(2)}) collective-permute-start(bf16[32,2048]{1,0:T(8,128)(2,1)S(1)} %constant_dynamic-update-slice_fusion.refs_0_), channel_id=1, source_target_pairs={{0,1},{1,0},{2,3},{3,2},{4,5},{5,4},{6,7},{7,6},{8,9},{9,8},{10,11... | collective-permute-start | bytes 393224 | tf_op jit(solution)/shard_map/ppermute | solution.py:21
  50.6 9.2 %collective-permute-start.13 = (bf16[128,1024]{1,0:T(8,128)(2,1)S(1)}, bf16[128,1024]{1,0:T(8,128)(2,1)S(1)}, u32[]{:S(2)}, u32[]{:S(2)}) collective-permute-start(bf16[128,1024]{1,0:T(8,128)(2,1)S(1)} %get-tuple-element.58), channel_id=1, source_target_pairs={{0,4},{4,0},{8,12},{12,8},{1,5},{5,1},{9,13},{13,9},{2,6},{6,2},{1... | collective-permute-start | bytes 786440 | tf_op jit(solution)/shard_map/ppermute | solution.py:21
  53.5 12.6 %collective-permute-start.15 = (bf16[128,1024]{1,0:T(8,128)(2,1)S(1)}, bf16[128,1024]{1,0:T(8,128)(2,1)S(1)}, u32[]{:S(2)}, u32[]{:S(2)}) collective-permute-start(bf16[128,1024]{1,0:T(8,128)(2,1)S(1)} %get-tuple-element.59), channel_id=1, source_target_pairs={{0,12},{4,8},{8,4},{12,0},{1,13},{5,9},{9,5},{13,1},{2,14},{6,10},... | collective-permute-start | bytes 786440 | tf_op jit(solution)/shard_map/ppermute | solution.py:21
  56.0 22.2 %collective-permute-start.17 = (bf16[128,1024]{1,0:T(8,128)(2,1)S(1)}, bf16[128,1024]{1,0:T(8,128)(2,1)S(1)}, u32[]{:S(2)}, u32[]{:S(2)}) collective-permute-start(bf16[128,1024]{1,0:T(8,128)(2,1)S(1)} %get-tuple-element.60), channel_id=1, source_target_pairs={{0,8},{4,12},{8,0},{12,4},{1,9},{5,13},{9,1},{13,5},{2,10},{6,14},... | collective-permute-start | bytes 786440 | tf_op jit(solution)/shard_map/ppermute | solution.py:21
  56.0 23.7 %collective-permute-start.19 = (bf16[128,1024]{1,0:T(8,128)(2,1)S(1)}, bf16[128,1024]{1,0:T(8,128)(2,1)S(1)}, u32[]{:S(2)}, u32[]{:S(2)}) collective-permute-start(bf16[128,1024]{1,0:T(8,128)(2,1)S(1)} %get-tuple-element.61), channel_id=1, source_target_pairs={{0,4},{4,0},{8,12},{12,8},{1,5},{5,1},{9,13},{13,9},{2,6},{6,2},{1... | collective-permute-start | bytes 786440 | tf_op jit(solution)/shard_map/ppermute | solution.py:21
  57.9 22.3 %collective-permute-start.10 = (bf16[128,1024]{1,0:T(8,128)(2,1)S(1)}, bf16[128,1024]{1,0:T(8,128)(2,1)S(1)}, u32[]{:S(2)}, u32[]{:S(2)}) collective-permute-start(bf16[128,1024]{1,0:T(8,128)(2,1)S(1)} %collective-permute-done.9.refs_5_), channel_id=1, source_target_pairs={{0,16},{16,0},{1,17},{17,1},{2,18},{18,2},{3,19},{19,3},{4,20},{20... | collective-permute-start | bytes 786440 | tf_op jit(solution)/shard_map/ppermute | solution.py:21
  59.8 21.9 %collective-permute-start.12 = (bf16[128,1024]{1,0:T(8,128)(2,1)S(1)}, bf16[128,1024]{1,0:T(8,128)(2,1)S(1)}, u32[]{:S(2)}, u32[]{:S(2)}) collective-permute-start(bf16[128,1024]{1,0:T(8,128)(2,1)S(1)} %collective-permute-done.11.refs_7_), channel_id=1, source_target_pairs={{0,16},{16,0},{1,17},{17,1},{2,18},{18,2},{3,19},{19,3},{4,20},{20... | collective-permute-start | bytes 786440 | tf_op jit(solution)/shard_map/ppermute | solution.py:21
  66.1 15.7 %collective-permute-start.14 = (bf16[128,1024]{1,0:T(8,128)(2,1)S(1)}, bf16[128,1024]{1,0:T(8,128)(2,1)S(1)}, u32[]{:S(2)}, u32[]{:S(2)}) collective-permute-start(bf16[128,1024]{1,0:T(8,128)(2,1)S(1)} %collective-permute-done.13.refs_9_), channel_id=1, source_target_pairs={{0,16},{16,0},{1,17},{17,1},{2,18},{18,2},{3,19},{19,3},{4,20},{20... | collective-permute-start | bytes 786440 | tf_op jit(solution)/shard_map/ppermute | solution.py:21
  78.2 9.2 %collective-permute-start.16 = (bf16[128,1024]{1,0:T(8,128)(2,1)S(1)}, bf16[128,1024]{1,0:T(8,128)(2,1)S(1)}, u32[]{:S(2)}, u32[]{:S(2)}) collective-permute-start(bf16[128,1024]{1,0:T(8,128)(2,1)S(1)} %collective-permute-done.15.refs_11_), channel_id=1, source_target_pairs={{0,16},{16,0},{1,17},{17,1},{2,18},{18,2},{3,19},{19,3},{4,20},{20... | collective-permute-start | bytes 786440 | tf_op jit(solution)/shard_map/ppermute | solution.py:21
  79.7 13.3 %collective-permute-start.18 = (bf16[128,1024]{1,0:T(8,128)(2,1)S(1)}, bf16[128,1024]{1,0:T(8,128)(2,1)S(1)}, u32[]{:S(2)}, u32[]{:S(2)}) collective-permute-start(bf16[128,1024]{1,0:T(8,128)(2,1)S(1)} %collective-permute-done.17.refs_13_), channel_id=1, source_target_pairs={{0,16},{16,0},{1,17},{17,1},{2,18},{18,2},{3,19},{19,3},{4,20},{20... | collective-permute-start | bytes 786440 | tf_op jit(solution)/shard_map/ppermute | solution.py:21
  80.2 16.6 %collective-permute-start.20 = (bf16[128,1024]{1,0:T(8,128)(2,1)S(1)}, bf16[128,1024]{1,0:T(8,128)(2,1)S(1)}, u32[]{:S(2)}, u32[]{:S(2)}) collective-permute-start(bf16[128,1024]{1,0:T(8,128)(2,1)S(1)} %collective-permute-done.19.refs_15_), channel_id=1, source_target_pairs={{0,16},{16,0},{1,17},{17,1},{2,18},{18,2},{3,19},{19,3},{4,20},{20... | collective-permute-start | bytes 786440 | tf_op jit(solution)/shard_map/ppermute | solution.py:21
  98.5 11.1 %collective-permute-start.22 = (bf16[128,1024]{1,0:T(8,128)(2,1)S(1)}, bf16[128,1024]{1,0:T(8,128)(2,1)S(1)}, u32[]{:S(2)}, u32[]{:S(2)}) collective-permute-start(bf16[128,1024]{1,0:T(8,128)(2,1)S(1)} %get-tuple-element.62.refs_0_.refs_5_.fresh_ref), channel_id=1, source_target_pairs={{0,12},{4,8},{8,4},{12,0},{1,13},{5,9},{9,5},{13,1},{2,14},{6,10},... | collective-permute-start | bytes 786440 | tf_op jit(solution)/shard_map/ppermute | solution.py:21
  101.0 11.7 %collective-permute-start.21 = (bf16[128,1024]{1,0:T(8,128)(2,1)S(1)}, bf16[128,1024]{1,0:T(8,128)(2,1)S(1)}, u32[]{:S(2)}, u32[]{:S(2)}) collective-permute-start(bf16[128,1024]{1,0:T(8,128)(2,1)S(1)} %get-tuple-element.62.refs_0_.refs_5_.fresh_ref), channel_id=1, source_target_pairs={{0,4},{4,0},{8,12},{12,8},{1,5},{5,1},{9,13},{13,9},{2,6},{6,2},{1... | collective-permute-start | bytes 786440 | tf_op jit(solution)/shard_map/ppermute | solution.py:21
  143.8 11.1 %collective-permute-start.34 = (bf16[128,1024]{1,0:T(8,128)(2,1)S(1)}, bf16[128,1024]{1,0:T(8,128)(2,1)S(1)}, u32[]{:S(2)}, u32[]{:S(2)}) collective-permute-start(bf16[128,1024]{1,0:T(8,128)(2,1)S(1)} %output.5.refs_0_.refs_5_.fresh_ref), channel_id=1, source_target_pairs={{0,12},{4,8},{8,4},{12,0},{1,13},{5,9},{9,5},{13,1},{2,14},{6,10},... | collective-permute-start | bytes 786440 | tf_op jit(solution)/shard_map/ppermute | solution.py:21
  144.7 13.9 %collective-permute-start.33 = (bf16[128,1024]{1,0:T(8,128)(2,1)S(1)}, bf16[128,1024]{1,0:T(8,128)(2,1)S(1)}, u32[]{:S(2)}, u32[]{:S(2)}) collective-permute-start(bf16[128,1024]{1,0:T(8,128)(2,1)S(1)} %output.5.refs_0_.refs_5_.fresh_ref), channel_id=1, source_target_pairs={{0,4},{4,0},{8,12},{12,8},{1,5},{5,1},{9,13},{13,9},{2,6},{6,2},{1... | collective-permute-start | bytes 786440 | tf_op jit(solution)/shard_map/ppermute | solution.py:21
  154.9 9.5 %collective-permute-start.35 = (bf16[128,1024]{1,0:T(8,128)(2,1)S(1)}, bf16[128,1024]{1,0:T(8,128)(2,1)S(1)}, u32[]{:S(2)}, u32[]{:S(2)}) collective-permute-start(bf16[128,1024]{1,0:T(8,128)(2,1)S(1)} %collective-permute-done.34.refs_3_), channel_id=1, source_target_pairs={{0,4},{4,0},{8,12},{12,8},{1,5},{5,1},{9,13},{13,9},{2,6},{6,2},{1... | collective-permute-start | bytes 786440 | tf_op jit(solution)/shard_map/ppermute | solution.py:21
  190.0 11.1 %collective-permute-start.46 = (bf16[128,1024]{1,0:T(8,128)(2,1)S(1)}, bf16[128,1024]{1,0:T(8,128)(2,1)S(1)}, u32[]{:S(2)}, u32[]{:S(2)}) collective-permute-start(bf16[128,1024]{1,0:T(8,128)(2,1)S(1)} %output.6.refs_0_.refs_5_.fresh_ref), channel_id=1, source_target_pairs={{0,12},{4,8},{8,4},{12,0},{1,13},{5,9},{9,5},{13,1},{2,14},{6,10},... | collective-permute-start | bytes 786440 | tf_op jit(solution)/shard_map/ppermute | solution.py:21
  191.6 13.9 %collective-permute-start.45 = (bf16[128,1024]{1,0:T(8,128)(2,1)S(1)}, bf16[128,1024]{1,0:T(8,128)(2,1)S(1)}, u32[]{:S(2)}, u32[]{:S(2)}) collective-permute-start(bf16[128,1024]{1,0:T(8,128)(2,1)S(1)} %output.6.refs_0_.refs_5_.fresh_ref), channel_id=1, source_target_pairs={{0,4},{4,0},{8,12},{12,8},{1,5},{5,1},{9,13},{13,9},{2,6},{6,2},{1... | collective-permute-start | bytes 786440 | tf_op jit(solution)/shard_map/ppermute | solution.py:21
  201.0 9.9 %collective-permute-start.47 = (bf16[128,1024]{1,0:T(8,128)(2,1)S(1)}, bf16[128,1024]{1,0:T(8,128)(2,1)S(1)}, u32[]{:S(2)}, u32[]{:S(2)}) collective-permute-start(bf16[128,1024]{1,0:T(8,128)(2,1)S(1)} %collective-permute-done.46.refs_3_), channel_id=1, source_target_pairs={{0,4},{4,0},{8,12},{12,8},{1,5},{5,1},{9,13},{13,9},{2,6},{6,2},{1... | collective-permute-start | bytes 786440 | tf_op jit(solution)/shard_map/ppermute | solution.py:21
  (39 other events, 218.4 us)

commit v4 on v3

--- a/solution.py
+++ b/solution.py
@@ -9,7 +9,6 @@
 
 HD = 128
 BATCHES = 1
-CHUNKS = 2
 EPSILON = 1e-05
 MASKED = -1e30
 LANES = 128
@@ -63,7 +62,7 @@
         grid_spec=pltpu.PrefetchScalarGridSpec(
             num_scalar_prefetch=1,
             grid=(1,),
-            in_specs=[pl.BlockSpec(memory_space=pl.ANY)],
+            in_specs=[pl.BlockSpec(memory_space=pltpu.HBM)],
             out_specs=[pl.BlockSpec(memory_space=pl.ANY) for _ in shapes],
             scratch_shapes=[pltpu.SemaphoreType.DMA((len(shapes),))],
         ),
@@ -103,14 +102,14 @@
 
 
 def prepare_kernel(batch, batches, dp, levels, branch, info_ref, parents_ref, *refs):
-    root_ref, chosen_refs = refs[0], refs[1 : levels]
-    mask_refs, table_ref = refs[levels : 2 * levels], refs[2 * levels]
-    rows, requests = root_ref.shape
+    count = len(levels)
+    chosen_refs, mask_refs, table_ref = refs[:count], refs[count : 2 * count], refs[-1]
+    rows, requests = table_ref.shape[0], parents_ref.shape[0]
     local = requests // dp
     per_block = local // batches
     own = per_block * branch
-    for level in range(levels):
-        width = requests if level == 0 else rows
+    for chosen_ref, level in zip(chosen_refs, levels):
+        width = chosen_ref.shape[1]
         line = lax.broadcasted_iota(jnp.int32, (branch, width), 0)
         column = lax.broadcasted_iota(jnp.int32, (branch, width), 1)
         for step in range(dp):
@@ -127,38 +126,35 @@
                 table_ref[first : first + branch, :width] = jnp.where(
                     column == place, 1.0, 0.0
                 )
-        chosen = table_ref[:, :width].astype(jnp.bfloat16)
-        if level == 0:
-            root_ref[...] = chosen
-        else:
-            chosen_refs[level - 1][...] = chosen
-    ups = [ref[:own, :own] for ref in chosen_refs]
+        chosen_ref[...] = table_ref[:, :width].astype(jnp.bfloat16)
     line = lax.broadcasted_iota(jnp.int32, (own, own), 0)
     column = lax.broadcasted_iota(jnp.int32, (own, own), 1)
-    for level in range(levels):
+    for mask_ref, level in zip(mask_refs, levels):
         current = jnp.where(line == column, 1.0, 0.0)
         blocks = [current]
         for upper in range(level, 0, -1):
+            above = chosen_refs[upper - levels[0]][:own, :own]
             current = jnp.dot(
-                current.astype(jnp.bfloat16), ups[upper - 1], preferred_element_type=jnp.float32
+                current.astype(jnp.bfloat16), above, preferred_element_type=jnp.float32
             )
             blocks.insert(0, current)
-        for place in range(levels):
+        for place in range(mask_ref.shape[1] // own):
             span = slice(place * own, (place + 1) * own)
             if place < len(blocks):
-                mask_refs[level][:, span] = blocks[place]
+                mask_ref[:, span] = blocks[place]
             else:
-                mask_refs[level][:, span] = jnp.zeros((own, own), jnp.float32)
-
-
-def prepare(batch, batches, info, parents, dp, levels, branch):
+                mask_ref[:, span] = jnp.zeros((own, own), jnp.float32)
+
+
+def prepare(batch, batches, info, parents, dp, levels, depths, branch):
     requests = parents.shape[0]
     own = requests // dp // batches * branch
     rows = dp * own
-    half, single = jnp.bfloat16, jnp.float32
-    out_shape = [jax.ShapeDtypeStruct((rows, requests), half)]
-    out_shape += [jax.ShapeDtypeStruct((rows, rows), half)] * (levels - 1)
-    out_shape += [jax.ShapeDtypeStruct((own, levels * own), single)] * levels
+    out_shape = [
+        jax.ShapeDtypeStruct((rows, rows if level else requests), jnp.bfloat16)
+        for level in levels
+    ]
+    out_shape += [jax.ShapeDtypeStruct((own, depths * own), jnp.float32) for _ in levels]
     outs = pl.pallas_call(
         functools.partial(prepare_kernel, batch, batches, dp, levels, branch),
         in_specs=[pl.BlockSpec(memory_space=pltpu.SMEM)] * 2,
@@ -168,19 +164,25 @@
         compiler_params=pltpu.CompilerParams(vmem_limit_bytes=VMEM_BYTES),
         name="prepare",
     )(info, parents)
-    return outs[:levels], outs[levels:]
-
-
-def project_kernel(level, batch, pieces, steps, dp, info_ref, index_ref, *refs):
+    return list(outs[: len(levels)]), list(outs[len(levels) :])
+
+
+def project_kernel(
+    level, batch, places, share, spread, last, dp, info_ref, index_ref, *refs
+):
+    pieces = len(places) if spread else 1
     features = refs[:pieces]
     embed_ref, gain_ref, query_ref, keyval_ref = refs[pieces : pieces + 4]
-    out_refs = refs[pieces + 4 : pieces + 4 + dp]
-    cols = query_ref.shape[0] // steps
+    rest = refs[pieces + 4 :]
+    head_cols = query_ref.shape[1]
+    width = head_cols + keyval_ref.shape[1]
     query = keyval = squares = None
-    for step in range(steps):
-        offset = pl.multiple_of(info_ref[dp + 3 + step] * cols, LANES)
+    for piece, place in enumerate(places):
+        place, start = place
+        cols = features[piece].shape[1] if spread else share
+        offset = pl.multiple_of(info_ref[dp + 3 + place] * share + start, LANES)
         columns = pl.ds(offset, cols)
-        held = features[step][...] if pieces == steps else features[0][:, columns]
+        held = features[piece][...] if spread else features[0][:, columns]
         state = parent_rows(index_ref, held) + embed_rows(
             info_ref, embed_ref, batch, level, columns
         )
@@ -189,11 +191,22 @@
         scaled = (state * gain).astype(jnp.bfloat16)
         first = jnp.dot(scaled, query_ref[columns, :], preferred_element_type=jnp.float32)
         second = jnp.dot(scaled, keyval_ref[columns, :], preferred_element_type=jnp.float32)
-        query = first if step == 0 else query + first
-        keyval = second if step == 0 else keyval + second
-        squares = square if step == 0 else squares + square
-    head_cols = query.shape[1]
-    width = head_cols + keyval.shape[1]
+        query = first if piece == 0 else query + first
+        keyval = second if piece == 0 else keyval + second
+        squares = square if piece == 0 else squares + square
+    if len(rest) != (dp if last else 1):
+        before_ref = rest[0]
+        rest = rest[1:]
+        query = query + before_ref[:, :head_cols]
+        keyval = keyval + before_ref[:, head_cols:width]
+        squares = squares + before_ref[:, width : width + 1]
+    if not last:
+        total_ref = rest[0]
+        total_ref[:, :head_cols] = query
+        total_ref[:, head_cols:width] = keyval
+        total_ref[:, width:] = jnp.broadcast_to(squares, (squares.shape[0], LANES))
+        return
+    out_refs = rest
     rows = out_refs[0].shape[0]
     lane = lax.broadcasted_iota(jnp.int32, (rows, LANES), 1)
     for block in range(dp):
@@ -283,26 +296,31 @@
             out_ref[:, (first + g) * HD : (first + g + 1) * HD] = block
 
 
-def output_kernel(level, batch, dp, weights, keep, info_ref, index_ref, *refs):
+def output_kernel(level, batch, dp, weights, keep, final, info_ref, index_ref, *refs):
     attended = refs[:dp]
     weight_refs = refs[dp : dp + len(weights)]
     feature_ref, embed_ref = refs[dp + len(weights) : dp + len(weights) + 2]
     rest = refs[dp + len(weights) + 2 :]
-    fresh_ref, gathered_ref = rest[0], rest[-1]
     rows = attended[0].shape[0]
-    share = fresh_ref.shape[1]
+    if final:
+        _, held_ref, gathered_ref, staged_ref, sems = rest
+        share = staged_ref.shape[3]
+    else:
+        kept, gathered_ref = rest[-2], rest[-1]
+        out_refs = rest[:-2] if keep else rest[:-1]
+        share = out_refs[0].shape[1]
     for step in range(dp):
         gathered_ref[step * rows : (step + 1) * rows, :] = attended[step][...]
     spans = []
     for weight_ref, (start, side) in zip(weight_refs, weights):
         depth = weight_ref.shape[0]
         if side is not None:
-            start = pl.multiple_of(start + info_ref[dp + side], LANES)
+            start = pl.multiple_of(start + info_ref[dp + side], LANES // 4)
         spans.append(pl.ds(start, depth))
         if keep:
-            rest[1][spans[-1], :] = weight_ref[...]
+            kept[spans[-1], :] = weight_ref[...]
     if keep:
-        weight_refs, spans = [rest[1]], [slice(None)]
+        weight_refs = [kept]
     offset = pl.multiple_of(info_ref[dp + 2] * share, LANES)
     block = min(2 * LANES, share)
     for start in range(0, share, block):
@@ -313,13 +331,34 @@
         fresh = parent_rows(index_ref, held) + embed_rows(
             info_ref, embed_ref, batch, level, pl.ds(offset + start, block)
         )
-        for weight_ref, span in zip(weight_refs, spans):
-            fresh = fresh + jnp.dot(
-                gathered_ref[:, span],
-                weight_ref[:, start : start + block],
-                preferred_element_type=jnp.float32,
+        fresh = fresh + jnp.dot(
+            gathered_ref[...],
+            weight_refs[0][:, start : start + block],
+            preferred_element_type=jnp.float32,
+        )
+        if not final:
+            write_halves(fresh.astype(jnp.bfloat16), start, out_refs)
+            continue
+        branch = staged_ref.shape[2]
+        for step in range(dp):
+            for request in range(staged_ref.shape[1]):
+                first = (step * staged_ref.shape[1] + request) * branch
+                staged_ref[step, request, :, start : start + block] = fresh[
+                    first : first + branch
+                ].astype(jnp.bfloat16)
+    if final:
+        copies = [
+            pltpu.make_async_copy(
+                staged_ref.at[step],
+                held_ref.at[info_ref[step], batch, :, level],
+                sems.at[step],
             )
-        fresh_ref[:, start : start + block] = fresh.astype(jnp.bfloat16)
+            for step in range(dp)
+        ]
+        for copy in copies:
+            copy.start()
+        for copy in copies:
+            copy.wait()
 
 
 def store_kernel(info_ref, fresh_ref, *refs):
@@ -333,25 +372,124 @@
             out_ref[info_ref[step], 0, request, 0] = block
 
 
+def partial_kernel(dp, info_ref, *refs):
+    attended, weight_ref = refs[:dp], refs[dp]
+    outs = refs[dp + 1 :]
+    left = jnp.concatenate([ref[...] for ref in attended], axis=0)
+    share = outs[0].shape[1]
+    block = min(4 * LANES, share)
+    for place, out_ref in enumerate(outs):
+        offset = pl.multiple_of(info_ref[dp + 3 + place] * share, LANES)
+        for start in range(0, share, block):
+            out_ref[:, start : start + block] = jnp.dot(
+                left,
+                weight_ref[:, pl.ds(offset + start, block)],
+                preferred_element_type=jnp.float32,
+            ).astype(jnp.bfloat16)
+
+
+def partial(info, attended, w_out, shares):
+    dp = len(attended)
+    rows = dp * attended[0].shape[0]
+    share_cols = w_out.shape[1] // shares
+    operands = [*attended, w_out]
+    return pl.pallas_call(
+        functools.partial(partial_kernel, dp),
+        grid_spec=pltpu.PrefetchScalarGridSpec(
+            num_scalar_prefetch=1,
+            grid=(),
+            in_specs=[pl.BlockSpec(memory_space=pltpu.VMEM)] * len(operands),
+            out_specs=[pl.BlockSpec(memory_space=pltpu.VMEM)] * shares,
+        ),
+        out_shape=[jax.ShapeDtypeStruct((rows, share_cols), jnp.bfloat16)] * shares,
+        compiler_params=pltpu.CompilerParams(vmem_limit_bytes=VMEM_BYTES),
+        name="partial",
+    )(info, *operands)
+
+
+def combine_kernel(level, batch, dp, info_ref, index_ref, *refs):
+    terms, (feature_ref, embed_ref, *out_refs) = refs[:-5], refs[-5:]
+    share = out_refs[0].shape[1]
+    offset = pl.multiple_of(info_ref[dp + 2] * share, LANES)
+    columns = pl.ds(offset, share)
+    fresh = parent_rows(index_ref, feature_ref[:, columns]) + embed_rows(
+        info_ref, embed_ref, batch, level, columns
+    )
+    for term in terms:
+        fresh = fresh + term[...].astype(jnp.float32)
+    write_halves(fresh.astype(jnp.bfloat16), 0, out_refs)
+
+
+def write_halves(fresh, start, out_refs):
+    width = fresh.shape[1]
+    out_refs[0][:, start : start + width] = fresh
+    for half_ref in out_refs[1:]:
+        half = half_ref.shape[1]
+        low, high = max(start, 0), min(start + width, half)
+        if low < high:
+            half_ref[:, low:high] = fresh[:, low - start : high - start]
+        start -= half
+
+
+def halves(rows, share_cols):
+    shapes = [(rows, share_cols), (rows, share_cols // 2), (rows, share_cols // 2)]
+    return [jax.ShapeDtypeStruct(shape, jnp.bfloat16) for shape in shapes]
+
+
+def combine(level, batch, info, index, terms, features, embeds):
+    operands = [index, *terms, features, embeds]
+    return pl.pallas_call(
+        functools.partial(combine_kernel, level, batch, embeds.shape[0]),
+        grid_spec=pltpu.PrefetchScalarGridSpec(
+            num_scalar_prefetch=1,
+            grid=(),
+            in_specs=[pl.BlockSpec(memory_space=pltpu.VMEM)] * len(operands),
+            out_specs=[pl.BlockSpec(memory_space=pltpu.VMEM)] * 3,
+        ),
+        out_shape=halves(*terms[0].shape),
+        compiler_params=pltpu.CompilerParams(vmem_limit_bytes=VMEM_BYTES),
+        name="combine",
+    )(info, *operands)
+
+
+def store_kernel(info_ref, fresh_ref, *refs):
+    out_ref = refs[-1]
+    dp, per_block, branch = out_ref.shape[0], out_ref.shape[2], out_ref.shape[4]
+    fresh = fresh_ref[...].astype(jnp.float32)
+    for step in range(dp):
+        for request in range(per_block):
+            start = (step * per_block + request) * branch
+            block = fresh[start : start + branch].astype(jnp.bfloat16)
+            out_ref[info_ref[step], 0, request, 0] = block
+
+
 def full(x):
     return pl.BlockSpec(x.shape, lambda i, *_: (0,) * x.ndim)
 
 
-def project(level, batch, steps, info, index, pieces, embeds, gain, w_query, keyval):
+def project(
+    level, batch, places, share, info, index, pieces, embeds, gain, w_query, keyval, before, last
+):
     dp, _, per_block, _, branch, feat_cols = embeds.shape
     head_cols, kv_cols = w_query.shape[1], keyval.shape[1]
     rows = per_block * branch
     width = head_cols + kv_cols + LANES
     operands = [index, *pieces, embeds, gain, w_query, keyval]
+    operands += [] if before is None else [before]
+    if last:
+        out_shape = [jax.ShapeDtypeStruct((rows, width), jnp.bfloat16)] * dp
+    else:
+        out_shape = [jax.ShapeDtypeStruct((dp * rows, width), jnp.float32)]
+    spread = level > 0 and len(pieces) == len(places)
     return pl.pallas_call(
-        functools.partial(project_kernel, level, batch, len(pieces), steps, dp),
+        functools.partial(project_kernel, level, batch, places, share, spread, last, dp),
         grid_spec=pltpu.PrefetchScalarGridSpec(
             num_scalar_prefetch=1,
             grid=(),
             in_specs=[pl.BlockSpec(memory_space=pltpu.VMEM)] * len(operands),
-            out_specs=[pl.BlockSpec(memory_space=pltpu.VMEM)] * dp,
-        ),
-        out_shape=[jax.ShapeDtypeStruct((rows, width), jnp.bfloat16)] * dp,
+            out_specs=[pl.BlockSpec(memory_space=pltpu.VMEM)] * len(out_shape),
+        ),
+        out_shape=out_shape,
         compiler_params=pltpu.CompilerParams(vmem_limit_bytes=VMEM_BYTES),
         cost_estimate=pl.CostEstimate(
             flops=2 * dp * rows * feat_cols * (head_cols + kv_cols),
@@ -396,27 +534,42 @@
     )(lengths, *operands)
 
 
-def output(level, batch, info, index, attended, weights, features, embeds, share_cols):
+def output(level, batch, info, index, attended, weights, features, embeds, share_cols, held):
     dp, _, per_block, _, branch, _ = embeds.shape
     rows = dp * per_block * branch
     arrays = [w for w, _, _ in weights]
     places = [(start, side) for _, start, side in weights]
     depth = sum(w.shape[0] for w in arrays)
     keep = len(weights) > 1
+    final = held is not None
     operands = [index, *attended, *arrays, features, embeds]
-    out_shape = [jax.ShapeDtypeStruct((rows, share_cols), jnp.bfloat16)]
-    if keep:
-        out_shape.append(pltpu.VMEM((depth, share_cols), jnp.bfloat16))
+    in_specs = [pl.BlockSpec(memory_space=pltpu.VMEM)] * len(operands)
+    scratch = [pltpu.VMEM((rows, depth), jnp.bfloat16)]
+    aliases = {}
+    if final:
+        out_shape = [jax.ShapeDtypeStruct(held.shape, held.dtype)]
+        out_specs = [pl.BlockSpec(memory_space=pl.ANY)]
+        aliases = {len(operands) + 1: 0}
+        operands.append(held)
+        in_specs.append(pl.BlockSpec(memory_space=pl.ANY))
+        scratch.append(pltpu.VMEM((dp, per_block, branch, share_cols), jnp.bfloat16))
+        scratch.append(pltpu.SemaphoreType.DMA((dp,)))
+    else:
+        out_shape = halves(rows, share_cols)
+        if keep:
+            out_shape.append(pltpu.VMEM((depth, share_cols), jnp.bfloat16))
+        out_specs = [pl.BlockSpec(memory_space=pltpu.VMEM)] * len(out_shape)
     return pl.pallas_call(
-        functools.partial(output_kernel, level, batch, dp, places, keep),
+        functools.partial(output_kernel, level, batch, dp, places, keep, final),
         grid_spec=pltpu.PrefetchScalarGridSpec(
             num_scalar_prefetch=1,
             grid=(),
-            in_specs=[pl.BlockSpec(memory_space=pltpu.VMEM)] * len(operands),
-            out_specs=[pl.BlockSpec(memory_space=pltpu.VMEM)] * len(out_shape),
-            scratch_shapes=[pltpu.VMEM((rows, depth), jnp.bfloat16)],
+            in_specs=in_specs,
+            out_specs=out_specs,
+            scratch_shapes=scratch,
         ),
         out_shape=out_shape,
+        input_output_aliases=aliases,
         compiler_params=pltpu.CompilerParams(vmem_limit_bytes=VMEM_BYTES),
         cost_estimate=pl.CostEstimate(
             flops=2 * rows * depth * share_cols,
@@ -482,37 +635,34 @@
     by_swaps = tensor == 4 and groups == 2
 
     half = head_rows // 2 if by_swaps else 0
-    steps = tensor if by_swaps else 1
+    steps = tuple(range(tensor)) if by_swaps else (0,)
     info = [dp_index ^ step for step in range(dp)]
     info += [group_index * half, (1 - group_index) * half, tensor_index]
     info += [tensor_index ^ step for step in range(tensor)] if by_swaps else [0 * dp_index]
     info = jnp.stack(info)
 
     if by_swaps:
-        depth = half // CHUNKS
-        plan = [(0, 0, head_rows)]
-        for chunk in range(CHUNKS):
-            plan += [(step, chunk * depth, depth) for step in (3, 2, 1)]
-        cuts = cut(info, w_out, tuple(plan), share_cols, dp)
+        early = half * 5 // 8
+        plan = ((0, 0, head_rows), (3, 0, early), (2, 0, early), (1, 0, half))
+        plan += ((3, early, half - early), (2, early, half - early))
+        cuts = cut(info, w_out, plan, share_cols, dp)
+        info, *cuts = lax.optimization_barrier((info, *cuts))
         weights = [(cuts[0], 0, None)]
-        for (step, start, _), sent in zip(plan[1:], cuts[1:]):
-            arrived = swap(sent, "tensor", step)
-            weights.append((arrived, step * head_rows + start, 0))
-            weights.append((swap(arrived, "groups", 1), step * head_rows + start, 1))
+        moved = [swap(sent, "tensor", step) for sent, (step, _, _) in zip(cuts[1:4], plan[1:4])]
     else:
         spread = lax.all_to_all(w_out, "tensor", 1, 0, tiled=True)
         weights = [(load(info, spread), 0, None)]
 
     chosen, masks = [], []
     for batch in range(batches):
-        made = prepare(batch, batches, info, parents, dp, depths, branch)
+        made = prepare(batch, batches, info, parents, dp, (0,), depths, branch)
         chosen.append(made[0])
         masks.append(made[1])
     embeds = branch_embeds.reshape(dp, batches, per_block, depths, branch, feat_cols)
     gain = norm_gain.reshape(1, feat_cols)
     keyval = w_keyval.reshape(feat_cols, -1)
     w_query, keyval, embeds, cache_kv = (
-        load(info, x) for x in (w_query, keyval, embeds, cache_kv)
+        x for x in (w_query, keyval, embeds, cache_kv)
     )
 
     earlier = [[] for _ in range(batches)]
@@ -522,18 +672,24 @@
     for level in range(depths):
         attended = []
         for batch in range(batches):
-            sums = project(
-                level,
-                batch,
-                steps,
-                info,
-                chosen[batch][level],
-                gathered[batch],
-                embeds,
-                gain,
-                w_query,
-                keyval,
-            )
+            fixed = (embeds, gain, w_query, keyval)
+            index = chosen[batch][level]
+            pieces = gathered[batch]
+            if by_swaps and level > 0:
+                first = ((0, 0), (1, 0), (3, 0), (3, share_cols // 2))
+                second = ((2, 0), (2, share_cols // 2))
+                before = project(
+                    level, batch, first, share_cols, info, index, pieces[:4], *fixed, None, False
+                )[0]
+                sums = project(
+                    level, batch, second, share_cols, info, index, pieces[4:], *fixed, before, True
+                )
+            else:
+                places = tuple((step, 0) for step in steps)
+                cols = feat_cols // len(steps)
+                sums = project(
+                    level, batch, places, cols, info, index, pieces, *fixed, None, True
+                )
             parts = [sums[0]] + [swap(sums[step], "dp", step) for step in range(1, dp)]
             mixed, fresh = attend(
                 batch,
@@ -547,35 +703,74 @@
                 earlier[batch],
             )
             earlier[batch] = earlier[batch] + [fresh]
-            if by_swaps:
+            if level == 0:
+                mixed, later = lax.optimization_barrier((mixed, info))
+                made = prepare(
+                    batch, batches, later, parents, dp, tuple(range(1, depths)), depths, branch
+                )
+                chosen[batch] += made[0]
+                masks[batch] += made[1]
+            if by_swaps and level == 0:
+                joined = mixed
+            elif by_swaps:
                 heads = [mixed] + [swap(mixed, "tensor", step) for step in range(1, tensor)]
                 joined = jnp.concatenate(heads, axis=1)
             else:
                 joined = lax.all_gather(mixed, "tensor", axis=1, tiled=True)
             attended.append([joined] + [swap(joined, "dp", step) for step in range(1, dp)])
         for batch in range(batches):
-            shares[batch], *kept = output(
-                level,
-                batch,
-                info,
-                chosen[batch][level],
-                attended[batch],
-                weights,
-                shares[batch],
-                embeds,
-                share_cols,
-            )
-            if kept:
-                weights = [(kept[0], 0, None)]
+            index = chosen[batch][level]
+            if by_swaps and level == 0:
+                terms = list(partial(info, attended[batch], w_out, tensor))
+                sent = terms[1:]
+                if batch + 1 == batches:
+                    terms[0], *moved = lax.optimization_barrier((terms[0], *moved))
+                    others = [swap(x, "groups", 1) for x in moved]
+                terms = terms[:1] + [swap(x, "tensor", step) for step, x in enumerate(sent, 1)]
+                if batch + 1 == batches:
+                    terms[0], *others[:2] = lax.optimization_barrier((terms[0], *others[:2]))
+                shares[batch], *split = combine(
+                    level, batch, info, index, terms, shares[batch], embeds
+                )
+            else:
+                final = level + 1 == depths
+                made = output(
+                    level,
+                    batch,
+                    info,
+                    index,
+                    attended[batch],
+                    weights,
+                    shares[batch],
+                    embeds,
+                    share_cols,
+                    held if final else None,
+                )
+                if final:
+                    held = made[0]
+                    continue
+                shares[batch], *split = made[:3]
+                if len(made) > 3:
+                    weights = [(made[3], 0, None)]
             held = store(
                 level, batch, embeds.shape[:-1] + (share_cols,), info, shares[batch], held
             )
-            if level + 1 == depths:
-                continue
             own = shares[batch]
             if by_swaps:
-                far = swap(own, "tensor", 3)
-                gathered[batch] = [own, swap(own, "tensor", 1), swap(far, "tensor", 1), far]
+                far, other = (swap(x, "tensor", 3) for x in split)
+                if level == 0 and batch + 1 == batches:
+                    other, others[2], *cuts[4:] = lax.optimization_barrier(
+                        (other, others[2], *cuts[4:])
+                    )
+                    for sent, (step, _, _) in zip(cuts[4:], plan[4:]):
+                        moved.append(swap(sent, "tensor", step))
+                    others += [swap(x, "groups", 1) for x in moved[3:]]
+                    for (step, start, _), one, two in zip(plan[1:], moved, others):
+                        weights.append((one, step * head_rows + start, 0))
+                        weights.append((two, step * head_rows + start, 1))
+                near = swap(own, "tensor", 1)
+                gathered[batch] = [own, near, far, other]
+                gathered[batch] += [swap(far, "tensor", 1), swap(other, "tensor", 1)]
             else:
                 gathered[batch] = [lax.all_gather(own, "tensor", axis=1, tiled=True)]
     return held.reshape(requests, depths, branch, share_cols)

time: 238 us -> 207 us (0.87)
  waiting for transfers between devices: 135 us -> 97.4 us
  starting transfers between devices: 66.7 us -> 69.4 us
  local copies, waits for them, and re-layouts: 4.87 us -> 7.36 us
    ppermute x57 -> x61, waiting for transfers between devices: 135 us -> 97.4 us  [swap(): return lax.ppermute(x, axis, [(i, i ^ step) for i in range(size)])]
    unnamed x26 -> x35, local copies, waits for them, and re-layouts: 4.05 us -> 7.25 us
    ppermute x57 -> x61, starting transfers between devices: 66.7 us -> 69.4 us  [swap(): return lax.ppermute(x, axis, [(i, i ^ step) for i in range(size)])]
    pallas_call x8 -> x9, Pallas kernels: 11.6 us -> 12.9 us  [the longest x7 10.8 us: project(): pl.pallas_call(functools.partial(project_kernel, level, batch, places, sh...]
    pallas_call x4 -> x3, Pallas kernels: 5.05 us -> 3.78 us  [store(): pl.pallas_call(store_kernel, grid_spec=pltpu.PrefetchScalarGridSpec(num_s...]
    pallas_call x4 -> x3, Pallas kernels: 5.52 us -> 4.99 us  [output(): pl.pallas_call(functools.partial(output_kernel, level, batch, dp, places,...]
  transfers between devices with their start and end apart: 57 -> 61, of which waited for: 35 -> 34; matrix products, arithmetic and copies ran while one was open for 0% -> 1% of each run, Pallas kernels for 3% -> 10%
where the time goes in v4:
time: 207 us; the launch traced here: 206 us
  waiting for transfers between devices  97.4 us (47%)
  starting transfers between devices  69.4 us (34%)
  Pallas kernels  31.7 us (15%)
  local copies, waits for them, and re-layouts  7.36 us (4%)
    ppermute x61, waiting for transfers between devices, swap(): return lax.ppermute(x, axis, [(i, i ^ step) for i in range(size)])  97.4 us
    ppermute x61, starting transfers between devices, swap(): return lax.ppermute(x, axis, [(i, i ^ step) for i in range(size)])  69.4 us
    pallas_call x7, Pallas kernels, project(): pl.pallas_call(functools.partial(project_kernel, level, batch, places, sh...  10.8 us
    unnamed x35, local copies, waits for them, and re-layouts  7.25 us
    pallas_call x4, Pallas kernels, attend(): pl.pallas_call(functools.partial(attend_kernel, len(parts), len(earlier),...  5.77 us
    pallas_call x3, Pallas kernels, output(): pl.pallas_call(functools.partial(output_kernel, level, batch, dp, places,...  4.99 us
  transfers between devices with their start and end apart: 61, of which 34 were waited for; matrix products, arithmetic and copies ran while one was open for 1% of the time, Pallas kernels for 10%

profile of v4, /device:TPU:0, one launch (start us, length us, event | category | flops | bytes accessed | tf_op | source)
XLA Modules:
  0.0 206.4 jit_solution(15329362511129557864)
XLA Ops:
  4.4 3.0 %collective-permute-start.8 = (bf16[256,1024]{1,0:T(8,128)(2,1)S(1)}, bf16[256,1024]{1,0:T(8,128)(2,1)S(1)}, u32[]{:S(2)}, u32[]{:S(2)}) collective-permute-start(bf16[256,1024]{1,0:T(8,128)(2,1)S(1)} %get-tuple-element.98), channel_id=1, source_target_pairs={{0,4},{4,0},{8,12},{12,8},{1,5},{5,1},{9,13},{13,9},{2,6},{6,2},{1... | collective-permute-start | bytes 1572872 | tf_op jit(solution)/shard_map/ppermute | solution.py:20
  7.5 2.5 %collective-permute-start.6 = (bf16[160,1024]{1,0:T(8,128)(2,1)}, bf16[160,1024]{1,0:T(8,128)(2,1)S(1)}, u32[]{:S(2)}, u32[]{:S(2)}) collective-permute-start(bf16[160,1024]{1,0:T(8,128)(2,1)} %get-tuple-element.96), channel_id=1, source_target_pairs={{0,12},{4,8},{8,4},{12,0},{1,13},{5,9},{9,5},{13,1},{2,14},{6,10},... | collective-permute-start | bytes 983048 | tf_op jit(solution)/shard_map/ppermute | solution.py:20
  31.2 7.6 %collective-permute-done.7.refs_7_ = bf16[160,1024]{1,0:T(8,128)(2,1)S(1)} collective-permute-done((bf16[160,1024]{1,0:T(8,128)(2,1)S(1)}, bf16[160,1024]{1,0:T(8,128)(2,1)S(1)}, u32[]{:S(2)}, u32[]{:S(2)}) %collective-permute-start.7) | collective-permute-done | bytes 327712 | tf_op jit(solution)/shard_map/ppermute | solution.py:20
  42.4 3.2 %collective-permute-start.12 = (bf16[128,1024]{1,0:T(8,128)(2,1)S(1)}, bf16[128,1024]{1,0:T(8,128)(2,1)S(1)}, u32[]{:S(2)}, u32[]{:S(2)}) collective-permute-start(bf16[128,1024]{1,0:T(8,128)(2,1)S(1)} %get-tuple-element.104), channel_id=1, source_target_pairs={{0,8},{4,12},{8,0},{12,4},{1,9},{5,13},{9,1},{13,5},{2,10},{6,14},... | collective-permute-start | bytes 786440 | tf_op jit(solution)/shard_map/ppermute | solution.py:20
  45.6 3.9 %collective-permute-done.9.refs_6_ = bf16[160,1024]{1,0:T(8,128)(2,1)S(1)} collective-permute-done((bf16[160,1024]{1,0:T(8,128)(2,1)S(1)}, bf16[160,1024]{1,0:T(8,128)(2,1)S(1)}, u32[]{:S(2)}, u32[]{:S(2)}) %collective-permute-start.9) | collective-permute-done | bytes 327712 | tf_op jit(solution)/shard_map/ppermute | solution.py:20
  49.5 2.6 %collective-permute-start.13 = (bf16[128,1024]{1,0:T(8,128)(2,1)S(1)}, bf16[128,1024]{1,0:T(8,128)(2,1)S(1)}, u32[]{:S(2)}, u32[]{:S(2)}) collective-permute-start(bf16[128,1024]{1,0:T(8,128)(2,1)S(1)} %get-tuple-element.105), channel_id=1, source_target_pairs={{0,12},{4,8},{8,4},{12,0},{1,13},{5,9},{9,5},{13,1},{2,14},{6,10},... | collective-permute-start | bytes 786440 | tf_op jit(solution)/shard_map/ppermute | solution.py:20
  52.1 4.4 %collective-permute-done.10.refs_8_ = bf16[160,1024]{1,0:T(8,128)(2,1)S(1)} collective-permute-done((bf16[160,1024]{1,0:T(8,128)(2,1)S(1)}, bf16[160,1024]{1,0:T(8,128)(2,1)S(1)}, u32[]{:S(2)}, u32[]{:S(2)}) %collective-permute-start.10) | collective-permute-done | bytes 327712 | tf_op jit(solution)/shard_map/ppermute | solution.py:20
  56.5 7.1 %collective-permute-done.12.refs_2_ = bf16[128,1024]{1,0:T(8,128)(2,1)S(1)} collective-permute-done((bf16[128,1024]{1,0:T(8,128)(2,1)S(1)}, bf16[128,1024]{1,0:T(8,128)(2,1)S(1)}, u32[]{:S(2)}, u32[]{:S(2)}) %collective-permute-start.12) | collective-permute-done | bytes 262176 | tf_op jit(solution)/shard_map/ppermute | solution.py:20
  64.5 3.5 %collective-permute-start.19 = (bf16[128,1024]{1,0:T(8,128)(2,1)S(1)}, bf16[128,1024]{1,0:T(8,128)(2,1)S(1)}, u32[]{:S(2)}, u32[]{:S(2)}) collective-permute-start(bf16[128,1024]{1,0:T(8,128)(2,1)S(1)} %get-tuple-element.112.refs_0_.refs_15_.fresh_ref), channel_id=1, source_target_pairs={{0,4},{4,0},{8,12},{12,8},{1,5},{5,1},{9,13},{13,9},{2,6},{6,2},{1... | collective-permute-start | bytes 786440 | tf_op jit(solution)/shard_map/ppermute | solution.py:20
  71.8 8.5 %collective-permute-done.14.refs_2_ = bf16[128,512]{1,0:T(8,128)(2,1)S(1)} collective-permute-done((bf16[128,512]{1,0:T(8,128)(2,1)S(1)}, bf16[128,512]{1,0:T(8,128)(2,1)S(1)}, u32[]{:S(2)}, u32[]{:S(2)}) %collective-permute-start.14) | collective-permute-done | bytes 131104 | tf_op jit(solution)/shard_map/ppermute | solution.py:20
  92.9 2.5 %collective-permute-done.21.refs_2_ = bf16[32,896]{1,0:T(8,128)(2,1)S(1)} collective-permute-done((bf16[32,896]{1,0:T(8,128)(2,1)S(1)}, bf16[32,896]{1,0:T(8,128)(2,1)S(1)}, u32[]{:S(2)}, u32[]{:S(2)}) %collective-permute-start.21) | collective-permute-done | bytes 57376 | tf_op jit(solution)/shard_map/ppermute | solution.py:20
  106.9 3.9 %collective-permute-done.28.refs_3_ = bf16[32,2048]{1,0:T(8,128)(2,1)S(1)} collective-permute-done((bf16[32,2048]{1,0:T(8,128)(2,1)S(1)}, bf16[32,2048]{1,0:T(8,128)(2,1)S(1)}, u32[]{:S(2)}, u32[]{:S(2)}) %collective-permute-start.28) | collective-permute-done | bytes 131104 | tf_op jit(solution)/shard_map/ppermute | solution.py:20
  110.8 2.7 %collective-permute-done.27.refs_2_ = bf16[32,2048]{1,0:T(8,128)(2,1)S(1)} collective-permute-done((bf16[32,2048]{1,0:T(8,128)(2,1)S(1)}, bf16[32,2048]{1,0:T(8,128)(2,1)S(1)}, u32[]{:S(2)}, u32[]{:S(2)}) %collective-permute-start.27) | collective-permute-done | bytes 131104 | tf_op jit(solution)/shard_map/ppermute | solution.py:20
  117.5 2.5 %collective-permute-start.35 = (bf16[128,512]{1,0:T(8,128)(2,1)S(1)}, bf16[128,512]{1,0:T(8,128)(2,1)S(1)}, u32[]{:S(2)}, u32[]{:S(2)}) collective-permute-start(bf16[128,512]{1,0:T(8,128)(2,1)S(1)} %get-tuple-element.127), channel_id=1, source_target_pairs={{0,12},{4,8},{8,4},{12,0},{1,13},{5,9},{9,5},{13,1},{2,14},{6,10},... | collective-permute-start | bytes 393224 | tf_op jit(solution)/shard_map/ppermute | solution.py:20
  120.0 7.6 %collective-permute-done.33.refs_2_ = bf16[128,512]{1,0:T(8,128)(2,1)S(1)} collective-permute-done((bf16[128,512]{1,0:T(8,128)(2,1)S(1)}, bf16[128,512]{1,0:T(8,128)(2,1)S(1)}, u32[]{:S(2)}, u32[]{:S(2)}) %collective-permute-start.33) | collective-permute-done | bytes 131104 | tf_op jit(solution)/shard_map/ppermute | solution.py:20
  138.4 2.9 %collective-permute-done.39.refs_2_ = bf16[32,896]{1,0:T(8,128)(2,1)S(1)} collective-permute-done((bf16[32,896]{1,0:T(8,128)(2,1)S(1)}, bf16[32,896]{1,0:T(8,128)(2,1)S(1)}, u32[]{:S(2)}, u32[]{:S(2)}) %collective-permute-start.39) | collective-permute-done | bytes 57376 | tf_op jit(solution)/shard_map/ppermute | solution.py:20
  143.2 2.4 %collective-permute-start.43 = (bf16[32,512]{1,0:T(8,128)(2,1)S(1)}, bf16[32,512]{1,0:T(8,128)(2,1)S(1)}, u32[]{:S(2)}, u32[]{:S(2)}) collective-permute-start(bf16[32,512]{1,0:T(8,128)(2,1)S(1)} %get-tuple-element.135), channel_id=1, source_target_pairs={{0,12},{4,8},{8,4},{12,0},{1,13},{5,9},{9,5},{13,1},{2,14},{6,10},... | collective-permute-start | bytes 98312 | tf_op jit(solution)/shard_map/ppermute | solution.py:20
  152.4 3.9 %collective-permute-done.46.refs_3_ = bf16[32,2048]{1,0:T(8,128)(2,1)S(1)} collective-permute-done((bf16[32,2048]{1,0:T(8,128)(2,1)S(1)}, bf16[32,2048]{1,0:T(8,128)(2,1)S(1)}, u32[]{:S(2)}, u32[]{:S(2)}) %collective-permute-start.46) | collective-permute-done | bytes 131104 | tf_op jit(solution)/shard_map/ppermute | solution.py:20
  164.4 8.5 %collective-permute-done.47.refs_2_ = bf16[128,512]{1,0:T(8,128)(2,1)S(1)} collective-permute-done((bf16[128,512]{1,0:T(8,128)(2,1)S(1)}, bf16[128,512]{1,0:T(8,128)(2,1)S(1)}, u32[]{:S(2)}, u32[]{:S(2)}) %collective-permute-start.47) | collective-permute-done | bytes 131104 | tf_op jit(solution)/shard_map/ppermute | solution.py:20
  172.8 2.8 %collective-permute-done.49.refs_3_ = bf16[128,512]{1,0:T(8,128)(2,1)S(1)} collective-permute-done((bf16[128,512]{1,0:T(8,128)(2,1)S(1)}, bf16[128,512]{1,0:T(8,128)(2,1)S(1)}, u32[]{:S(2)}, u32[]{:S(2)}) %collective-permute-start.49) | collective-permute-done | bytes 131104 | tf_op jit(solution)/shard_map/ppermute | solution.py:20
  183.8 2.5 %collective-permute-done.53.refs_2_ = bf16[32,896]{1,0:T(8,128)(2,1)S(1)} collective-permute-done((bf16[32,896]{1,0:T(8,128)(2,1)S(1)}, bf16[32,896]{1,0:T(8,128)(2,1)S(1)}, u32[]{:S(2)}, u32[]{:S(2)}) %collective-permute-start.53) | collective-permute-done | bytes 57376 | tf_op jit(solution)/shard_map/ppermute | solution.py:20
  190.2 2.8 %collective-permute-start.55 = (bf16[32,512]{1,0:T(8,128)(2,1)S(1)}, bf16[32,512]{1,0:T(8,128)(2,1)S(1)}, u32[]{:S(2)}, u32[]{:S(2)}) collective-permute-start(bf16[32,512]{1,0:T(8,128)(2,1)S(1)} %get-tuple-element.146), channel_id=1, source_target_pairs={{0,4},{4,0},{8,12},{12,8},{1,5},{5,1},{9,13},{13,9},{2,6},{6,2},{1... | collective-permute-start | bytes 98312 | tf_op jit(solution)/shard_map/ppermute | solution.py:20
  193.1 2.5 %collective-permute-done.55 = bf16[32,512]{1,0:T(8,128)(2,1)S(1)} collective-permute-done((bf16[32,512]{1,0:T(8,128)(2,1)S(1)}, bf16[32,512]{1,0:T(8,128)(2,1)S(1)}, u32[]{:S(2)}, u32[]{:S(2)}) %collective-permute-start.55) | collective-permute-done | bytes 32800 | tf_op jit(solution)/shard_map/ppermute | solution.py:20
  201.5 2.7 %collective-permute-done.59.refs_2_ = bf16[32,2048]{1,0:T(8,128)(2,1)S(1)} collective-permute-done((bf16[32,2048]{1,0:T(8,128)(2,1)S(1)}, bf16[32,2048]{1,0:T(8,128)(2,1)S(1)}, u32[]{:S(2)}, u32[]{:S(2)}) %collective-permute-start.59) | collective-permute-done | bytes 131104 | tf_op jit(solution)/shard_map/ppermute | solution.py:20
  (160 shorter events, 109.4 us)
Async XLA Ops:
  4.4 34.4 %collective-permute-start.8 = (bf16[256,1024]{1,0:T(8,128)(2,1)S(1)}, bf16[256,1024]{1,0:T(8,128)(2,1)S(1)}, u32[]{:S(2)}, u32[]{:S(2)}) collective-permute-start(bf16[256,1024]{1,0:T(8,128)(2,1)S(1)} %get-tuple-element.98), channel_id=1, source_target_pairs={{0,4},{4,0},{8,12},{12,8},{1,5},{5,1},{9,13},{13,9},{2,6},{6,2},{1... | collective-permute-start | bytes 1572872 | tf_op jit(solution)/shard_map/ppermute | solution.py:20
  7.5 23.7 %collective-permute-start.6 = (bf16[160,1024]{1,0:T(8,128)(2,1)}, bf16[160,1024]{1,0:T(8,128)(2,1)S(1)}, u32[]{:S(2)}, u32[]{:S(2)}) collective-permute-start(bf16[160,1024]{1,0:T(8,128)(2,1)} %get-tuple-element.96), channel_id=1, source_target_pairs={{0,12},{4,8},{8,4},{12,0},{1,13},{5,9},{9,5},{13,1},{2,14},{6,10},... | collective-permute-start | bytes 983048 | tf_op jit(solution)/shard_map/ppermute | solution.py:20
  9.9 28.9 %collective-permute-start.7 = (bf16[160,1024]{1,0:T(8,128)(2,1)S(1)}, bf16[160,1024]{1,0:T(8,128)(2,1)S(1)}, u32[]{:S(2)}, u32[]{:S(2)}) collective-permute-start(bf16[160,1024]{1,0:T(8,128)(2,1)S(1)} %get-tuple-element.97), channel_id=1, source_target_pairs={{0,8},{4,12},{8,0},{12,4},{1,9},{5,13},{9,1},{13,5},{2,10},{6,14},... | collective-permute-start | bytes 983048 | tf_op jit(solution)/shard_map/ppermute | solution.py:20
  38.8 10.6 %collective-permute-start.9 = (bf16[160,1024]{1,0:T(8,128)(2,1)S(1)}, bf16[160,1024]{1,0:T(8,128)(2,1)S(1)}, u32[]{:S(2)}, u32[]{:S(2)}) collective-permute-start(bf16[160,1024]{1,0:T(8,128)(2,1)S(1)} %collective-permute-done.6.refs_5_), channel_id=1, source_target_pairs={{0,16},{16,0},{1,17},{17,1},{2,18},{18,2},{3,19},{19,3},{4,20},{20... | collective-permute-start | bytes 983048 | tf_op jit(solution)/shard_map/ppermute | solution.py:20
  40.3 16.2 %collective-permute-start.10 = (bf16[160,1024]{1,0:T(8,128)(2,1)S(1)}, bf16[160,1024]{1,0:T(8,128)(2,1)S(1)}, u32[]{:S(2)}, u32[]{:S(2)}) collective-permute-start(bf16[160,1024]{1,0:T(8,128)(2,1)S(1)} %collective-permute-done.7.refs_7_), channel_id=1, source_target_pairs={{0,16},{16,0},{1,17},{17,1},{2,18},{18,2},{3,19},{19,3},{4,20},{20... | collective-permute-start | bytes 983048 | tf_op jit(solution)/shard_map/ppermute | solution.py:20
  40.8 41.9 %collective-permute-start.17 = (bf16[256,1024]{1,0:T(8,128)(2,1)S(1)}, bf16[256,1024]{1,0:T(8,128)(2,1)S(1)}, u32[]{:S(2)}, u32[]{:S(2)}) collective-permute-start(bf16[256,1024]{1,0:T(8,128)(2,1)S(1)} %collective-permute-done.8.refs_9_), channel_id=1, source_target_pairs={{0,16},{16,0},{1,17},{17,1},{2,18},{18,2},{3,19},{19,3},{4,20},{20... | collective-permute-start | bytes 1572872 | tf_op jit(solution)/shard_map/ppermute | solution.py:20
  42.4 14.1 %collective-permute-start.11 = (bf16[128,1024]{1,0:T(8,128)(2,1)S(1)}, bf16[128,1024]{1,0:T(8,128)(2,1)S(1)}, u32[]{:S(2)}, u32[]{:S(2)}) collective-permute-start(bf16[128,1024]{1,0:T(8,128)(2,1)S(1)} %get-tuple-element.103), channel_id=1, source_target_pairs={{0,4},{4,0},{8,12},{12,8},{1,5},{5,1},{9,13},{13,9},{2,6},{6,2},{1... | collective-permute-start | bytes 786440 | tf_op jit(solution)/shard_map/ppermute | solution.py:20
  42.4 21.3 %collective-permute-start.12 = (bf16[128,1024]{1,0:T(8,128)(2,1)S(1)}, bf16[128,1024]{1,0:T(8,128)(2,1)S(1)}, u32[]{:S(2)}, u32[]{:S(2)}) collective-permute-start(bf16[128,1024]{1,0:T(8,128)(2,1)S(1)} %get-tuple-element.104), channel_id=1, source_target_pairs={{0,8},{4,12},{8,0},{12,4},{1,9},{5,13},{9,1},{13,5},{2,10},{6,14},... | collective-permute-start | bytes 786440 | tf_op jit(solution)/shard_map/ppermute | solution.py:20
  49.5 14.2 %collective-permute-start.13 = (bf16[128,1024]{1,0:T(8,128)(2,1)S(1)}, bf16[128,1024]{1,0:T(8,128)(2,1)S(1)}, u32[]{:S(2)}, u32[]{:S(2)}) collective-permute-start(bf16[128,1024]{1,0:T(8,128)(2,1)S(1)} %get-tuple-element.105), channel_id=1, source_target_pairs={{0,12},{4,8},{8,4},{12,0},{1,13},{5,9},{9,5},{13,1},{2,14},{6,10},... | collective-permute-start | bytes 786440 | tf_op jit(solution)/shard_map/ppermute | solution.py:20
  64.5 23.6 %collective-permute-start.19 = (bf16[128,1024]{1,0:T(8,128)(2,1)S(1)}, bf16[128,1024]{1,0:T(8,128)(2,1)S(1)}, u32[]{:S(2)}, u32[]{:S(2)}) collective-permute-start(bf16[128,1024]{1,0:T(8,128)(2,1)S(1)} %get-tuple-element.112.refs_0_.refs_15_.fresh_ref), channel_id=1, source_target_pairs={{0,4},{4,0},{8,12},{12,8},{1,5},{5,1},{9,13},{13,9},{2,6},{6,2},{1... | collective-permute-start | bytes 786440 | tf_op jit(solution)/shard_map/ppermute | solution.py:20
  68.0 12.3 %collective-permute-start.14 = (bf16[128,512]{1,0:T(8,128)(2,1)S(1)}, bf16[128,512]{1,0:T(8,128)(2,1)S(1)}, u32[]{:S(2)}, u32[]{:S(2)}) collective-permute-start(bf16[128,512]{1,0:T(8,128)(2,1)S(1)} %get-tuple-element.106), channel_id=1, source_target_pairs={{0,12},{4,8},{8,4},{12,0},{1,13},{5,9},{9,5},{13,1},{2,14},{6,10},... | collective-permute-start | bytes 393224 | tf_op jit(solution)/shard_map/ppermute | solution.py:20
  70.3 12.5 %collective-permute-start.16 = (bf16[128,512]{1,0:T(8,128)(2,1)S(1)}, bf16[128,512]{1,0:T(8,128)(2,1)S(1)}, u32[]{:S(2)}, u32[]{:S(2)}) collective-permute-start(bf16[128,512]{1,0:T(8,128)(2,1)S(1)} %get-tuple-element.107), channel_id=1, source_target_pairs={{0,12},{4,8},{8,4},{12,0},{1,13},{5,9},{9,5},{13,1},{2,14},{6,10},... | collective-permute-start | bytes 393224 | tf_op jit(solution)/shard_map/ppermute | solution.py:20
  80.3 9.5 %collective-permute-start.15 = (bf16[128,512]{1,0:T(8,128)(2,1)S(1)}, bf16[128,512]{1,0:T(8,128)(2,1)S(1)}, u32[]{:S(2)}, u32[]{:S(2)}) collective-permute-start(bf16[128,512]{1,0:T(8,128)(2,1)S(1)} %collective-permute-done.14.refs_2_), channel_id=1, source_target_pairs={{0,4},{4,0},{8,12},{12,8},{1,5},{5,1},{9,13},{13,9},{2,6},{6,2},{1... | collective-permute-start | bytes 393224 | tf_op jit(solution)/shard_map/ppermute | solution.py:20
  84.5 17.9 %collective-permute-start.29 = (bf16[96,1024]{1,0:T(8,128)(2,1)S(1)}, bf16[96,1024]{1,0:T(8,128)(2,1)S(1)}, u32[]{:S(2)}, u32[]{:S(2)}) collective-permute-start(bf16[96,1024]{1,0:T(8,128)(2,1)S(1)} %copy-done.9), channel_id=1, source_target_pairs={{0,12},{4,8},{8,4},{12,0},{1,13},{5,9},{9,5},{13,1},{2,14},{6,10},... | collective-permute-start | bytes 589832 | tf_op jit(solution)/shard_map/ppermute | solution.py:20
  85.9 17.0 %collective-permute-start.31 = (bf16[96,1024]{1,0:T(8,128)(2,1)S(1)}, bf16[96,1024]{1,0:T(8,128)(2,1)S(1)}, u32[]{:S(2)}, u32[]{:S(2)}) collective-permute-start(bf16[96,1024]{1,0:T(8,128)(2,1)S(1)} %get-tuple-element.125), channel_id=1, source_target_pairs={{0,8},{4,12},{8,0},{12,4},{1,9},{5,13},{9,1},{13,5},{2,10},{6,14},... | collective-permute-start | bytes 589832 | tf_op jit(solution)/shard_map/ppermute | solution.py:20
  102.4 11.1 %collective-permute-start.30 = (bf16[96,1024]{1,0:T(8,128)(2,1)S(1)}, bf16[96,1024]{1,0:T(8,128)(2,1)S(1)}, u32[]{:S(2)}, u32[]{:S(2)}) collective-permute-start(bf16[96,1024]{1,0:T(8,128)(2,1)S(1)} %collective-permute-done.29.refs_11_), channel_id=1, source_target_pairs={{0,16},{16,0},{1,17},{17,1},{2,18},{18,2},{3,19},{19,3},{4,20},{20... | collective-permute-start | bytes 589832 | tf_op jit(solution)/shard_map/ppermute | solution.py:20
  102.9 10.6 %collective-permute-start.32 = (bf16[96,1024]{1,0:T(8,128)(2,1)S(1)}, bf16[96,1024]{1,0:T(8,128)(2,1)S(1)}, u32[]{:S(2)}, u32[]{:S(2)}) collective-permute-start(bf16[96,1024]{1,0:T(8,128)(2,1)S(1)} %collective-permute-done.31.refs_13_), channel_id=1, source_target_pairs={{0,16},{16,0},{1,17},{17,1},{2,18},{18,2},{3,19},{19,3},{4,20},{20... | collective-permute-start | bytes 589832 | tf_op jit(solution)/shard_map/ppermute | solution.py:20
  115.1 15.8 %collective-permute-start.37 = (bf16[128,1024]{1,0:T(8,128)(2,1)S(1)}, bf16[128,1024]{1,0:T(8,128)(2,1)S(1)}, u32[]{:S(2)}, u32[]{:S(2)}) collective-permute-start(bf16[128,1024]{1,0:T(8,128)(2,1)S(1)} %get-tuple-element.128.refs_0_.refs_5_.fresh_ref), channel_id=1, source_target_pairs={{0,4},{4,0},{8,12},{12,8},{1,5},{5,1},{9,13},{13,9},{2,6},{6,2},{1... | collective-permute-start | bytes 786440 | tf_op jit(solution)/shard_map/ppermute | solution.py:20
  116.1 11.4 %collective-permute-start.33 = (bf16[128,512]{1,0:T(8,128)(2,1)S(1)}, bf16[128,512]{1,0:T(8,128)(2,1)S(1)}, u32[]{:S(2)}, u32[]{:S(2)}) collective-permute-start(bf16[128,512]{1,0:T(8,128)(2,1)S(1)} %get-tuple-element.126), channel_id=1, source_target_pairs={{0,12},{4,8},{8,4},{12,0},{1,13},{5,9},{9,5},{13,1},{2,14},{6,10},... | collective-permute-start | bytes 393224 | tf_op jit(solution)/shard_map/ppermute | solution.py:20
  117.5 12.1 %collective-permute-start.35 = (bf16[128,512]{1,0:T(8,128)(2,1)S(1)}, bf16[128,512]{1,0:T(8,128)(2,1)S(1)}, u32[]{:S(2)}, u32[]{:S(2)}) collective-permute-start(bf16[128,512]{1,0:T(8,128)(2,1)S(1)} %get-tuple-element.127), channel_id=1, source_target_pairs={{0,12},{4,8},{8,4},{12,0},{1,13},{5,9},{9,5},{13,1},{2,14},{6,10},... | collective-permute-start | bytes 393224 | tf_op jit(solution)/shard_map/ppermute | solution.py:20
  159.3 16.3 %collective-permute-start.51 = (bf16[128,1024]{1,0:T(8,128)(2,1)S(1)}, bf16[128,1024]{1,0:T(8,128)(2,1)S(1)}, u32[]{:S(2)}, u32[]{:S(2)}) collective-permute-start(bf16[128,1024]{1,0:T(8,128)(2,1)S(1)} %get-tuple-element.139.refs_0_.fresh_ref.refs_5_), channel_id=1, source_target_pairs={{0,4},{4,0},{8,12},{12,8},{1,5},{5,1},{9,13},{13,9},{2,6},{6,2},{1... | collective-permute-start | bytes 786440 | tf_op jit(solution)/shard_map/ppermute | solution.py:20
  160.6 12.3 %collective-permute-start.47 = (bf16[128,512]{1,0:T(8,128)(2,1)S(1)}, bf16[128,512]{1,0:T(8,128)(2,1)S(1)}, u32[]{:S(2)}, u32[]{:S(2)}) collective-permute-start(bf16[128,512]{1,0:T(8,128)(2,1)S(1)} %get-tuple-element.137), channel_id=1, source_target_pairs={{0,12},{4,8},{8,4},{12,0},{1,13},{5,9},{9,5},{13,1},{2,14},{6,10},... | collective-permute-start | bytes 393224 | tf_op jit(solution)/shard_map/ppermute | solution.py:20
  162.9 12.7 %collective-permute-start.49 = (bf16[128,512]{1,0:T(8,128)(2,1)S(1)}, bf16[128,512]{1,0:T(8,128)(2,1)S(1)}, u32[]{:S(2)}, u32[]{:S(2)}) collective-permute-start(bf16[128,512]{1,0:T(8,128)(2,1)S(1)} %get-tuple-element.138), channel_id=1, source_target_pairs={{0,12},{4,8},{8,4},{12,0},{1,13},{5,9},{9,5},{13,1},{2,14},{6,10},... | collective-permute-start | bytes 393224 | tf_op jit(solution)/shard_map/ppermute | solution.py:20
  196.3 7.8 %collective-permute-start.59 = (bf16[32,2048]{1,0:T(8,128)(2,1)S(1)}, bf16[32,2048]{1,0:T(8,128)(2,1)S(1)}, u32[]{:S(2)}, u32[]{:S(2)}) collective-permute-start(bf16[32,2048]{1,0:T(8,128)(2,1)S(1)} %constant_dynamic-update-slice_fusion.8.refs_0_), channel_id=1, source_target_pairs={{0,2},{1,3},{2,0},{3,1},{4,6},{5,7},{6,4},{7,5},{8,10},{9,11},{10,... | collective-permute-start | bytes 393224 | tf_op jit(solution)/shard_map/ppermute | solution.py:20
  (49 other events, 377.2 us)

commit v5 on v4

--- a/solution.py
+++ b/solution.py
@@ -63,10 +63,10 @@
             num_scalar_prefetch=1,
             grid=(1,),
             in_specs=[pl.BlockSpec(memory_space=pltpu.HBM)],
-            out_specs=[pl.BlockSpec(memory_space=pl.ANY) for _ in shapes],
+            out_specs=[pl.BlockSpec(memory_space=pltpu.VMEM) for _ in shapes],
             scratch_shapes=[pltpu.SemaphoreType.DMA((len(shapes),))],
         ),
-        out_shape=[jax.ShapeDtypeStruct(shape, w_out.dtype) for shape in shapes],
+        out_shape=[pltpu.VMEM(shape, w_out.dtype) for shape in shapes],
         compiler_params=pltpu.CompilerParams(vmem_limit_bytes=VMEM_BYTES),
         name="cut",
     )(info, w_out)
@@ -407,6 +407,22 @@
     )(info, *operands)
 
 
+def add_kernel(first_ref, second_ref, out_ref):
+    total = first_ref[...].astype(jnp.float32) + second_ref[...].astype(jnp.float32)
+    out_ref[...] = total.astype(jnp.bfloat16)
+
+
+def add(first, second):
+    return pl.pallas_call(
+        add_kernel,
+        in_specs=[pl.BlockSpec(memory_space=pltpu.VMEM)] * 2,
+        out_specs=pl.BlockSpec(memory_space=pltpu.VMEM),
+        out_shape=jax.ShapeDtypeStruct(first.shape, first.dtype),
+        compiler_params=pltpu.CompilerParams(vmem_limit_bytes=VMEM_BYTES),
+        name="add",
+    )(first, second)
+
+
 def combine_kernel(level, batch, dp, info_ref, index_ref, *refs):
     terms, (feature_ref, embed_ref, *out_refs) = refs[:-5], refs[-5:]
     share = out_refs[0].shape[1]
@@ -642,13 +658,13 @@
     info = jnp.stack(info)
 
     if by_swaps:
-        early = half * 5 // 8
-        plan = ((0, 0, head_rows), (3, 0, early), (2, 0, early), (1, 0, half))
-        plan += ((3, early, half - early), (2, early, half - early))
-        cuts = cut(info, w_out, plan, share_cols, dp)
+        chunk = half * 3 // 8
+        plan = ((3, 0, half), (1, 0, half), (2, 0, chunk), (2, chunk, half - chunk))
+        plan += ((0, 0, head_rows),)
+        source = pltpu.with_memory_space_constraint(w_out, pltpu.HBM)
+        cuts = cut(info, source, plan[:3], share_cols, dp)
         info, *cuts = lax.optimization_barrier((info, *cuts))
-        weights = [(cuts[0], 0, None)]
-        moved = [swap(sent, "tensor", step) for sent, (step, _, _) in zip(cuts[1:4], plan[1:4])]
+        moved = [swap(sent, "tensor", step) for sent, (step, _, _) in zip(cuts, plan)]
     else:
         spread = lax.all_to_all(w_out, "tensor", 1, 0, tiled=True)
         weights = [(load(info, spread), 0, None)]
@@ -690,6 +706,12 @@
                 sums = project(
                     level, batch, places, cols, info, index, pieces, *fixed, None, True
                 )
+            sums = list(sums)
+            if by_swaps and level == 0 and batch + 1 == batches:
+                sums[0], later = lax.optimization_barrier((sums[0], info))
+                cuts = list(cut(later, source, plan[3:], share_cols, dp))
+                weights = [(cuts[1], 0, None)]
+                sums[0], cuts[0] = lax.optimization_barrier((sums[0], cuts[0]))
             parts = [sums[0]] + [swap(sums[step], "dp", step) for step in range(1, dp)]
             mixed, fresh = attend(
                 batch,
@@ -722,13 +744,17 @@
             index = chosen[batch][level]
             if by_swaps and level == 0:
                 terms = list(partial(info, attended[batch], w_out, tensor))
-                sent = terms[1:]
+                own, near, other, far = terms
+                other = swap(other, "tensor", 1)
                 if batch + 1 == batches:
-                    terms[0], *moved = lax.optimization_barrier((terms[0], *moved))
-                    others = [swap(x, "groups", 1) for x in moved]
-                terms = terms[:1] + [swap(x, "tensor", step) for step, x in enumerate(sent, 1)]
+                    own, *moved[:2] = lax.optimization_barrier((own, *moved[:2]))
+                    others = [swap(x, "groups", 1) for x in moved[:2]]
                 if batch + 1 == batches:
-                    terms[0], *others[:2] = lax.optimization_barrier((terms[0], *others[:2]))
+                    far, moved[2] = lax.optimization_barrier((far, moved[2]))
+                far = swap(add(far, other), "tensor", 3)
+                near = swap(near, "tensor", 1)
+                own, *chosen[batch][1:] = lax.optimization_barrier((own, *chosen[batch][1:]))
+                terms = [own, near, far]
                 shares[batch], *split = combine(
                     level, batch, info, index, terms, shares[batch], embeds
                 )
@@ -758,19 +784,22 @@
             own = shares[batch]
             if by_swaps:
                 far, other = (swap(x, "tensor", 3) for x in split)
-                if level == 0 and batch + 1 == batches:
-                    other, others[2], *cuts[4:] = lax.optimization_barrier(
-                        (other, others[2], *cuts[4:])
+                first = level == 0 and batch + 1 == batches
+                if first:
+                    far, other, moved[2], *others = lax.optimization_barrier(
+                        (far, other, moved[2], *others)
                     )
-                    for sent, (step, _, _) in zip(cuts[4:], plan[4:]):
-                        moved.append(swap(sent, "tensor", step))
-                    others += [swap(x, "groups", 1) for x in moved[3:]]
-                    for (step, start, _), one, two in zip(plan[1:], moved, others):
+                    others.append(swap(moved[2], "groups", 1))
+                near = swap(own, "tensor", 1)
+                last = [swap(far, "tensor", 1), swap(other, "tensor", 1)]
+                if first:
+                    *last, cuts[0] = lax.optimization_barrier((*last, cuts[0]))
+                    moved.append(swap(cuts[0], "tensor", 2))
+                    others.append(swap(moved[3], "groups", 1))
+                    for (step, start, _), one, two in zip(plan, moved, others):
                         weights.append((one, step * head_rows + start, 0))
                         weights.append((two, step * head_rows + start, 1))
-                near = swap(own, "tensor", 1)
-                gathered[batch] = [own, near, far, other]
-                gathered[batch] += [swap(far, "tensor", 1), swap(other, "tensor", 1)]
+                gathered[batch] = [own, near, far, other, *last]
             else:
                 gathered[batch] = [lax.all_gather(own, "tensor", axis=1, tiled=True)]
     return held.reshape(requests, depths, branch, share_cols)

time: 207 us -> 195 us (0.942)
  waiting for transfers between devices: 97.4 us -> 88.3 us
  local copies, waits for them, and re-layouts: 7.36 us -> 4.45 us
  starting transfers between devices: 69.4 us -> 67.1 us
  Pallas kernels: 31.7 us -> 34 us
    ppermute x61 -> x59, waiting for transfers between devices: 97.4 us -> 88.3 us  [swap(): return lax.ppermute(x, axis, [(i, i ^ step) for i in range(size)])]
    unnamed x35 -> x29, local copies, waits for them, and re-layouts: 7.25 us -> 4.34 us
    ppermute x61 -> x59, starting transfers between devices: 69.4 us -> 67.1 us  [swap(): return lax.ppermute(x, axis, [(i, i ^ step) for i in range(size)])]
    pallas_call x1 -> x2, Pallas kernels: 1.47 us -> 3.71 us  [cut(): pl.pallas_call(functools.partial(cut_kernel, plan, dp), grid_spec=pltpu.P...]
  transfers between devices with their start and end apart: 61 -> 59, of which waited for: 34 -> 37; matrix products, arithmetic and copies ran while one was open for 1% -> 1% of each run, Pallas kernels for 10% -> 11%
where the time goes in v5:
time: 195 us; the launch traced here: 194 us
  waiting for transfers between devices  88.3 us (45%)
  starting transfers between devices  67.1 us (34%)
  Pallas kernels  34 us (17%)
  local copies, waits for them, and re-layouts  4.45 us (2%)
    ppermute x59, waiting for transfers between devices, swap(): return lax.ppermute(x, axis, [(i, i ^ step) for i in range(size)])  88.3 us
    ppermute x59, starting transfers between devices, swap(): return lax.ppermute(x, axis, [(i, i ^ step) for i in range(size)])  67.1 us
    pallas_call x7, Pallas kernels, project(): pl.pallas_call(functools.partial(project_kernel, level, batch, places, sh...  10.8 us
    pallas_call x4, Pallas kernels, attend(): pl.pallas_call(functools.partial(attend_kernel, len(parts), len(earlier),...  5.77 us
    pallas_call x3, Pallas kernels, output(): pl.pallas_call(functools.partial(output_kernel, level, batch, dp, places,...  4.97 us
    unnamed x29, local copies, waits for them, and re-layouts  4.34 us
  transfers between devices with their start and end apart: 59, of which 37 were waited for; matrix products, arithmetic and copies ran while one was open for 1% of the time, Pallas kernels for 11%

profile of v5, /device:TPU:0, one launch (start us, length us, event | category | flops | bytes accessed | tf_op | source)
XLA Modules:
  0.0 194.4 jit_solution(13648480465394839551)
XLA Ops:
  1.9 5.1 %collective-permute-start.6 = (bf16[256,1024]{1,0:T(8,128)(2,1)S(1)}, bf16[256,1024]{1,0:T(8,128)(2,1)S(1)}, u32[]{:S(2)}, u32[]{:S(2)}) collective-permute-start(bf16[256,1024]{1,0:T(8,128)(2,1)S(1)} %get-tuple-element.99), channel_id=1, source_target_pairs={{0,12},{4,8},{8,4},{12,0},{1,13},{5,9},{9,5},{13,1},{2,14},{6,10},... | collective-permute-start | bytes 1572872 | tf_op jit(solution)/shard_map/ppermute | solution.py:20
  34.0 7.2 %collective-permute-done.9.refs_9_ = bf16[96,1024]{1,0:T(8,128)(2,1)S(1)} collective-permute-done((bf16[96,1024]{1,0:T(8,128)(2,1)S(1)}, bf16[96,1024]{1,0:T(8,128)(2,1)S(1)}, u32[]{:S(2)}, u32[]{:S(2)}) %collective-permute-start.9) | collective-permute-done | bytes 196640 | tf_op jit(solution)/shard_map/ppermute | solution.py:20
  44.7 2.8 %collective-permute-done.8.refs_1_ = bf16[128,1024]{1,0:T(8,128)(2,1)S(1)} collective-permute-done((bf16[128,1024]{1,0:T(8,128)(2,1)S(1)}, bf16[128,1024]{1,0:T(8,128)(2,1)S(1)}, u32[]{:S(2)}, u32[]{:S(2)}) %collective-permute-start.8) | collective-permute-done | bytes 262176 | tf_op jit(solution)/shard_map/ppermute | solution.py:20
  47.5 3.9 %collective-permute-done.11.refs_2_ = bf16[128,1024]{1,0:T(8,128)(2,1)S(1)} collective-permute-done((bf16[128,1024]{1,0:T(8,128)(2,1)S(1)}, bf16[128,1024]{1,0:T(8,128)(2,1)S(1)}, u32[]{:S(2)}, u32[]{:S(2)}) %collective-permute-start.11) | collective-permute-done | bytes 262176 | tf_op jit(solution)/shard_map/ppermute | solution.py:20
  52.3 2.7 %collective-permute-start.18 = (bf16[128,1024]{1,0:T(8,128)(2,1)S(1)}, bf16[128,1024]{1,0:T(8,128)(2,1)S(1)}, u32[]{:S(2)}, u32[]{:S(2)}) collective-permute-start(bf16[128,1024]{1,0:T(8,128)(2,1)S(1)} %get-tuple-element.125.refs_0_.refs_13_.fresh_ref), channel_id=1, source_target_pairs={{0,4},{4,0},{8,12},{12,8},{1,5},{5,1},{9,13},{13,9},{2,6},{6,2},{1... | collective-permute-start | bytes 786440 | tf_op jit(solution)/shard_map/ppermute | solution.py:20
  55.0 3.2 %collective-permute-start.12 = (bf16[128,512]{1,0:T(8,128)(2,1)S(1)}, bf16[128,512]{1,0:T(8,128)(2,1)S(1)}, u32[]{:S(2)}, u32[]{:S(2)}) collective-permute-start(bf16[128,512]{1,0:T(8,128)(2,1)S(1)} %get-tuple-element.115), channel_id=1, source_target_pairs={{0,12},{4,8},{8,4},{12,0},{1,13},{5,9},{9,5},{13,1},{2,14},{6,10},... | collective-permute-start | bytes 393224 | tf_op jit(solution)/shard_map/ppermute | solution.py:20
  58.8 6.1 %collective-permute-done.12.refs_2_ = bf16[128,512]{1,0:T(8,128)(2,1)S(1)} collective-permute-done((bf16[128,512]{1,0:T(8,128)(2,1)S(1)}, bf16[128,512]{1,0:T(8,128)(2,1)S(1)}, u32[]{:S(2)}, u32[]{:S(2)}) %collective-permute-start.12) | collective-permute-done | bytes 131104 | tf_op jit(solution)/shard_map/ppermute | solution.py:20
  72.7 2.9 %collective-permute-start.29 = (bf16[160,1024]{1,0:T(8,128)(2,1)S(1)}, bf16[160,1024]{1,0:T(8,128)(2,1)S(1)}, u32[]{:S(2)}, u32[]{:S(2)}) collective-permute-start(bf16[160,1024]{1,0:T(8,128)(2,1)S(1)} %get-tuple-element.137), channel_id=1, source_target_pairs={{0,8},{4,12},{8,0},{12,4},{1,9},{5,13},{9,1},{13,5},{2,10},{6,14},... | collective-permute-start | bytes 983048 | tf_op jit(solution)/shard_map/ppermute | solution.py:20
  86.1 2.7 %collective-permute-start.22 = (bf16[32,512]{1,0:T(8,128)(2,1)S(1)}, bf16[32,512]{1,0:T(8,128)(2,1)S(1)}, u32[]{:S(2)}, u32[]{:S(2)}) collective-permute-start(bf16[32,512]{1,0:T(8,128)(2,1)S(1)} %get-tuple-element.132), channel_id=1, source_target_pairs={{0,4},{4,0},{8,12},{12,8},{1,5},{5,1},{9,13},{13,9},{2,6},{6,2},{1... | collective-permute-start | bytes 98312 | tf_op jit(solution)/shard_map/ppermute | solution.py:20
  94.5 3.6 %collective-permute-done.27.refs_3_ = bf16[32,2048]{1,0:T(8,128)(2,1)S(1)} collective-permute-done((bf16[32,2048]{1,0:T(8,128)(2,1)S(1)}, bf16[32,2048]{1,0:T(8,128)(2,1)S(1)}, u32[]{:S(2)}, u32[]{:S(2)}) %collective-permute-start.27) | collective-permute-done | bytes 131104 | tf_op jit(solution)/shard_map/ppermute | solution.py:20
  98.1 3.1 %collective-permute-done.26.refs_2_ = bf16[32,2048]{1,0:T(8,128)(2,1)S(1)} collective-permute-done((bf16[32,2048]{1,0:T(8,128)(2,1)S(1)}, bf16[32,2048]{1,0:T(8,128)(2,1)S(1)}, u32[]{:S(2)}, u32[]{:S(2)}) %collective-permute-start.26) | collective-permute-done | bytes 131104 | tf_op jit(solution)/shard_map/ppermute | solution.py:20
  105.4 2.6 %collective-permute-start.33 = (bf16[128,512]{1,0:T(8,128)(2,1)S(1)}, bf16[128,512]{1,0:T(8,128)(2,1)S(1)}, u32[]{:S(2)}, u32[]{:S(2)}) collective-permute-start(bf16[128,512]{1,0:T(8,128)(2,1)S(1)} %get-tuple-element.139), channel_id=1, source_target_pairs={{0,12},{4,8},{8,4},{12,0},{1,13},{5,9},{9,5},{13,1},{2,14},{6,10},... | collective-permute-start | bytes 393224 | tf_op jit(solution)/shard_map/ppermute | solution.py:20
  108.0 7.5 %collective-permute-done.31.refs_2_ = bf16[128,512]{1,0:T(8,128)(2,1)S(1)} collective-permute-done((bf16[128,512]{1,0:T(8,128)(2,1)S(1)}, bf16[128,512]{1,0:T(8,128)(2,1)S(1)}, u32[]{:S(2)}, u32[]{:S(2)}) %collective-permute-start.31) | collective-permute-done | bytes 131104 | tf_op jit(solution)/shard_map/ppermute | solution.py:20
  126.3 2.9 %collective-permute-done.37.refs_2_ = bf16[32,896]{1,0:T(8,128)(2,1)S(1)} collective-permute-done((bf16[32,896]{1,0:T(8,128)(2,1)S(1)}, bf16[32,896]{1,0:T(8,128)(2,1)S(1)}, u32[]{:S(2)}, u32[]{:S(2)}) %collective-permute-start.37) | collective-permute-done | bytes 57376 | tf_op jit(solution)/shard_map/ppermute | solution.py:20
  131.1 2.5 %collective-permute-start.41 = (bf16[32,512]{1,0:T(8,128)(2,1)S(1)}, bf16[32,512]{1,0:T(8,128)(2,1)S(1)}, u32[]{:S(2)}, u32[]{:S(2)}) collective-permute-start(bf16[32,512]{1,0:T(8,128)(2,1)S(1)} %get-tuple-element.147), channel_id=1, source_target_pairs={{0,12},{4,8},{8,4},{12,0},{1,13},{5,9},{9,5},{13,1},{2,14},{6,10},... | collective-permute-start | bytes 98312 | tf_op jit(solution)/shard_map/ppermute | solution.py:20
  135.6 2.3 %collective-permute-done.39 = bf16[32,512]{1,0:T(8,128)(2,1)S(1)} collective-permute-done((bf16[32,512]{1,0:T(8,128)(2,1)S(1)}, bf16[32,512]{1,0:T(8,128)(2,1)S(1)}, u32[]{:S(2)}, u32[]{:S(2)}) %collective-permute-start.39) | collective-permute-done | bytes 32800 | tf_op jit(solution)/shard_map/ppermute | solution.py:20
  140.4 3.9 %collective-permute-done.44.refs_3_ = bf16[32,2048]{1,0:T(8,128)(2,1)S(1)} collective-permute-done((bf16[32,2048]{1,0:T(8,128)(2,1)S(1)}, bf16[32,2048]{1,0:T(8,128)(2,1)S(1)}, u32[]{:S(2)}, u32[]{:S(2)}) %collective-permute-start.44) | collective-permute-done | bytes 131104 | tf_op jit(solution)/shard_map/ppermute | solution.py:20
  148.5 2.5 %collective-permute-start.45 = (bf16[128,512]{1,0:T(8,128)(2,1)S(1)}, bf16[128,512]{1,0:T(8,128)(2,1)S(1)}, u32[]{:S(2)}, u32[]{:S(2)}) collective-permute-start(bf16[128,512]{1,0:T(8,128)(2,1)S(1)} %get-tuple-element.149), channel_id=1, source_target_pairs={{0,12},{4,8},{8,4},{12,0},{1,13},{5,9},{9,5},{13,1},{2,14},{6,10},... | collective-permute-start | bytes 393224 | tf_op jit(solution)/shard_map/ppermute | solution.py:20
  152.3 8.6 %collective-permute-done.45.refs_2_ = bf16[128,512]{1,0:T(8,128)(2,1)S(1)} collective-permute-done((bf16[128,512]{1,0:T(8,128)(2,1)S(1)}, bf16[128,512]{1,0:T(8,128)(2,1)S(1)}, u32[]{:S(2)}, u32[]{:S(2)}) %collective-permute-start.45) | collective-permute-done | bytes 131104 | tf_op jit(solution)/shard_map/ppermute | solution.py:20
  160.9 2.8 %collective-permute-done.47.refs_3_ = bf16[128,512]{1,0:T(8,128)(2,1)S(1)} collective-permute-done((bf16[128,512]{1,0:T(8,128)(2,1)S(1)}, bf16[128,512]{1,0:T(8,128)(2,1)S(1)}, u32[]{:S(2)}, u32[]{:S(2)}) %collective-permute-start.47) | collective-permute-done | bytes 131104 | tf_op jit(solution)/shard_map/ppermute | solution.py:20
  171.8 2.5 %collective-permute-done.51.refs_2_ = bf16[32,896]{1,0:T(8,128)(2,1)S(1)} collective-permute-done((bf16[32,896]{1,0:T(8,128)(2,1)S(1)}, bf16[32,896]{1,0:T(8,128)(2,1)S(1)}, u32[]{:S(2)}, u32[]{:S(2)}) %collective-permute-start.51) | collective-permute-done | bytes 57376 | tf_op jit(solution)/shard_map/ppermute | solution.py:20
  178.2 2.9 %collective-permute-start.53 = (bf16[32,512]{1,0:T(8,128)(2,1)S(1)}, bf16[32,512]{1,0:T(8,128)(2,1)S(1)}, u32[]{:S(2)}, u32[]{:S(2)}) collective-permute-start(bf16[32,512]{1,0:T(8,128)(2,1)S(1)} %get-tuple-element.158), channel_id=1, source_target_pairs={{0,4},{4,0},{8,12},{12,8},{1,5},{5,1},{9,13},{13,9},{2,6},{6,2},{1... | collective-permute-start | bytes 98312 | tf_op jit(solution)/shard_map/ppermute | solution.py:20
  181.1 2.5 %collective-permute-done.53 = bf16[32,512]{1,0:T(8,128)(2,1)S(1)} collective-permute-done((bf16[32,512]{1,0:T(8,128)(2,1)S(1)}, bf16[32,512]{1,0:T(8,128)(2,1)S(1)}, u32[]{:S(2)}, u32[]{:S(2)}) %collective-permute-start.53) | collective-permute-done | bytes 32800 | tf_op jit(solution)/shard_map/ppermute | solution.py:20
  189.4 2.7 %collective-permute-done.57.refs_2_ = bf16[32,2048]{1,0:T(8,128)(2,1)S(1)} collective-permute-done((bf16[32,2048]{1,0:T(8,128)(2,1)S(1)}, bf16[32,2048]{1,0:T(8,128)(2,1)S(1)}, u32[]{:S(2)}, u32[]{:S(2)}) %collective-permute-start.57) | collective-permute-done | bytes 131104 | tf_op jit(solution)/shard_map/ppermute | solution.py:20
  (152 shorter events, 104.4 us)
Async XLA Ops:
  1.9 28.3 %collective-permute-start.6 = (bf16[256,1024]{1,0:T(8,128)(2,1)S(1)}, bf16[256,1024]{1,0:T(8,128)(2,1)S(1)}, u32[]{:S(2)}, u32[]{:S(2)}) collective-permute-start(bf16[256,1024]{1,0:T(8,128)(2,1)S(1)} %get-tuple-element.99), channel_id=1, source_target_pairs={{0,12},{4,8},{8,4},{12,0},{1,13},{5,9},{9,5},{13,1},{2,14},{6,10},... | collective-permute-start | bytes 1572872 | tf_op jit(solution)/shard_map/ppermute | solution.py:20
  7.0 23.3 %collective-permute-start.7 = (bf16[256,1024]{1,0:T(8,128)(2,1)S(1)}, bf16[256,1024]{1,0:T(8,128)(2,1)S(1)}, u32[]{:S(2)}, u32[]{:S(2)}) collective-permute-start(bf16[256,1024]{1,0:T(8,128)(2,1)S(1)} %get-tuple-element.100), channel_id=1, source_target_pairs={{0,4},{4,0},{8,12},{12,8},{1,5},{5,1},{9,13},{13,9},{2,6},{6,2},{1... | collective-permute-start | bytes 1572872 | tf_op jit(solution)/shard_map/ppermute | solution.py:20
  28.1 13.5 %collective-permute-start.10 = (bf16[128,1024]{1,0:T(8,128)(2,1)S(1)}, bf16[128,1024]{1,0:T(8,128)(2,1)S(1)}, u32[]{:S(2)}, u32[]{:S(2)}) collective-permute-start(bf16[128,1024]{1,0:T(8,128)(2,1)S(1)} %get-tuple-element.114), channel_id=1, source_target_pairs={{0,4},{4,0},{8,12},{12,8},{1,5},{5,1},{9,13},{13,9},{2,6},{6,2},{1... | collective-permute-start | bytes 786440 | tf_op jit(solution)/shard_map/ppermute | solution.py:20
  30.2 11.0 %collective-permute-start.9 = (bf16[96,1024]{1,0:T(8,128)(2,1)S(1)}, bf16[96,1024]{1,0:T(8,128)(2,1)S(1)}, u32[]{:S(2)}, u32[]{:S(2)}) collective-permute-start(bf16[96,1024]{1,0:T(8,128)(2,1)S(1)} %get-tuple-element.112), channel_id=1, source_target_pairs={{0,8},{4,12},{8,0},{12,4},{1,9},{5,13},{9,1},{13,5},{2,10},{6,14},... | collective-permute-start | bytes 589832 | tf_op jit(solution)/shard_map/ppermute | solution.py:20
  30.3 36.0 %collective-permute-start.14 = (bf16[256,1024]{1,0:T(8,128)(2,1)S(1)}, bf16[256,1024]{1,0:T(8,128)(2,1)S(1)}, u32[]{:S(2)}, u32[]{:S(2)}) collective-permute-start(bf16[256,1024]{1,0:T(8,128)(2,1)S(1)} %collective-permute-done.6.refs_5_), channel_id=1, source_target_pairs={{0,16},{16,0},{1,17},{17,1},{2,18},{18,2},{3,19},{19,3},{4,20},{20... | collective-permute-start | bytes 1572872 | tf_op jit(solution)/shard_map/ppermute | solution.py:20
  31.8 34.5 %collective-permute-start.15 = (bf16[256,1024]{1,0:T(8,128)(2,1)S(1)}, bf16[256,1024]{1,0:T(8,128)(2,1)S(1)}, u32[]{:S(2)}, u32[]{:S(2)}) collective-permute-start(bf16[256,1024]{1,0:T(8,128)(2,1)S(1)} %collective-permute-done.7.refs_7_), channel_id=1, source_target_pairs={{0,16},{16,0},{1,17},{17,1},{2,18},{18,2},{3,19},{19,3},{4,20},{20... | collective-permute-start | bytes 1572872 | tf_op jit(solution)/shard_map/ppermute | solution.py:20
  32.3 15.2 %collective-permute-start.8 = (bf16[128,1024]{1,0:T(8,128)(2,1)S(1)}, bf16[128,1024]{1,0:T(8,128)(2,1)S(1)}, u32[]{:S(2)}, u32[]{:S(2)}) collective-permute-start(bf16[128,1024]{1,0:T(8,128)(2,1)S(1)} %get-tuple-element.110), channel_id=1, source_target_pairs={{0,4},{4,0},{8,12},{12,8},{1,5},{5,1},{9,13},{13,9},{2,6},{6,2},{1... | collective-permute-start | bytes 786440 | tf_op jit(solution)/shard_map/ppermute | solution.py:20
  41.7 9.7 %collective-permute-start.11 = (bf16[128,1024]{1,0:T(8,128)(2,1)S(1)}, bf16[128,1024]{1,0:T(8,128)(2,1)S(1)}, u32[]{:S(2)}, u32[]{:S(2)}) collective-permute-start(bf16[128,1024]{1,0:T(8,128)(2,1)S(1)} %add.1), channel_id=1, source_target_pairs={{0,12},{4,8},{8,4},{12,0},{1,13},{5,9},{9,5},{13,1},{2,14},{6,10},... | collective-permute-start | bytes 786440 | tf_op jit(solution)/shard_map/ppermute | solution.py:20
  52.3 16.1 %collective-permute-start.18 = (bf16[128,1024]{1,0:T(8,128)(2,1)S(1)}, bf16[128,1024]{1,0:T(8,128)(2,1)S(1)}, u32[]{:S(2)}, u32[]{:S(2)}) collective-permute-start(bf16[128,1024]{1,0:T(8,128)(2,1)S(1)} %get-tuple-element.125.refs_0_.refs_13_.fresh_ref), channel_id=1, source_target_pairs={{0,4},{4,0},{8,12},{12,8},{1,5},{5,1},{9,13},{13,9},{2,6},{6,2},{1... | collective-permute-start | bytes 786440 | tf_op jit(solution)/shard_map/ppermute | solution.py:20
  55.0 9.9 %collective-permute-start.12 = (bf16[128,512]{1,0:T(8,128)(2,1)S(1)}, bf16[128,512]{1,0:T(8,128)(2,1)S(1)}, u32[]{:S(2)}, u32[]{:S(2)}) collective-permute-start(bf16[128,512]{1,0:T(8,128)(2,1)S(1)} %get-tuple-element.115), channel_id=1, source_target_pairs={{0,12},{4,8},{8,4},{12,0},{1,13},{5,9},{9,5},{13,1},{2,14},{6,10},... | collective-permute-start | bytes 393224 | tf_op jit(solution)/shard_map/ppermute | solution.py:20
  58.2 8.2 %collective-permute-start.13 = (bf16[128,512]{1,0:T(8,128)(2,1)S(1)}, bf16[128,512]{1,0:T(8,128)(2,1)S(1)}, u32[]{:S(2)}, u32[]{:S(2)}) collective-permute-start(bf16[128,512]{1,0:T(8,128)(2,1)S(1)} %get-tuple-element.116), channel_id=1, source_target_pairs={{0,12},{4,8},{8,4},{12,0},{1,13},{5,9},{9,5},{13,1},{2,14},{6,10},... | collective-permute-start | bytes 393224 | tf_op jit(solution)/shard_map/ppermute | solution.py:20
  72.7 18.3 %collective-permute-start.29 = (bf16[160,1024]{1,0:T(8,128)(2,1)S(1)}, bf16[160,1024]{1,0:T(8,128)(2,1)S(1)}, u32[]{:S(2)}, u32[]{:S(2)}) collective-permute-start(bf16[160,1024]{1,0:T(8,128)(2,1)S(1)} %get-tuple-element.137), channel_id=1, source_target_pairs={{0,8},{4,12},{8,0},{12,4},{1,9},{5,13},{9,1},{13,5},{2,10},{6,14},... | collective-permute-start | bytes 983048 | tf_op jit(solution)/shard_map/ppermute | solution.py:20
  79.2 15.3 %collective-permute-start.28 = (bf16[96,1024]{1,0:T(8,128)(2,1)S(1)}, bf16[96,1024]{1,0:T(8,128)(2,1)S(1)}, u32[]{:S(2)}, u32[]{:S(2)}) collective-permute-start(bf16[96,1024]{1,0:T(8,128)(2,1)S(1)} %collective-permute-done.9.refs_9_), channel_id=1, source_target_pairs={{0,16},{16,0},{1,17},{17,1},{2,18},{18,2},{3,19},{19,3},{4,20},{20... | collective-permute-start | bytes 589832 | tf_op jit(solution)/shard_map/ppermute | solution.py:20
  84.4 8.1 %collective-permute-start.24 = (bf16[32,512]{1,0:T(8,128)(2,1)S(1)}, bf16[32,512]{1,0:T(8,128)(2,1)S(1)}, u32[]{:S(2)}, u32[]{:S(2)}) collective-permute-start(bf16[32,512]{1,0:T(8,128)(2,1)S(1)} %get-tuple-element.132), channel_id=1, source_target_pairs={{0,12},{4,8},{8,4},{12,0},{1,13},{5,9},{9,5},{13,1},{2,14},{6,10},... | collective-permute-start | bytes 98312 | tf_op jit(solution)/shard_map/ppermute | solution.py:20
  84.8 7.7 %collective-permute-start.23 = (bf16[32,512]{1,0:T(8,128)(2,1)S(1)}, bf16[32,512]{1,0:T(8,128)(2,1)S(1)}, u32[]{:S(2)}, u32[]{:S(2)}) collective-permute-start(bf16[32,512]{1,0:T(8,128)(2,1)S(1)} %get-tuple-element.132), channel_id=1, source_target_pairs={{0,8},{4,12},{8,0},{12,4},{1,9},{5,13},{9,1},{13,5},{2,10},{6,14},... | collective-permute-start | bytes 98312 | tf_op jit(solution)/shard_map/ppermute | solution.py:20
  91.0 10.2 %collective-permute-start.30 = (bf16[160,1024]{1,0:T(8,128)(2,1)S(1)}, bf16[160,1024]{1,0:T(8,128)(2,1)S(1)}, u32[]{:S(2)}, u32[]{:S(2)}) collective-permute-start(bf16[160,1024]{1,0:T(8,128)(2,1)S(1)} %collective-permute-done.29.refs_11_), channel_id=1, source_target_pairs={{0,16},{16,0},{1,17},{17,1},{2,18},{18,2},{3,19},{19,3},{4,20},{20... | collective-permute-start | bytes 983048 | tf_op jit(solution)/shard_map/ppermute | solution.py:20
  92.9 8.3 %collective-permute-start.26 = (bf16[32,2048]{1,0:T(8,128)(2,1)S(1)}, bf16[32,2048]{1,0:T(8,128)(2,1)S(1)}, u32[]{:S(2)}, u32[]{:S(2)}) collective-permute-start(bf16[32,2048]{1,0:T(8,128)(2,1)S(1)} %constant_dynamic-update-slice_fusion.refs_0_), channel_id=1, source_target_pairs={{0,2},{1,3},{2,0},{3,1},{4,6},{5,7},{6,4},{7,5},{8,10},{9,11},{10,... | collective-permute-start | bytes 393224 | tf_op jit(solution)/shard_map/ppermute | solution.py:20
  102.8 15.4 %collective-permute-start.35 = (bf16[128,1024]{1,0:T(8,128)(2,1)S(1)}, bf16[128,1024]{1,0:T(8,128)(2,1)S(1)}, u32[]{:S(2)}, u32[]{:S(2)}) collective-permute-start(bf16[128,1024]{1,0:T(8,128)(2,1)S(1)} %get-tuple-element.140.refs_0_.refs_5_.fresh_ref), channel_id=1, source_target_pairs={{0,4},{4,0},{8,12},{12,8},{1,5},{5,1},{9,13},{13,9},{2,6},{6,2},{1... | collective-permute-start | bytes 786440 | tf_op jit(solution)/shard_map/ppermute | solution.py:20
  104.1 11.3 %collective-permute-start.31 = (bf16[128,512]{1,0:T(8,128)(2,1)S(1)}, bf16[128,512]{1,0:T(8,128)(2,1)S(1)}, u32[]{:S(2)}, u32[]{:S(2)}) collective-permute-start(bf16[128,512]{1,0:T(8,128)(2,1)S(1)} %get-tuple-element.138), channel_id=1, source_target_pairs={{0,12},{4,8},{8,4},{12,0},{1,13},{5,9},{9,5},{13,1},{2,14},{6,10},... | collective-permute-start | bytes 393224 | tf_op jit(solution)/shard_map/ppermute | solution.py:20
  105.4 12.1 %collective-permute-start.33 = (bf16[128,512]{1,0:T(8,128)(2,1)S(1)}, bf16[128,512]{1,0:T(8,128)(2,1)S(1)}, u32[]{:S(2)}, u32[]{:S(2)}) collective-permute-start(bf16[128,512]{1,0:T(8,128)(2,1)S(1)} %get-tuple-element.139), channel_id=1, source_target_pairs={{0,12},{4,8},{8,4},{12,0},{1,13},{5,9},{9,5},{13,1},{2,14},{6,10},... | collective-permute-start | bytes 393224 | tf_op jit(solution)/shard_map/ppermute | solution.py:20
  147.4 16.3 %collective-permute-start.49 = (bf16[128,1024]{1,0:T(8,128)(2,1)S(1)}, bf16[128,1024]{1,0:T(8,128)(2,1)S(1)}, u32[]{:S(2)}, u32[]{:S(2)}) collective-permute-start(bf16[128,1024]{1,0:T(8,128)(2,1)S(1)} %get-tuple-element.151.refs_0_.fresh_ref.refs_5_), channel_id=1, source_target_pairs={{0,4},{4,0},{8,12},{12,8},{1,5},{5,1},{9,13},{13,9},{2,6},{6,2},{1... | collective-permute-start | bytes 786440 | tf_op jit(solution)/shard_map/ppermute | solution.py:20
  148.5 12.4 %collective-permute-start.45 = (bf16[128,512]{1,0:T(8,128)(2,1)S(1)}, bf16[128,512]{1,0:T(8,128)(2,1)S(1)}, u32[]{:S(2)}, u32[]{:S(2)}) collective-permute-start(bf16[128,512]{1,0:T(8,128)(2,1)S(1)} %get-tuple-element.149), channel_id=1, source_target_pairs={{0,12},{4,8},{8,4},{12,0},{1,13},{5,9},{9,5},{13,1},{2,14},{6,10},... | collective-permute-start | bytes 393224 | tf_op jit(solution)/shard_map/ppermute | solution.py:20
  151.0 12.7 %collective-permute-start.47 = (bf16[128,512]{1,0:T(8,128)(2,1)S(1)}, bf16[128,512]{1,0:T(8,128)(2,1)S(1)}, u32[]{:S(2)}, u32[]{:S(2)}) collective-permute-start(bf16[128,512]{1,0:T(8,128)(2,1)S(1)} %get-tuple-element.150), channel_id=1, source_target_pairs={{0,12},{4,8},{8,4},{12,0},{1,13},{5,9},{9,5},{13,1},{2,14},{6,10},... | collective-permute-start | bytes 393224 | tf_op jit(solution)/shard_map/ppermute | solution.py:20
  184.3 7.8 %collective-permute-start.57 = (bf16[32,2048]{1,0:T(8,128)(2,1)S(1)}, bf16[32,2048]{1,0:T(8,128)(2,1)S(1)}, u32[]{:S(2)}, u32[]{:S(2)}) collective-permute-start(bf16[32,2048]{1,0:T(8,128)(2,1)S(1)} %constant_dynamic-update-slice_fusion.8.refs_0_), channel_id=1, source_target_pairs={{0,2},{1,3},{2,0},{3,1},{4,6},{5,7},{6,4},{7,5},{8,10},{9,11},{10,... | collective-permute-start | bytes 393224 | tf_op jit(solution)/shard_map/ppermute | solution.py:20
  (44 other events, 276.0 us)

commit v6 on v5

--- a/solution.py
+++ b/solution.py
@@ -697,6 +697,7 @@
                 before = project(
                     level, batch, first, share_cols, info, index, pieces[:4], *fixed, None, False
                 )[0]
+                before, held = lax.optimization_barrier((before, held))
                 sums = project(
                     level, batch, second, share_cols, info, index, pieces[4:], *fixed, before, True
                 )
@@ -739,7 +740,11 @@
                 joined = jnp.concatenate(heads, axis=1)
             else:
                 joined = lax.all_gather(mixed, "tensor", axis=1, tiled=True)
-            attended.append([joined] + [swap(joined, "dp", step) for step in range(1, dp)])
+            if dp == 4 and level > 1:
+                across = swap(joined, "dp", 2)
+                attended.append([joined, swap(joined, "dp", 1), across, swap(across, "dp", 1)])
+            else:
+                attended.append([joined] + [swap(joined, "dp", step) for step in range(1, dp)])
         for batch in range(batches):
             index = chosen[batch][level]
             if by_swaps and level == 0:

time: 195 us -> 191 us (0.979)
  transfers between devices with their start and end apart: 59 -> 59, of which waited for: 37 -> 36; matrix products, arithmetic and copies ran while one was open for 1% -> 1% of each run, Pallas kernels for 11% -> 11%
where the time goes in v6:
time: 191 us
  waiting for transfers between devices  86.7 us (45%)
  starting transfers between devices  65.4 us (34%)
  Pallas kernels  33.9 us (18%)
  local copies, waits for them, and re-layouts  4.45 us (2%)
    ppermute x59, waiting for transfers between devices, swap(): return lax.ppermute(x, axis, [(i, i ^ step) for i in range(size)])  86.7 us
    ppermute x59, starting transfers between devices, swap(): return lax.ppermute(x, axis, [(i, i ^ step) for i in range(size)])  65.4 us
    pallas_call x7, Pallas kernels, project(): pl.pallas_call(functools.partial(project_kernel, level, batch, places, sh...  10.8 us
    pallas_call x4, Pallas kernels, attend(): pl.pallas_call(functools.partial(attend_kernel, len(parts), len(earlier),...  5.78 us
    pallas_call x3, Pallas kernels, output(): pl.pallas_call(functools.partial(output_kernel, level, batch, dp, places,...  4.95 us
    unnamed x29, local copies, waits for them, and re-layouts  4.34 us
  transfers between devices with their start and end apart: 59, of which 36 were waited for; matrix products, arithmetic and copies ran while one was open for 1% of the time, Pallas kernels for 11%

profile of v6, /device:TPU:0, one launch (start us, length us, event | category | flops | bytes accessed | tf_op | source)
XLA Modules:
  0.0 191.1 jit_solution(12807039562777214036)
XLA Ops:
  1.9 5.1 %collective-permute-start.6 = (bf16[256,1024]{1,0:T(8,128)(2,1)S(1)}, bf16[256,1024]{1,0:T(8,128)(2,1)S(1)}, u32[]{:S(2)}, u32[]{:S(2)}) collective-permute-start(bf16[256,1024]{1,0:T(8,128)(2,1)S(1)} %get-tuple-element.105), channel_id=1, source_target_pairs={{0,12},{4,8},{8,4},{12,0},{1,13},{5,9},{9,5},{13,1},{2,14},{6,10},... | collective-permute-start | bytes 1572872 | tf_op jit(solution)/shard_map/ppermute | solution.py:20
  34.0 7.2 %collective-permute-done.9.refs_9_ = bf16[96,1024]{1,0:T(8,128)(2,1)S(1)} collective-permute-done((bf16[96,1024]{1,0:T(8,128)(2,1)S(1)}, bf16[96,1024]{1,0:T(8,128)(2,1)S(1)}, u32[]{:S(2)}, u32[]{:S(2)}) %collective-permute-start.9) | collective-permute-done | bytes 196640 | tf_op jit(solution)/shard_map/ppermute | solution.py:20
  44.7 2.8 %collective-permute-done.8.refs_1_ = bf16[128,1024]{1,0:T(8,128)(2,1)S(1)} collective-permute-done((bf16[128,1024]{1,0:T(8,128)(2,1)S(1)}, bf16[128,1024]{1,0:T(8,128)(2,1)S(1)}, u32[]{:S(2)}, u32[]{:S(2)}) %collective-permute-start.8) | collective-permute-done | bytes 262176 | tf_op jit(solution)/shard_map/ppermute | solution.py:20
  47.5 3.9 %collective-permute-done.11.refs_2_ = bf16[128,1024]{1,0:T(8,128)(2,1)S(1)} collective-permute-done((bf16[128,1024]{1,0:T(8,128)(2,1)S(1)}, bf16[128,1024]{1,0:T(8,128)(2,1)S(1)}, u32[]{:S(2)}, u32[]{:S(2)}) %collective-permute-start.11) | collective-permute-done | bytes 262176 | tf_op jit(solution)/shard_map/ppermute | solution.py:20
  52.3 2.7 %collective-permute-start.18 = (bf16[128,1024]{1,0:T(8,128)(2,1)S(1)}, bf16[128,1024]{1,0:T(8,128)(2,1)S(1)}, u32[]{:S(2)}, u32[]{:S(2)}) collective-permute-start(bf16[128,1024]{1,0:T(8,128)(2,1)S(1)} %get-tuple-element.131.refs_0_.fresh_ref.refs_13_), channel_id=1, source_target_pairs={{0,4},{4,0},{8,12},{12,8},{1,5},{5,1},{9,13},{13,9},{2,6},{6,2},{1... | collective-permute-start | bytes 786440 | tf_op jit(solution)/shard_map/ppermute | solution.py:20
  55.0 3.2 %collective-permute-start.12 = (bf16[128,512]{1,0:T(8,128)(2,1)S(1)}, bf16[128,512]{1,0:T(8,128)(2,1)S(1)}, u32[]{:S(2)}, u32[]{:S(2)}) collective-permute-start(bf16[128,512]{1,0:T(8,128)(2,1)S(1)} %get-tuple-element.121), channel_id=1, source_target_pairs={{0,12},{4,8},{8,4},{12,0},{1,13},{5,9},{9,5},{13,1},{2,14},{6,10},... | collective-permute-start | bytes 393224 | tf_op jit(solution)/shard_map/ppermute | solution.py:20
  58.8 6.1 %collective-permute-done.12.refs_2_ = bf16[128,512]{1,0:T(8,128)(2,1)S(1)} collective-permute-done((bf16[128,512]{1,0:T(8,128)(2,1)S(1)}, bf16[128,512]{1,0:T(8,128)(2,1)S(1)}, u32[]{:S(2)}, u32[]{:S(2)}) %collective-permute-start.12) | collective-permute-done | bytes 131104 | tf_op jit(solution)/shard_map/ppermute | solution.py:20
  72.7 2.9 %collective-permute-start.29 = (bf16[160,1024]{1,0:T(8,128)(2,1)S(1)}, bf16[160,1024]{1,0:T(8,128)(2,1)S(1)}, u32[]{:S(2)}, u32[]{:S(2)}) collective-permute-start(bf16[160,1024]{1,0:T(8,128)(2,1)S(1)} %get-tuple-element.144), channel_id=1, source_target_pairs={{0,8},{4,12},{8,0},{12,4},{1,9},{5,13},{9,1},{13,5},{2,10},{6,14},... | collective-permute-start | bytes 983048 | tf_op jit(solution)/shard_map/ppermute | solution.py:20
  76.8 2.3 %collective-permute-start.20 = (bf16[32,896]{1,0:T(8,128)(2,1)S(1)}, bf16[32,896]{1,0:T(8,128)(2,1)S(1)}, u32[]{:S(2)}, u32[]{:S(2)}) collective-permute-start(bf16[32,896]{1,0:T(8,128)(2,1)S(1)} %get-tuple-element.135), channel_id=1, source_target_pairs={{0,2},{1,3},{2,0},{3,1},{4,6},{5,7},{6,4},{7,5},{8,10},{9,11},{10,... | collective-permute-start | bytes 172040 | tf_op jit(solution)/shard_map/ppermute | solution.py:20
  86.2 2.7 %collective-permute-start.22 = (bf16[32,512]{1,0:T(8,128)(2,1)S(1)}, bf16[32,512]{1,0:T(8,128)(2,1)S(1)}, u32[]{:S(2)}, u32[]{:S(2)}) collective-permute-start(bf16[32,512]{1,0:T(8,128)(2,1)S(1)} %get-tuple-element.139), channel_id=1, source_target_pairs={{0,4},{4,0},{8,12},{12,8},{1,5},{5,1},{9,13},{13,9},{2,6},{6,2},{1... | collective-permute-start | bytes 98312 | tf_op jit(solution)/shard_map/ppermute | solution.py:20
  94.5 3.6 %collective-permute-done.27.refs_3_ = bf16[32,2048]{1,0:T(8,128)(2,1)S(1)} collective-permute-done((bf16[32,2048]{1,0:T(8,128)(2,1)S(1)}, bf16[32,2048]{1,0:T(8,128)(2,1)S(1)}, u32[]{:S(2)}, u32[]{:S(2)}) %collective-permute-start.27) | collective-permute-done | bytes 131104 | tf_op jit(solution)/shard_map/ppermute | solution.py:20
  98.1 3.1 %collective-permute-done.26.refs_2_ = bf16[32,2048]{1,0:T(8,128)(2,1)S(1)} collective-permute-done((bf16[32,2048]{1,0:T(8,128)(2,1)S(1)}, bf16[32,2048]{1,0:T(8,128)(2,1)S(1)}, u32[]{:S(2)}, u32[]{:S(2)}) %collective-permute-start.26) | collective-permute-done | bytes 131104 | tf_op jit(solution)/shard_map/ppermute | solution.py:20
  105.4 2.5 %collective-permute-start.33 = (bf16[128,512]{1,0:T(8,128)(2,1)S(1)}, bf16[128,512]{1,0:T(8,128)(2,1)S(1)}, u32[]{:S(2)}, u32[]{:S(2)}) collective-permute-start(bf16[128,512]{1,0:T(8,128)(2,1)S(1)} %get-tuple-element.146), channel_id=1, source_target_pairs={{0,12},{4,8},{8,4},{12,0},{1,13},{5,9},{9,5},{13,1},{2,14},{6,10},... | collective-permute-start | bytes 393224 | tf_op jit(solution)/shard_map/ppermute | solution.py:20
  107.9 7.5 %collective-permute-done.31.refs_2_ = bf16[128,512]{1,0:T(8,128)(2,1)S(1)} collective-permute-done((bf16[128,512]{1,0:T(8,128)(2,1)S(1)}, bf16[128,512]{1,0:T(8,128)(2,1)S(1)}, u32[]{:S(2)}, u32[]{:S(2)}) %collective-permute-start.31) | collective-permute-done | bytes 131104 | tf_op jit(solution)/shard_map/ppermute | solution.py:20
  126.3 2.9 %collective-permute-done.37.refs_2_ = bf16[32,896]{1,0:T(8,128)(2,1)S(1)} collective-permute-done((bf16[32,896]{1,0:T(8,128)(2,1)S(1)}, bf16[32,896]{1,0:T(8,128)(2,1)S(1)}, u32[]{:S(2)}, u32[]{:S(2)}) %collective-permute-start.37) | collective-permute-done | bytes 57376 | tf_op jit(solution)/shard_map/ppermute | solution.py:20
  131.1 2.5 %collective-permute-start.41 = (bf16[32,512]{1,0:T(8,128)(2,1)S(1)}, bf16[32,512]{1,0:T(8,128)(2,1)S(1)}, u32[]{:S(2)}, u32[]{:S(2)}) collective-permute-start(bf16[32,512]{1,0:T(8,128)(2,1)S(1)} %get-tuple-element.156), channel_id=1, source_target_pairs={{0,12},{4,8},{8,4},{12,0},{1,13},{5,9},{9,5},{13,1},{2,14},{6,10},... | collective-permute-start | bytes 98312 | tf_op jit(solution)/shard_map/ppermute | solution.py:20
  139.4 4.1 %collective-permute-done.43.refs_2_ = bf16[32,2048]{1,0:T(8,128)(2,1)S(1)} collective-permute-done((bf16[32,2048]{1,0:T(8,128)(2,1)S(1)}, bf16[32,2048]{1,0:T(8,128)(2,1)S(1)}, u32[]{:S(2)}, u32[]{:S(2)}) %collective-permute-start.43) | collective-permute-done | bytes 131104 | tf_op jit(solution)/shard_map/ppermute | solution.py:20
  147.3 2.4 %collective-permute-start.45 = (bf16[128,512]{1,0:T(8,128)(2,1)S(1)}, bf16[128,512]{1,0:T(8,128)(2,1)S(1)}, u32[]{:S(2)}, u32[]{:S(2)}) collective-permute-start(bf16[128,512]{1,0:T(8,128)(2,1)S(1)} %get-tuple-element.158), channel_id=1, source_target_pairs={{0,12},{4,8},{8,4},{12,0},{1,13},{5,9},{9,5},{13,1},{2,14},{6,10},... | collective-permute-start | bytes 393224 | tf_op jit(solution)/shard_map/ppermute | solution.py:20
  151.1 8.5 %collective-permute-done.45.refs_2_ = bf16[128,512]{1,0:T(8,128)(2,1)S(1)} collective-permute-done((bf16[128,512]{1,0:T(8,128)(2,1)S(1)}, bf16[128,512]{1,0:T(8,128)(2,1)S(1)}, u32[]{:S(2)}, u32[]{:S(2)}) %collective-permute-start.45) | collective-permute-done | bytes 131104 | tf_op jit(solution)/shard_map/ppermute | solution.py:20
  159.7 2.8 %collective-permute-done.47.refs_3_ = bf16[128,512]{1,0:T(8,128)(2,1)S(1)} collective-permute-done((bf16[128,512]{1,0:T(8,128)(2,1)S(1)}, bf16[128,512]{1,0:T(8,128)(2,1)S(1)}, u32[]{:S(2)}, u32[]{:S(2)}) %collective-permute-start.47) | collective-permute-done | bytes 131104 | tf_op jit(solution)/shard_map/ppermute | solution.py:20
  170.5 2.9 %collective-permute-done.51.refs_2_ = bf16[32,896]{1,0:T(8,128)(2,1)S(1)} collective-permute-done((bf16[32,896]{1,0:T(8,128)(2,1)S(1)}, bf16[32,896]{1,0:T(8,128)(2,1)S(1)}, u32[]{:S(2)}, u32[]{:S(2)}) %collective-permute-start.51) | collective-permute-done | bytes 57376 | tf_op jit(solution)/shard_map/ppermute | solution.py:20
  176.9 2.8 %collective-permute-start.53 = (bf16[32,512]{1,0:T(8,128)(2,1)S(1)}, bf16[32,512]{1,0:T(8,128)(2,1)S(1)}, u32[]{:S(2)}, u32[]{:S(2)}) collective-permute-start(bf16[32,512]{1,0:T(8,128)(2,1)S(1)} %get-tuple-element.169), channel_id=1, source_target_pairs={{0,4},{4,0},{8,12},{12,8},{1,5},{5,1},{9,13},{13,9},{2,6},{6,2},{1... | collective-permute-start | bytes 98312 | tf_op jit(solution)/shard_map/ppermute | solution.py:20
  179.7 2.5 %collective-permute-done.53 = bf16[32,512]{1,0:T(8,128)(2,1)S(1)} collective-permute-done((bf16[32,512]{1,0:T(8,128)(2,1)S(1)}, bf16[32,512]{1,0:T(8,128)(2,1)S(1)}, u32[]{:S(2)}, u32[]{:S(2)}) %collective-permute-start.53) | collective-permute-done | bytes 32800 | tf_op jit(solution)/shard_map/ppermute | solution.py:20
  183.3 4.2 %collective-permute-done.57.refs_2_ = bf16[32,2048]{1,0:T(8,128)(2,1)S(1)} collective-permute-done((bf16[32,2048]{1,0:T(8,128)(2,1)S(1)}, bf16[32,2048]{1,0:T(8,128)(2,1)S(1)}, u32[]{:S(2)}, u32[]{:S(2)}) %collective-permute-start.57) | collective-permute-done | bytes 131104 | tf_op jit(solution)/shard_map/ppermute | solution.py:20
  (152 shorter events, 99.3 us)
Async XLA Ops:
  1.9 28.3 %collective-permute-start.6 = (bf16[256,1024]{1,0:T(8,128)(2,1)S(1)}, bf16[256,1024]{1,0:T(8,128)(2,1)S(1)}, u32[]{:S(2)}, u32[]{:S(2)}) collective-permute-start(bf16[256,1024]{1,0:T(8,128)(2,1)S(1)} %get-tuple-element.105), channel_id=1, source_target_pairs={{0,12},{4,8},{8,4},{12,0},{1,13},{5,9},{9,5},{13,1},{2,14},{6,10},... | collective-permute-start | bytes 1572872 | tf_op jit(solution)/shard_map/ppermute | solution.py:20
  7.0 23.3 %collective-permute-start.7 = (bf16[256,1024]{1,0:T(8,128)(2,1)S(1)}, bf16[256,1024]{1,0:T(8,128)(2,1)S(1)}, u32[]{:S(2)}, u32[]{:S(2)}) collective-permute-start(bf16[256,1024]{1,0:T(8,128)(2,1)S(1)} %get-tuple-element.106), channel_id=1, source_target_pairs={{0,4},{4,0},{8,12},{12,8},{1,5},{5,1},{9,13},{13,9},{2,6},{6,2},{1... | collective-permute-start | bytes 1572872 | tf_op jit(solution)/shard_map/ppermute | solution.py:20
  28.1 13.5 %collective-permute-start.10 = (bf16[128,1024]{1,0:T(8,128)(2,1)S(1)}, bf16[128,1024]{1,0:T(8,128)(2,1)S(1)}, u32[]{:S(2)}, u32[]{:S(2)}) collective-permute-start(bf16[128,1024]{1,0:T(8,128)(2,1)S(1)} %get-tuple-element.120), channel_id=1, source_target_pairs={{0,4},{4,0},{8,12},{12,8},{1,5},{5,1},{9,13},{13,9},{2,6},{6,2},{1... | collective-permute-start | bytes 786440 | tf_op jit(solution)/shard_map/ppermute | solution.py:20
  30.2 11.0 %collective-permute-start.9 = (bf16[96,1024]{1,0:T(8,128)(2,1)S(1)}, bf16[96,1024]{1,0:T(8,128)(2,1)S(1)}, u32[]{:S(2)}, u32[]{:S(2)}) collective-permute-start(bf16[96,1024]{1,0:T(8,128)(2,1)S(1)} %get-tuple-element.118), channel_id=1, source_target_pairs={{0,8},{4,12},{8,0},{12,4},{1,9},{5,13},{9,1},{13,5},{2,10},{6,14},... | collective-permute-start | bytes 589832 | tf_op jit(solution)/shard_map/ppermute | solution.py:20
  30.3 36.0 %collective-permute-start.14 = (bf16[256,1024]{1,0:T(8,128)(2,1)S(1)}, bf16[256,1024]{1,0:T(8,128)(2,1)S(1)}, u32[]{:S(2)}, u32[]{:S(2)}) collective-permute-start(bf16[256,1024]{1,0:T(8,128)(2,1)S(1)} %collective-permute-done.6.refs_5_), channel_id=1, source_target_pairs={{0,16},{16,0},{1,17},{17,1},{2,18},{18,2},{3,19},{19,3},{4,20},{20... | collective-permute-start | bytes 1572872 | tf_op jit(solution)/shard_map/ppermute | solution.py:20
  31.8 34.5 %collective-permute-start.15 = (bf16[256,1024]{1,0:T(8,128)(2,1)S(1)}, bf16[256,1024]{1,0:T(8,128)(2,1)S(1)}, u32[]{:S(2)}, u32[]{:S(2)}) collective-permute-start(bf16[256,1024]{1,0:T(8,128)(2,1)S(1)} %collective-permute-done.7.refs_7_), channel_id=1, source_target_pairs={{0,16},{16,0},{1,17},{17,1},{2,18},{18,2},{3,19},{19,3},{4,20},{20... | collective-permute-start | bytes 1572872 | tf_op jit(solution)/shard_map/ppermute | solution.py:20
  32.3 15.2 %collective-permute-start.8 = (bf16[128,1024]{1,0:T(8,128)(2,1)S(1)}, bf16[128,1024]{1,0:T(8,128)(2,1)S(1)}, u32[]{:S(2)}, u32[]{:S(2)}) collective-permute-start(bf16[128,1024]{1,0:T(8,128)(2,1)S(1)} %get-tuple-element.116), channel_id=1, source_target_pairs={{0,4},{4,0},{8,12},{12,8},{1,5},{5,1},{9,13},{13,9},{2,6},{6,2},{1... | collective-permute-start | bytes 786440 | tf_op jit(solution)/shard_map/ppermute | solution.py:20
  41.7 9.7 %collective-permute-start.11 = (bf16[128,1024]{1,0:T(8,128)(2,1)S(1)}, bf16[128,1024]{1,0:T(8,128)(2,1)S(1)}, u32[]{:S(2)}, u32[]{:S(2)}) collective-permute-start(bf16[128,1024]{1,0:T(8,128)(2,1)S(1)} %add.1), channel_id=1, source_target_pairs={{0,12},{4,8},{8,4},{12,0},{1,13},{5,9},{9,5},{13,1},{2,14},{6,10},... | collective-permute-start | bytes 786440 | tf_op jit(solution)/shard_map/ppermute | solution.py:20
  52.3 17.3 %collective-permute-start.18 = (bf16[128,1024]{1,0:T(8,128)(2,1)S(1)}, bf16[128,1024]{1,0:T(8,128)(2,1)S(1)}, u32[]{:S(2)}, u32[]{:S(2)}) collective-permute-start(bf16[128,1024]{1,0:T(8,128)(2,1)S(1)} %get-tuple-element.131.refs_0_.fresh_ref.refs_13_), channel_id=1, source_target_pairs={{0,4},{4,0},{8,12},{12,8},{1,5},{5,1},{9,13},{13,9},{2,6},{6,2},{1... | collective-permute-start | bytes 786440 | tf_op jit(solution)/shard_map/ppermute | solution.py:20
  55.0 9.9 %collective-permute-start.12 = (bf16[128,512]{1,0:T(8,128)(2,1)S(1)}, bf16[128,512]{1,0:T(8,128)(2,1)S(1)}, u32[]{:S(2)}, u32[]{:S(2)}) collective-permute-start(bf16[128,512]{1,0:T(8,128)(2,1)S(1)} %get-tuple-element.121), channel_id=1, source_target_pairs={{0,12},{4,8},{8,4},{12,0},{1,13},{5,9},{9,5},{13,1},{2,14},{6,10},... | collective-permute-start | bytes 393224 | tf_op jit(solution)/shard_map/ppermute | solution.py:20
  58.2 8.2 %collective-permute-start.13 = (bf16[128,512]{1,0:T(8,128)(2,1)S(1)}, bf16[128,512]{1,0:T(8,128)(2,1)S(1)}, u32[]{:S(2)}, u32[]{:S(2)}) collective-permute-start(bf16[128,512]{1,0:T(8,128)(2,1)S(1)} %get-tuple-element.122), channel_id=1, source_target_pairs={{0,12},{4,8},{8,4},{12,0},{1,13},{5,9},{9,5},{13,1},{2,14},{6,10},... | collective-permute-start | bytes 393224 | tf_op jit(solution)/shard_map/ppermute | solution.py:20
  72.7 18.3 %collective-permute-start.29 = (bf16[160,1024]{1,0:T(8,128)(2,1)S(1)}, bf16[160,1024]{1,0:T(8,128)(2,1)S(1)}, u32[]{:S(2)}, u32[]{:S(2)}) collective-permute-start(bf16[160,1024]{1,0:T(8,128)(2,1)S(1)} %get-tuple-element.144), channel_id=1, source_target_pairs={{0,8},{4,12},{8,0},{12,4},{1,9},{5,13},{9,1},{13,5},{2,10},{6,14},... | collective-permute-start | bytes 983048 | tf_op jit(solution)/shard_map/ppermute | solution.py:20
  79.2 15.3 %collective-permute-start.28 = (bf16[96,1024]{1,0:T(8,128)(2,1)S(1)}, bf16[96,1024]{1,0:T(8,128)(2,1)S(1)}, u32[]{:S(2)}, u32[]{:S(2)}) collective-permute-start(bf16[96,1024]{1,0:T(8,128)(2,1)S(1)} %collective-permute-done.9.refs_9_), channel_id=1, source_target_pairs={{0,16},{16,0},{1,17},{17,1},{2,18},{18,2},{3,19},{19,3},{4,20},{20... | collective-permute-start | bytes 589832 | tf_op jit(solution)/shard_map/ppermute | solution.py:20
  84.4 8.1 %collective-permute-start.24 = (bf16[32,512]{1,0:T(8,128)(2,1)S(1)}, bf16[32,512]{1,0:T(8,128)(2,1)S(1)}, u32[]{:S(2)}, u32[]{:S(2)}) collective-permute-start(bf16[32,512]{1,0:T(8,128)(2,1)S(1)} %get-tuple-element.139), channel_id=1, source_target_pairs={{0,12},{4,8},{8,4},{12,0},{1,13},{5,9},{9,5},{13,1},{2,14},{6,10},... | collective-permute-start | bytes 98312 | tf_op jit(solution)/shard_map/ppermute | solution.py:20
  84.8 7.7 %collective-permute-start.23 = (bf16[32,512]{1,0:T(8,128)(2,1)S(1)}, bf16[32,512]{1,0:T(8,128)(2,1)S(1)}, u32[]{:S(2)}, u32[]{:S(2)}) collective-permute-start(bf16[32,512]{1,0:T(8,128)(2,1)S(1)} %get-tuple-element.139), channel_id=1, source_target_pairs={{0,8},{4,12},{8,0},{12,4},{1,9},{5,13},{9,1},{13,5},{2,10},{6,14},... | collective-permute-start | bytes 98312 | tf_op jit(solution)/shard_map/ppermute | solution.py:20
  91.0 10.2 %collective-permute-start.30 = (bf16[160,1024]{1,0:T(8,128)(2,1)S(1)}, bf16[160,1024]{1,0:T(8,128)(2,1)S(1)}, u32[]{:S(2)}, u32[]{:S(2)}) collective-permute-start(bf16[160,1024]{1,0:T(8,128)(2,1)S(1)} %collective-permute-done.29.refs_11_), channel_id=1, source_target_pairs={{0,16},{16,0},{1,17},{17,1},{2,18},{18,2},{3,19},{19,3},{4,20},{20... | collective-permute-start | bytes 983048 | tf_op jit(solution)/shard_map/ppermute | solution.py:20
  93.0 8.3 %collective-permute-start.26 = (bf16[32,2048]{1,0:T(8,128)(2,1)S(1)}, bf16[32,2048]{1,0:T(8,128)(2,1)S(1)}, u32[]{:S(2)}, u32[]{:S(2)}) collective-permute-start(bf16[32,2048]{1,0:T(8,128)(2,1)S(1)} %constant_dynamic-update-slice_fusion.refs_0_), channel_id=1, source_target_pairs={{0,2},{1,3},{2,0},{3,1},{4,6},{5,7},{6,4},{7,5},{8,10},{9,11},{10,... | collective-permute-start | bytes 393224 | tf_op jit(solution)/shard_map/ppermute | solution.py:20
  102.8 16.7 %collective-permute-start.35 = (bf16[128,1024]{1,0:T(8,128)(2,1)S(1)}, bf16[128,1024]{1,0:T(8,128)(2,1)S(1)}, u32[]{:S(2)}, u32[]{:S(2)}) collective-permute-start(bf16[128,1024]{1,0:T(8,128)(2,1)S(1)} %get-tuple-element.147.refs_0_.fresh_ref.refs_5_), channel_id=1, source_target_pairs={{0,4},{4,0},{8,12},{12,8},{1,5},{5,1},{9,13},{13,9},{2,6},{6,2},{1... | collective-permute-start | bytes 786440 | tf_op jit(solution)/shard_map/ppermute | solution.py:20
  104.1 11.3 %collective-permute-start.31 = (bf16[128,512]{1,0:T(8,128)(2,1)S(1)}, bf16[128,512]{1,0:T(8,128)(2,1)S(1)}, u32[]{:S(2)}, u32[]{:S(2)}) collective-permute-start(bf16[128,512]{1,0:T(8,128)(2,1)S(1)} %get-tuple-element.145), channel_id=1, source_target_pairs={{0,12},{4,8},{8,4},{12,0},{1,13},{5,9},{9,5},{13,1},{2,14},{6,10},... | collective-permute-start | bytes 393224 | tf_op jit(solution)/shard_map/ppermute | solution.py:20
  105.4 12.1 %collective-permute-start.33 = (bf16[128,512]{1,0:T(8,128)(2,1)S(1)}, bf16[128,512]{1,0:T(8,128)(2,1)S(1)}, u32[]{:S(2)}, u32[]{:S(2)}) collective-permute-start(bf16[128,512]{1,0:T(8,128)(2,1)S(1)} %get-tuple-element.146), channel_id=1, source_target_pairs={{0,12},{4,8},{8,4},{12,0},{1,13},{5,9},{9,5},{13,1},{2,14},{6,10},... | collective-permute-start | bytes 393224 | tf_op jit(solution)/shard_map/ppermute | solution.py:20
  131.1 7.3 %collective-permute-start.41 = (bf16[32,512]{1,0:T(8,128)(2,1)S(1)}, bf16[32,512]{1,0:T(8,128)(2,1)S(1)}, u32[]{:S(2)}, u32[]{:S(2)}) collective-permute-start(bf16[32,512]{1,0:T(8,128)(2,1)S(1)} %get-tuple-element.156), channel_id=1, source_target_pairs={{0,12},{4,8},{8,4},{12,0},{1,13},{5,9},{9,5},{13,1},{2,14},{6,10},... | collective-permute-start | bytes 98312 | tf_op jit(solution)/shard_map/ppermute | solution.py:20
  146.2 17.6 %collective-permute-start.49 = (bf16[128,1024]{1,0:T(8,128)(2,1)S(1)}, bf16[128,1024]{1,0:T(8,128)(2,1)S(1)}, u32[]{:S(2)}, u32[]{:S(2)}) collective-permute-start(bf16[128,1024]{1,0:T(8,128)(2,1)S(1)} %get-tuple-element.160.refs_0_.fresh_ref.refs_5_), channel_id=1, source_target_pairs={{0,4},{4,0},{8,12},{12,8},{1,5},{5,1},{9,13},{13,9},{2,6},{6,2},{1... | collective-permute-start | bytes 786440 | tf_op jit(solution)/shard_map/ppermute | solution.py:20
  147.3 12.4 %collective-permute-start.45 = (bf16[128,512]{1,0:T(8,128)(2,1)S(1)}, bf16[128,512]{1,0:T(8,128)(2,1)S(1)}, u32[]{:S(2)}, u32[]{:S(2)}) collective-permute-start(bf16[128,512]{1,0:T(8,128)(2,1)S(1)} %get-tuple-element.158), channel_id=1, source_target_pairs={{0,12},{4,8},{8,4},{12,0},{1,13},{5,9},{9,5},{13,1},{2,14},{6,10},... | collective-permute-start | bytes 393224 | tf_op jit(solution)/shard_map/ppermute | solution.py:20
  149.7 12.7 %collective-permute-start.47 = (bf16[128,512]{1,0:T(8,128)(2,1)S(1)}, bf16[128,512]{1,0:T(8,128)(2,1)S(1)}, u32[]{:S(2)}, u32[]{:S(2)}) collective-permute-start(bf16[128,512]{1,0:T(8,128)(2,1)S(1)} %get-tuple-element.159), channel_id=1, source_target_pairs={{0,12},{4,8},{8,4},{12,0},{1,13},{5,9},{9,5},{13,1},{2,14},{6,10},... | collective-permute-start | bytes 393224 | tf_op jit(solution)/shard_map/ppermute | solution.py:20
  (44 other events, 252.9 us)
